TPU v7x, 512 devices: a whole 4x8x8 slice. The times are simulated.
512 devices in a mesh: inst: 4 (over x), cell: 128 (over y, z, core).
Axes of the slice: x: 4, y: 8, z: 8, core: 2. Of those that a mesh axis runs over, the one named last changes fastest.
Arguments:
- adjoint_init: float32 [8, 384, 8, 320], P('inst', 'cell'), may hold values from -6 to 6
- source_term: float32 [8, 384, 8, 320], P('inst', 'cell'), may hold values from -6 to 6
- jacobian: bfloat16 [8, 384, 3, 320, 320], P('inst', 'cell')
- volume: float32 [384, 320], P('cell'), may hold values from 0.5 to 2
- pseudo_step: float32 [384, 320], P('cell'), may hold values from 0.2 to 0.6
- neighbor_slots: int32 [384, 3], P('cell'), may hold values from 0 to 6, as said below
- halo_blocks: int32 [512], P('cell'), may hold values from 0 to 2, as said below
- padded_rows: int32 [128], P('cell'), may hold values from 0 to 1
Outputs:
- adjoint: float32 [8, 384, 8, 320], P('inst', 'cell')
- residual: float32 [8, 384, 8, 320], P('inst', 'cell')
Inputs may be any that keep to these rules, and one draw needn't show every extreme that they name: `neighbor_slots`: slot 0 of block row r is its own block, 2 + (r mod 3); slot 1 is below 2; slot 2 is 5 or more. `halo_blocks`: each device's 2 * 2 entries are its local block rows, the first 2 for the previous device, the others for the next; every entry is below 3 minus that device's padded rows.
All inputs are finite; a program needn't handle non-finite values.
Results may differ from a plain program's by a relative error of at most 0.0003.
Values sent between devices are 32-bit elements; how exact they have to be, the bound alone decides.
No kernel may reach another device: no remote copies, remote signals or barrier semaphores. Data moves between devices by JAX's collectives and lax.ppermute only.
A program may use at most 64 MiB of HBM per device.

v0:
```python
import math

import jax
import jax.numpy as jnp
from jax import lax
from jax.sharding import PartitionSpec as P

NT = 8
ITERS = 16


spectral_scale = 0.15


def extended_2(block, sides, width):
    for axis, dim in sides:
        count = lax.axis_size(axis)
        forward = [(i, i + 1) for i in range(count - 1)]
        forward.append((count - 1, 0))
        backward = [(target, source) for source, target in forward]
        low = lax.ppermute(
            lax.slice_in_dim(block, block.shape[dim] - width, None, axis=dim), axis, forward
        )
        high = lax.ppermute(lax.slice_in_dim(block, 0, width, axis=dim), axis, backward)
        block = jnp.concatenate([low, block, high], axis=dim)
    return block


def time_matrix():
    idx = jnp.arange(NT, dtype=jnp.int32)
    diff = idx[:, None] - idx[None, :]
    parity = jnp.where(jnp.remainder(diff, 2) == 0, 1.0, -1.0).astype(jnp.float32)
    angle = jnp.float32(math.pi) * diff.astype(jnp.float32) / NT
    sine = jnp.where(diff == 0, jnp.float32(1.0), jnp.sin(angle))
    return jnp.where(diff == 0, jnp.float32(0.0), 0.5 * parity * jnp.cos(angle) / sine)


def on_device(
    adjoint_init,
    source_term,
    jacobian,
    volume,
    pseudo_step,
    neighbor_slots,
    halo_blocks,
    padded_rows,
):
    inst_local = adjoint_init.shape[0]
    rows = adjoint_init.shape[1]
    objectives = adjoint_init.shape[2]
    width = adjoint_init.shape[3]
    slots_per_row = neighbor_slots.shape[1]
    reach = halo_blocks.shape[0] // 2
    live = (jnp.arange(rows) < rows - padded_rows[0]).astype(jnp.float32)[None, :, None, None]
    weights = time_matrix()
    scale = (spectral_scale * volume)[None, :, None, :]
    step_size = pseudo_step[None, :, None, :]
    flat_slots = neighbor_slots.reshape(-1)
    wide_blocks = jacobian.astype(jnp.float32)
    adjoint = adjoint_init
    residual = jnp.zeros_like(adjoint_init)
    for sweep in range(ITERS):
        outgoing = jnp.take(adjoint, halo_blocks, axis=1)
        extended = extended_2(outgoing, (("cell", 1),), reach)
        buffer = jnp.concatenate([extended[:, :reach], adjoint, extended[:, 3 * reach :]], axis=1)
        gathered = jnp.take(buffer, flat_slots, axis=1).reshape(
            inst_local, rows, slots_per_row, objectives, width
        )
        flux = jnp.einsum(
            "irkop,irkpq->iroq", gathered, wide_blocks, precision=lax.Precision.HIGHEST
        )
        mixed = jnp.einsum(
            "ji,jroq->iroq",
            weights,
            lax.all_to_all(adjoint, "inst", split_axis=3, concat_axis=0, tiled=True),
            precision=lax.Precision.HIGHEST,
        )
        coupled = lax.all_to_all(mixed, "inst", split_axis=0, concat_axis=3, tiled=True)
        residual = live * (source_term - flux - scale * coupled)
        adjoint = adjoint + step_size * residual
    return (adjoint, residual)


def solution(mesh):
    return jax.shard_map(
        on_device,
        mesh=mesh,
        in_specs=(
            P("inst", "cell", None, None),
            P("inst", "cell", None, None),
            P("inst", "cell", None, None, None),
            P("cell", None),
            P("cell", None),
            P("cell", None),
            P("cell"),
            P("cell"),
        ),
        out_specs=(P("inst", "cell", None, None), P("inst", "cell", None, None)),
        check_vma=False,
    )
```

profile of v0, /device:TPU:2, one launch (start us, length us, event | category | flops | bytes accessed | tf_op | source)
XLA Modules:
  0.0 629.5 jit_solution(5888789733682526058)
XLA Ops:
  5.5 13.3 %collective-permute-start.1 = (f32[2,2,8,320]{3,2,0,1:T(8,128)S(1)}, f32[2,2,8,320]{3,2,0,1:T(8,128)S(1)}, u32[]{:S(2)}, u32[]{:S(2)}) collective-permute-start(f32[2,2,8,320]{3,2,0,1:T(8,128)S(1)} %get-tuple-element.35), channel_id=1, source_target_pairs={{1,0},{2,1},{3,2},{4,3},{5,4},{6,5},{7,6},{8,7},{9,8},{10,9},{11,1... | collective-permute-start | bytes 122888 | tf_op jit(solution)/shard_map/ppermute | solution.py:24
  21.7 4.8 all-to-all-start
  34.1 4.7 all-to-all-start.1
  50.2 7.0 %collective-permute-start.3 = (f32[2,2,8,320]{3,2,1,0:T(8,128)S(1)}, f32[2,2,8,320]{3,2,1,0:T(8,128)S(1)}, u32[]{:S(2)}, u32[]{:S(2)}) collective-permute-start(f32[2,2,8,320]{3,2,1,0:T(8,128)S(1)} %get-tuple-element.33), channel_id=1, source_target_pairs={{1,0},{2,1},{3,2},{4,3},{5,4},{6,5},{7,6},{8,7},{9,8},{10,9},{11,1... | collective-permute-start | bytes 122888 | tf_op jit(solution)/shard_map/ppermute | solution.py:24
  88.8 7.0 %collective-permute-start.5 = (f32[2,2,8,320]{3,2,1,0:T(8,128)S(1)}, f32[2,2,8,320]{3,2,1,0:T(8,128)S(1)}, u32[]{:S(2)}, u32[]{:S(2)}) collective-permute-start(f32[2,2,8,320]{3,2,1,0:T(8,128)S(1)} %get-tuple-element.31), channel_id=1, source_target_pairs={{1,0},{2,1},{3,2},{4,3},{5,4},{6,5},{7,6},{8,7},{9,8},{10,9},{11,1... | collective-permute-start | bytes 122888 | tf_op jit(solution)/shard_map/ppermute | solution.py:24
  98.8 5.2 all-to-all-start.4
  127.9 7.0 %collective-permute-start.7 = (f32[2,2,8,320]{3,2,1,0:T(8,128)S(1)}, f32[2,2,8,320]{3,2,1,0:T(8,128)S(1)}, u32[]{:S(2)}, u32[]{:S(2)}) collective-permute-start(f32[2,2,8,320]{3,2,1,0:T(8,128)S(1)} %get-tuple-element.29), channel_id=1, source_target_pairs={{1,0},{2,1},{3,2},{4,3},{5,4},{6,5},{7,6},{8,7},{9,8},{10,9},{11,1... | collective-permute-start | bytes 122888 | tf_op jit(solution)/shard_map/ppermute | solution.py:24
  166.5 7.0 %collective-permute-start.9 = (f32[2,2,8,320]{3,2,1,0:T(8,128)S(1)}, f32[2,2,8,320]{3,2,1,0:T(8,128)S(1)}, u32[]{:S(2)}, u32[]{:S(2)}) collective-permute-start(f32[2,2,8,320]{3,2,1,0:T(8,128)S(1)} %get-tuple-element.27), channel_id=1, source_target_pairs={{1,0},{2,1},{3,2},{4,3},{5,4},{6,5},{7,6},{8,7},{9,8},{10,9},{11,1... | collective-permute-start | bytes 122888 | tf_op jit(solution)/shard_map/ppermute | solution.py:24
  189.1 4.9 all-to-all-start.9
  205.3 7.0 %collective-permute-start.11 = (f32[2,2,8,320]{3,2,1,0:T(8,128)S(1)}, f32[2,2,8,320]{3,2,1,0:T(8,128)S(1)}, u32[]{:S(2)}, u32[]{:S(2)}) collective-permute-start(f32[2,2,8,320]{3,2,1,0:T(8,128)S(1)} %get-tuple-element.25), channel_id=1, source_target_pairs={{1,0},{2,1},{3,2},{4,3},{5,4},{6,5},{7,6},{8,7},{9,8},{10,9},{11,1... | collective-permute-start | bytes 122888 | tf_op jit(solution)/shard_map/ppermute | solution.py:24
  227.9 4.7 all-to-all-start.11
  244.0 7.0 %collective-permute-start.13 = (f32[2,2,8,320]{3,2,1,0:T(8,128)S(1)}, f32[2,2,8,320]{3,2,1,0:T(8,128)S(1)}, u32[]{:S(2)}, u32[]{:S(2)}) collective-permute-start(f32[2,2,8,320]{3,2,1,0:T(8,128)S(1)} %get-tuple-element.23), channel_id=1, source_target_pairs={{1,0},{2,1},{3,2},{4,3},{5,4},{6,5},{7,6},{8,7},{9,8},{10,9},{11,1... | collective-permute-start | bytes 122888 | tf_op jit(solution)/shard_map/ppermute | solution.py:24
  282.6 7.2 %collective-permute-start.15 = (f32[2,2,8,320]{3,2,1,0:T(8,128)S(1)}, f32[2,2,8,320]{3,2,1,0:T(8,128)S(1)}, u32[]{:S(2)}, u32[]{:S(2)}) collective-permute-start(f32[2,2,8,320]{3,2,1,0:T(8,128)S(1)} %get-tuple-element.21), channel_id=1, source_target_pairs={{1,0},{2,1},{3,2},{4,3},{5,4},{6,5},{7,6},{8,7},{9,8},{10,9},{11,1... | collective-permute-start | bytes 122888 | tf_op jit(solution)/shard_map/ppermute | solution.py:24
  321.4 7.0 %collective-permute-start.17 = (f32[2,2,8,320]{3,2,1,0:T(8,128)S(1)}, f32[2,2,8,320]{3,2,1,0:T(8,128)S(1)}, u32[]{:S(2)}, u32[]{:S(2)}) collective-permute-start(f32[2,2,8,320]{3,2,1,0:T(8,128)S(1)} %get-tuple-element.19), channel_id=1, source_target_pairs={{1,0},{2,1},{3,2},{4,3},{5,4},{6,5},{7,6},{8,7},{9,8},{10,9},{11,1... | collective-permute-start | bytes 122888 | tf_op jit(solution)/shard_map/ppermute | solution.py:24
  360.0 7.0 %collective-permute-start.19 = (f32[2,2,8,320]{3,2,1,0:T(8,128)S(1)}, f32[2,2,8,320]{3,2,1,0:T(8,128)S(1)}, u32[]{:S(2)}, u32[]{:S(2)}) collective-permute-start(f32[2,2,8,320]{3,2,1,0:T(8,128)S(1)} %get-tuple-element.17), channel_id=1, source_target_pairs={{1,0},{2,1},{3,2},{4,3},{5,4},{6,5},{7,6},{8,7},{9,8},{10,9},{11,1... | collective-permute-start | bytes 122888 | tf_op jit(solution)/shard_map/ppermute | solution.py:24
  370.1 5.1 all-to-all-start.18
  399.1 7.0 %collective-permute-start.21 = (f32[2,2,8,320]{3,2,1,0:T(8,128)S(1)}, f32[2,2,8,320]{3,2,1,0:T(8,128)S(1)}, u32[]{:S(2)}, u32[]{:S(2)}) collective-permute-start(f32[2,2,8,320]{3,2,1,0:T(8,128)S(1)} %get-tuple-element.15), channel_id=1, source_target_pairs={{1,0},{2,1},{3,2},{4,3},{5,4},{6,5},{7,6},{8,7},{9,8},{10,9},{11,1... | collective-permute-start | bytes 122888 | tf_op jit(solution)/shard_map/ppermute | solution.py:24
  437.7 7.0 %collective-permute-start.23 = (f32[2,2,8,320]{3,2,1,0:T(8,128)S(1)}, f32[2,2,8,320]{3,2,1,0:T(8,128)S(1)}, u32[]{:S(2)}, u32[]{:S(2)}) collective-permute-start(f32[2,2,8,320]{3,2,1,0:T(8,128)S(1)} %get-tuple-element.13), channel_id=1, source_target_pairs={{1,0},{2,1},{3,2},{4,3},{5,4},{6,5},{7,6},{8,7},{9,8},{10,9},{11,1... | collective-permute-start | bytes 122888 | tf_op jit(solution)/shard_map/ppermute | solution.py:24
  460.3 4.9 all-to-all-start.23
  476.5 7.0 %collective-permute-start.25 = (f32[2,2,8,320]{3,2,1,0:T(8,128)S(1)}, f32[2,2,8,320]{3,2,1,0:T(8,128)S(1)}, u32[]{:S(2)}, u32[]{:S(2)}) collective-permute-start(f32[2,2,8,320]{3,2,1,0:T(8,128)S(1)} %get-tuple-element.11), channel_id=1, source_target_pairs={{1,0},{2,1},{3,2},{4,3},{5,4},{6,5},{7,6},{8,7},{9,8},{10,9},{11,1... | collective-permute-start | bytes 122888 | tf_op jit(solution)/shard_map/ppermute | solution.py:24
  515.1 7.0 %collective-permute-start.27 = (f32[2,2,8,320]{3,2,1,0:T(8,128)S(1)}, f32[2,2,8,320]{3,2,1,0:T(8,128)S(1)}, u32[]{:S(2)}, u32[]{:S(2)}) collective-permute-start(f32[2,2,8,320]{3,2,1,0:T(8,128)S(1)} %get-tuple-element.9), channel_id=1, source_target_pairs={{1,0},{2,1},{3,2},{4,3},{5,4},{6,5},{7,6},{8,7},{9,8},{10,9},{11,1... | collective-permute-start | bytes 122888 | tf_op jit(solution)/shard_map/ppermute | solution.py:24
  553.7 7.2 %collective-permute-start.29 = (f32[2,2,8,320]{3,2,1,0:T(8,128)S(1)}, f32[2,2,8,320]{3,2,1,0:T(8,128)S(1)}, u32[]{:S(2)}, u32[]{:S(2)}) collective-permute-start(f32[2,2,8,320]{3,2,1,0:T(8,128)S(1)} %get-tuple-element.7), channel_id=1, source_target_pairs={{1,0},{2,1},{3,2},{4,3},{5,4},{6,5},{7,6},{8,7},{9,8},{10,9},{11,1... | collective-permute-start | bytes 122888 | tf_op jit(solution)/shard_map/ppermute | solution.py:24
  592.6 7.0 %collective-permute-start.31 = (f32[2,2,8,320]{3,2,1,0:T(8,128)S(1)}, f32[2,2,8,320]{3,2,1,0:T(8,128)S(1)}, u32[]{:S(2)}, u32[]{:S(2)}) collective-permute-start(f32[2,2,8,320]{3,2,1,0:T(8,128)S(1)} %get-tuple-element.5), channel_id=1, source_target_pairs={{1,0},{2,1},{3,2},{4,3},{5,4},{6,5},{7,6},{8,7},{9,8},{10,9},{11,1... | collective-permute-start | bytes 122888 | tf_op jit(solution)/shard_map/ppermute | solution.py:24
  624.4 4.9 multiply_add_fusion
  (376 shorter events, 469.1 us)
Async XLA Ops:
  3.6 25.1 %collective-permute-start = (f32[2,2,8,320]{3,2,0,1:T(8,128)S(1)}, f32[2,2,8,320]{3,2,0,1:T(8,128)S(1)}, u32[]{:S(2)}, u32[]{:S(2)}) collective-permute-start(f32[2,2,8,320]{3,2,0,1:T(8,128)S(1)} %get-tuple-element.34), channel_id=1, source_target_pairs={{0,1},{1,2},{2,3},{3,4},{4,5},{5,6},{6,7},{7,8},{8,9},{9,10},{10,1... | collective-permute-start | bytes 122888 | tf_op jit(solution)/shard_map/ppermute | solution.py:21
  5.5 23.2 %collective-permute-start.1 = (f32[2,2,8,320]{3,2,0,1:T(8,128)S(1)}, f32[2,2,8,320]{3,2,0,1:T(8,128)S(1)}, u32[]{:S(2)}, u32[]{:S(2)}) collective-permute-start(f32[2,2,8,320]{3,2,0,1:T(8,128)S(1)} %get-tuple-element.35), channel_id=1, source_target_pairs={{1,0},{2,1},{3,2},{4,3},{5,4},{6,5},{7,6},{8,7},{9,8},{10,9},{11,1... | collective-permute-start | bytes 122888 | tf_op jit(solution)/shard_map/ppermute | solution.py:24
  48.3 16.6 %collective-permute-start.2 = (f32[2,2,8,320]{3,2,1,0:T(8,128)S(1)}, f32[2,2,8,320]{3,2,1,0:T(8,128)S(1)}, u32[]{:S(2)}, u32[]{:S(2)}) collective-permute-start(f32[2,2,8,320]{3,2,1,0:T(8,128)S(1)} %get-tuple-element.32), channel_id=1, source_target_pairs={{0,1},{1,2},{2,3},{3,4},{4,5},{5,6},{6,7},{7,8},{8,9},{9,10},{10,1... | collective-permute-start | bytes 122888 | tf_op jit(solution)/shard_map/ppermute | solution.py:21
  50.2 14.7 %collective-permute-start.3 = (f32[2,2,8,320]{3,2,1,0:T(8,128)S(1)}, f32[2,2,8,320]{3,2,1,0:T(8,128)S(1)}, u32[]{:S(2)}, u32[]{:S(2)}) collective-permute-start(f32[2,2,8,320]{3,2,1,0:T(8,128)S(1)} %get-tuple-element.33), channel_id=1, source_target_pairs={{1,0},{2,1},{3,2},{4,3},{5,4},{6,5},{7,6},{8,7},{9,8},{10,9},{11,1... | collective-permute-start | bytes 122888 | tf_op jit(solution)/shard_map/ppermute | solution.py:24
  86.9 17.1 %collective-permute-start.4 = (f32[2,2,8,320]{3,2,1,0:T(8,128)S(1)}, f32[2,2,8,320]{3,2,1,0:T(8,128)S(1)}, u32[]{:S(2)}, u32[]{:S(2)}) collective-permute-start(f32[2,2,8,320]{3,2,1,0:T(8,128)S(1)} %get-tuple-element.30), channel_id=1, source_target_pairs={{0,1},{1,2},{2,3},{3,4},{4,5},{5,6},{6,7},{7,8},{8,9},{9,10},{10,1... | collective-permute-start | bytes 122888 | tf_op jit(solution)/shard_map/ppermute | solution.py:21
  88.8 15.2 %collective-permute-start.5 = (f32[2,2,8,320]{3,2,1,0:T(8,128)S(1)}, f32[2,2,8,320]{3,2,1,0:T(8,128)S(1)}, u32[]{:S(2)}, u32[]{:S(2)}) collective-permute-start(f32[2,2,8,320]{3,2,1,0:T(8,128)S(1)} %get-tuple-element.31), channel_id=1, source_target_pairs={{1,0},{2,1},{3,2},{4,3},{5,4},{6,5},{7,6},{8,7},{9,8},{10,9},{11,1... | collective-permute-start | bytes 122888 | tf_op jit(solution)/shard_map/ppermute | solution.py:24
  126.0 16.6 %collective-permute-start.6 = (f32[2,2,8,320]{3,2,1,0:T(8,128)S(1)}, f32[2,2,8,320]{3,2,1,0:T(8,128)S(1)}, u32[]{:S(2)}, u32[]{:S(2)}) collective-permute-start(f32[2,2,8,320]{3,2,1,0:T(8,128)S(1)} %get-tuple-element.28), channel_id=1, source_target_pairs={{0,1},{1,2},{2,3},{3,4},{4,5},{5,6},{6,7},{7,8},{8,9},{9,10},{10,1... | collective-permute-start | bytes 122888 | tf_op jit(solution)/shard_map/ppermute | solution.py:21
  127.9 14.7 %collective-permute-start.7 = (f32[2,2,8,320]{3,2,1,0:T(8,128)S(1)}, f32[2,2,8,320]{3,2,1,0:T(8,128)S(1)}, u32[]{:S(2)}, u32[]{:S(2)}) collective-permute-start(f32[2,2,8,320]{3,2,1,0:T(8,128)S(1)} %get-tuple-element.29), channel_id=1, source_target_pairs={{1,0},{2,1},{3,2},{4,3},{5,4},{6,5},{7,6},{8,7},{9,8},{10,9},{11,1... | collective-permute-start | bytes 122888 | tf_op jit(solution)/shard_map/ppermute | solution.py:24
  164.6 16.6 %collective-permute-start.8 = (f32[2,2,8,320]{3,2,1,0:T(8,128)S(1)}, f32[2,2,8,320]{3,2,1,0:T(8,128)S(1)}, u32[]{:S(2)}, u32[]{:S(2)}) collective-permute-start(f32[2,2,8,320]{3,2,1,0:T(8,128)S(1)} %get-tuple-element.26), channel_id=1, source_target_pairs={{0,1},{1,2},{2,3},{3,4},{4,5},{5,6},{6,7},{7,8},{8,9},{9,10},{10,1... | collective-permute-start | bytes 122888 | tf_op jit(solution)/shard_map/ppermute | solution.py:21
  166.5 14.7 %collective-permute-start.9 = (f32[2,2,8,320]{3,2,1,0:T(8,128)S(1)}, f32[2,2,8,320]{3,2,1,0:T(8,128)S(1)}, u32[]{:S(2)}, u32[]{:S(2)}) collective-permute-start(f32[2,2,8,320]{3,2,1,0:T(8,128)S(1)} %get-tuple-element.27), channel_id=1, source_target_pairs={{1,0},{2,1},{3,2},{4,3},{5,4},{6,5},{7,6},{8,7},{9,8},{10,9},{11,1... | collective-permute-start | bytes 122888 | tf_op jit(solution)/shard_map/ppermute | solution.py:24
  203.4 16.6 %collective-permute-start.10 = (f32[2,2,8,320]{3,2,1,0:T(8,128)S(1)}, f32[2,2,8,320]{3,2,1,0:T(8,128)S(1)}, u32[]{:S(2)}, u32[]{:S(2)}) collective-permute-start(f32[2,2,8,320]{3,2,1,0:T(8,128)S(1)} %get-tuple-element.24), channel_id=1, source_target_pairs={{0,1},{1,2},{2,3},{3,4},{4,5},{5,6},{6,7},{7,8},{8,9},{9,10},{10,1... | collective-permute-start | bytes 122888 | tf_op jit(solution)/shard_map/ppermute | solution.py:21
  242.0 16.6 %collective-permute-start.12 = (f32[2,2,8,320]{3,2,1,0:T(8,128)S(1)}, f32[2,2,8,320]{3,2,1,0:T(8,128)S(1)}, u32[]{:S(2)}, u32[]{:S(2)}) collective-permute-start(f32[2,2,8,320]{3,2,1,0:T(8,128)S(1)} %get-tuple-element.22), channel_id=1, source_target_pairs={{0,1},{1,2},{2,3},{3,4},{4,5},{5,6},{6,7},{7,8},{8,9},{9,10},{10,1... | collective-permute-start | bytes 122888 | tf_op jit(solution)/shard_map/ppermute | solution.py:21
  280.7 16.9 %collective-permute-start.14 = (f32[2,2,8,320]{3,2,1,0:T(8,128)S(1)}, f32[2,2,8,320]{3,2,1,0:T(8,128)S(1)}, u32[]{:S(2)}, u32[]{:S(2)}) collective-permute-start(f32[2,2,8,320]{3,2,1,0:T(8,128)S(1)} %get-tuple-element.20), channel_id=1, source_target_pairs={{0,1},{1,2},{2,3},{3,4},{4,5},{5,6},{6,7},{7,8},{8,9},{9,10},{10,1... | collective-permute-start | bytes 122888 | tf_op jit(solution)/shard_map/ppermute | solution.py:21
  282.6 14.9 %collective-permute-start.15 = (f32[2,2,8,320]{3,2,1,0:T(8,128)S(1)}, f32[2,2,8,320]{3,2,1,0:T(8,128)S(1)}, u32[]{:S(2)}, u32[]{:S(2)}) collective-permute-start(f32[2,2,8,320]{3,2,1,0:T(8,128)S(1)} %get-tuple-element.21), channel_id=1, source_target_pairs={{1,0},{2,1},{3,2},{4,3},{5,4},{6,5},{7,6},{8,7},{9,8},{10,9},{11,1... | collective-permute-start | bytes 122888 | tf_op jit(solution)/shard_map/ppermute | solution.py:24
  319.5 16.6 %collective-permute-start.16 = (f32[2,2,8,320]{3,2,1,0:T(8,128)S(1)}, f32[2,2,8,320]{3,2,1,0:T(8,128)S(1)}, u32[]{:S(2)}, u32[]{:S(2)}) collective-permute-start(f32[2,2,8,320]{3,2,1,0:T(8,128)S(1)} %get-tuple-element.18), channel_id=1, source_target_pairs={{0,1},{1,2},{2,3},{3,4},{4,5},{5,6},{6,7},{7,8},{8,9},{9,10},{10,1... | collective-permute-start | bytes 122888 | tf_op jit(solution)/shard_map/ppermute | solution.py:21
  358.1 17.1 %collective-permute-start.18 = (f32[2,2,8,320]{3,2,1,0:T(8,128)S(1)}, f32[2,2,8,320]{3,2,1,0:T(8,128)S(1)}, u32[]{:S(2)}, u32[]{:S(2)}) collective-permute-start(f32[2,2,8,320]{3,2,1,0:T(8,128)S(1)} %get-tuple-element.16), channel_id=1, source_target_pairs={{0,1},{1,2},{2,3},{3,4},{4,5},{5,6},{6,7},{7,8},{8,9},{9,10},{10,1... | collective-permute-start | bytes 122888 | tf_op jit(solution)/shard_map/ppermute | solution.py:21
  360.0 15.1 %collective-permute-start.19 = (f32[2,2,8,320]{3,2,1,0:T(8,128)S(1)}, f32[2,2,8,320]{3,2,1,0:T(8,128)S(1)}, u32[]{:S(2)}, u32[]{:S(2)}) collective-permute-start(f32[2,2,8,320]{3,2,1,0:T(8,128)S(1)} %get-tuple-element.17), channel_id=1, source_target_pairs={{1,0},{2,1},{3,2},{4,3},{5,4},{6,5},{7,6},{8,7},{9,8},{10,9},{11,1... | collective-permute-start | bytes 122888 | tf_op jit(solution)/shard_map/ppermute | solution.py:24
  397.1 16.6 %collective-permute-start.20 = (f32[2,2,8,320]{3,2,1,0:T(8,128)S(1)}, f32[2,2,8,320]{3,2,1,0:T(8,128)S(1)}, u32[]{:S(2)}, u32[]{:S(2)}) collective-permute-start(f32[2,2,8,320]{3,2,1,0:T(8,128)S(1)} %get-tuple-element.14), channel_id=1, source_target_pairs={{0,1},{1,2},{2,3},{3,4},{4,5},{5,6},{6,7},{7,8},{8,9},{9,10},{10,1... | collective-permute-start | bytes 122888 | tf_op jit(solution)/shard_map/ppermute | solution.py:21
  435.8 16.6 %collective-permute-start.22 = (f32[2,2,8,320]{3,2,1,0:T(8,128)S(1)}, f32[2,2,8,320]{3,2,1,0:T(8,128)S(1)}, u32[]{:S(2)}, u32[]{:S(2)}) collective-permute-start(f32[2,2,8,320]{3,2,1,0:T(8,128)S(1)} %get-tuple-element.12), channel_id=1, source_target_pairs={{0,1},{1,2},{2,3},{3,4},{4,5},{5,6},{6,7},{7,8},{8,9},{9,10},{10,1... | collective-permute-start | bytes 122888 | tf_op jit(solution)/shard_map/ppermute | solution.py:21
  474.6 16.6 %collective-permute-start.24 = (f32[2,2,8,320]{3,2,1,0:T(8,128)S(1)}, f32[2,2,8,320]{3,2,1,0:T(8,128)S(1)}, u32[]{:S(2)}, u32[]{:S(2)}) collective-permute-start(f32[2,2,8,320]{3,2,1,0:T(8,128)S(1)} %get-tuple-element.10), channel_id=1, source_target_pairs={{0,1},{1,2},{2,3},{3,4},{4,5},{5,6},{6,7},{7,8},{8,9},{9,10},{10,1... | collective-permute-start | bytes 122888 | tf_op jit(solution)/shard_map/ppermute | solution.py:21
  513.2 16.6 %collective-permute-start.26 = (f32[2,2,8,320]{3,2,1,0:T(8,128)S(1)}, f32[2,2,8,320]{3,2,1,0:T(8,128)S(1)}, u32[]{:S(2)}, u32[]{:S(2)}) collective-permute-start(f32[2,2,8,320]{3,2,1,0:T(8,128)S(1)} %get-tuple-element.8), channel_id=1, source_target_pairs={{0,1},{1,2},{2,3},{3,4},{4,5},{5,6},{6,7},{7,8},{8,9},{9,10},{10,1... | collective-permute-start | bytes 122888 | tf_op jit(solution)/shard_map/ppermute | solution.py:21
  551.8 16.9 %collective-permute-start.28 = (f32[2,2,8,320]{3,2,1,0:T(8,128)S(1)}, f32[2,2,8,320]{3,2,1,0:T(8,128)S(1)}, u32[]{:S(2)}, u32[]{:S(2)}) collective-permute-start(f32[2,2,8,320]{3,2,1,0:T(8,128)S(1)} %get-tuple-element.6), channel_id=1, source_target_pairs={{0,1},{1,2},{2,3},{3,4},{4,5},{5,6},{6,7},{7,8},{8,9},{9,10},{10,1... | collective-permute-start | bytes 122888 | tf_op jit(solution)/shard_map/ppermute | solution.py:21
  553.7 14.9 %collective-permute-start.29 = (f32[2,2,8,320]{3,2,1,0:T(8,128)S(1)}, f32[2,2,8,320]{3,2,1,0:T(8,128)S(1)}, u32[]{:S(2)}, u32[]{:S(2)}) collective-permute-start(f32[2,2,8,320]{3,2,1,0:T(8,128)S(1)} %get-tuple-element.7), channel_id=1, source_target_pairs={{1,0},{2,1},{3,2},{4,3},{5,4},{6,5},{7,6},{8,7},{9,8},{10,9},{11,1... | collective-permute-start | bytes 122888 | tf_op jit(solution)/shard_map/ppermute | solution.py:24
  590.7 16.6 %collective-permute-start.30 = (f32[2,2,8,320]{3,2,1,0:T(8,128)S(1)}, f32[2,2,8,320]{3,2,1,0:T(8,128)S(1)}, u32[]{:S(2)}, u32[]{:S(2)}) collective-permute-start(f32[2,2,8,320]{3,2,1,0:T(8,128)S(1)} %get-tuple-element.4), channel_id=1, source_target_pairs={{0,1},{1,2},{2,3},{3,4},{4,5},{5,6},{6,7},{7,8},{8,9},{9,10},{10,1... | collective-permute-start | bytes 122888 | tf_op jit(solution)/shard_map/ppermute | solution.py:21
  (43 other events, 534.1 us)
where the time goes:
time: 642 us; the launch traced here: 630 us
  starting transfers between devices  301 us (47%)
  waiting for transfers between devices  122 us (19%)
  local copies, waits for them, and re-layouts  112 us (17%)
  matrix products  73.2 us (11%)
  other arithmetic  18.6 us (3%)
    ppermute x16, starting transfers between devices, extended_2(): lax.ppermute(lax.slice_in_dim(block, 0, width, axis=dim), axis, backward)  118 us
    all_to_all x16, starting transfers between devices, on_device(): lax.all_to_all(adjoint, 'inst', split_axis=3, concat_axis=0, tiled=True)  76.3 us
    all_to_all x16, starting transfers between devices, on_device(): lax.all_to_all(mixed, 'inst', split_axis=0, concat_axis=3, tiled=True)  76 us
    dot_general x16, matrix products, on_device(): jnp.einsum('irkop,irkpq->iroq', gathered, wide_blocks, precision=lax.Prec...  68.6 us
    all_to_all x16, waiting for transfers between devices, on_device(): lax.all_to_all(mixed, 'inst', split_axis=0, concat_axis=3, tiled=True)  68.1 us
    unnamed x39, local copies, waits for them, and re-layouts  57.8 us
    all_to_all x16, waiting for transfers between devices, on_device(): lax.all_to_all(adjoint, 'inst', split_axis=3, concat_axis=0, tiled=True)  53.8 us
    ppermute x16, starting transfers between devices, extended_2(): lax.ppermute(lax.slice_in_dim(block, block.shape[dim] - width, None, axis...  30.7 us
  transfers between devices with their start and end apart: 64, of which 32 were waited for; matrix products, arithmetic and copies ran while one was open for 10% of the time, Pallas kernels for 0%

commit v1 on v0

v1 whole, which is shorter than its diff:
```python
import functools
import math

import jax
import jax.numpy as jnp
import numpy as np
from jax import lax
from jax.experimental import pallas as pl
from jax.experimental.pallas import tpu as pltpu
from jax.sharding import PartitionSpec as P

NT = 8
ITERS = 16
SCALE = 0.15
REACH = 2
INST = 2
NEAR_PICK, FAR_PICK, LIVE, NEAR_SEND, FAR_SEND, WEIGHT, TABLE = 0, 3, 6, 9, 13, 17, 40
VMEM = pl.BlockSpec(memory_space=pltpu.VMEM)
HBM = pl.BlockSpec(memory_space=pltpu.HBM)
SMEM = pl.BlockSpec(memory_space=pltpu.SMEM)


def time_matrix():
    out = np.zeros((NT, NT))
    for j in range(NT):
        for i in range(NT):
            if i != j and (j - i) % NT != NT // 2:
                angle = math.pi * (j - i) / NT
                out[j, i] = 0.5 * (-1.0) ** (j - i) * math.cos(angle) / math.sin(angle)
    return out.astype(np.float32)


def split_rows(block):
    high = block.astype(jnp.bfloat16).astype(jnp.float32)
    return jnp.concatenate([high, block - high], axis=0).astype(jnp.bfloat16)


def product(block, matrix):
    rows = block.shape[0]
    out = jnp.dot(split_rows(block), matrix, preferred_element_type=jnp.float32)
    return out[:rows] + out[rows:]


def chosen(mask_ref, row, yes, no):
    return jnp.where(mask_ref[pl.ds(row, 1), :] > 0.0, yes, no)


def listed(tables_ref, first, entry, blocks_ref, t):
    row = first + 2 * entry
    middle = chosen(tables_ref, row, blocks_ref[t, 1], blocks_ref[t, 0])
    return chosen(tables_ref, row + 1, blocks_ref[t, 2], middle)


def tables_kernel(place_ref, slots_ref, lists_ref, pad_ref, weights_ref, tables_ref):
    width = tables_ref.shape[1]
    side = place_ref[0]
    rows = slots_ref.shape[0]

    def put(row, flag):
        tables_ref[pl.ds(row, 1), :] = jnp.full((1, width), jnp.where(flag, 1.0, 0.0), jnp.float32)

    for r in range(rows):
        put(NEAR_PICK + r, slots_ref[r, REACH - side] == 1 + (REACH + rows) * (1 - side))
        put(FAR_PICK + r, slots_ref[r, 1 + side] == 1 + (REACH + rows) * side)
        put(LIVE + r, r < rows - pad_ref[0])
    for e in range(REACH):
        for v in (1, 2):
            put(NEAR_SEND + 2 * e + v - 1, lists_ref[REACH - REACH * side + e] == v)
            put(FAR_SEND + 2 * e + v - 1, lists_ref[REACH * side + e] == v)
    inst = INST
    for j in range(NT):
        for i in range(inst):
            tables_ref[pl.ds(WEIGHT + inst * j + i, 1), :] = jnp.full(
                (1, width), weights_ref[j, place_ref[1] * inst + i], jnp.float32
            )


def send_copies(block_ref, peers_ref, sems, t):
    return [
        pltpu.make_async_copy(block_ref.at[t], peers_ref.at[p, t], sems.at[t, p])
        for p in range(peers_ref.shape[0])
    ]


def begin_kernel(place_ref, lists_ref, adjoint_ref, far_ref, peers_ref, sems):
    inst = adjoint_ref.shape[0]
    copies = [c for t in range(inst) for c in send_copies(adjoint_ref, peers_ref, sems, t)]
    for copy in copies:
        copy.start()
    for t in range(inst):
        for e in range(REACH):
            far_ref[t, e] = adjoint_ref[t, lists_ref[REACH * place_ref[0] + e]]
    for copy in copies:
        copy.wait()


def pack_kernel(place_ref, jacobian_ref, near_ref, sem):
    copy = pltpu.make_async_copy(jacobian_ref.at[:, :, REACH - place_ref[0]], near_ref, sem)
    copy.start()
    copy.wait()


def own_kernel(tables_ref, adjoint_ref, jacobian_ref, source_ref, out_ref, near_ref):
    inst, rows = adjoint_ref.shape[:2]
    for t in range(inst):
        for e in range(REACH):
            near_ref[t, e] = listed(tables_ref, NEAR_SEND, e, adjoint_ref, t)
        for r in range(rows):
            out_ref[t, r] = source_ref[t, r] - product(adjoint_ref[t, r], jacobian_ref[t, r, 0])


def picked(tables_ref, first, blocks_ref, t, r):
    return chosen(tables_ref, first + r, blocks_ref[t, 1], blocks_ref[t, 0])


def far_kernel(tables_ref, far_ref, jacobian_ref, partial_ref, out_ref):
    inst, rows = partial_ref.shape[:2]
    k = 1 + lax.rem(lax.axis_index("cell"), 2)
    for t in range(inst):
        for r in range(rows):
            flux = product(picked(tables_ref, FAR_PICK, far_ref, t, r), jacobian_ref[t, r, k])
            out_ref[t, r] = partial_ref[t, r] - flux


def update_kernel(
    last, tables_ref, near_ref, peers_ref, jacobian_ref, partial_ref, adjoint_ref, volume_ref,
    step_ref, adjoint_out, *outs
):
    inst, rows = partial_ref.shape[:2]
    copies = []
    for t in range(inst):
        for r in range(rows):
            flux = product(picked(tables_ref, NEAR_PICK, near_ref, t, r), jacobian_ref[t, r])
            coupled = None
            for p in range(peers_ref.shape[0]):
                for j in range(inst):
                    row = WEIGHT + inst * (p * inst + j) + t
                    term = tables_ref[pl.ds(row, 1), :] * peers_ref[p, j, r]
                    coupled = term if coupled is None else coupled + term
            scale = SCALE * volume_ref[pl.ds(r, 1), :]
            live = tables_ref[pl.ds(LIVE + r, 1), :]
            residual = live * (partial_ref[t, r] - flux - scale * coupled)
            adjoint_out[t, r] = adjoint_ref[t, r] + step_ref[pl.ds(r, 1), :] * residual
            if last:
                outs[0][t, r] = residual
        if not last:
            far_out, peers_out, sems = outs
            started = send_copies(adjoint_out, peers_out, sems, t)
            for copy in started:
                copy.start()
            copies += started
            for e in range(REACH):
                far_out[t, e] = listed(tables_ref, FAR_SEND, e, adjoint_out, t)
    for copy in copies:
        copy.wait()


def call(kernel, ins, outs, *args, scratch=(), cost=None):
    spaces = {"s": SMEM, "v": VMEM, "a": HBM}
    return pl.pallas_call(
        kernel,
        in_specs=[spaces[c] for c in ins],
        out_specs=[spaces[c] for c, _ in outs],
        out_shape=[jax.ShapeDtypeStruct(*o) for _, o in outs],
        scratch_shapes=list(scratch),
        compiler_params=pltpu.CompilerParams(vmem_limit_bytes=4 << 20),
        cost_estimate=cost and pl.CostEstimate(flops=0, bytes_accessed=cost, transcendentals=0),
    )(*args)


def on_device(adjoint, source, jacobian, volume, step, slots, lists, pads):
    inst, rows, objectives, width = adjoint.shape
    peers = lax.axis_size("inst")
    cells = lax.axis_size("cell")
    near_pairs = [(i, i ^ 1) for i in range(cells)]
    far_pairs = [(i, (i + 1 if i % 2 else i - 1) % cells) for i in range(cells)]
    side = lax.rem(lax.axis_index("cell"), 2).astype(jnp.int32)
    place = jnp.stack([side, lax.axis_index("inst").astype(jnp.int32)])
    f32 = jnp.float32
    block = (adjoint.shape, f32)
    halo = ((inst, REACH, objectives, width), f32)
    gathered = ((peers,) + adjoint.shape, f32)
    packed = ((inst, rows, width, width), jacobian.dtype)
    sends = [pltpu.SemaphoreType.DMA((inst, peers))]
    far, spread = call(
        begin_kernel, "ssv", (("v", halo), ("a", gathered)), place, lists, adjoint, scratch=sends
    )
    tables = call(
        tables_kernel, "sssss", (("v", ((TABLE, width), f32)),), place, slots, lists, pads,
        jnp.asarray(time_matrix()),
    )[0]
    near_j = call(
        pack_kernel, "sa", (("v", packed),), place, jacobian, scratch=[pltpu.SemaphoreType.DMA]
    )[0]
    for sweep in range(ITERS):
        last = sweep == ITERS - 1
        spread = lax.all_to_all(spread, "inst", 0, 0)
        far = lax.ppermute(far, "cell", far_pairs)
        partial, near = call(
            own_kernel, "vvvv", (("v", block), ("v", halo)), tables, adjoint, jacobian, source
        )
        near = lax.ppermute(near, "cell", near_pairs)
        partial = call(far_kernel, "vvvv", (("v", block),), tables, far, jacobian, partial)[0]
        outs = (("v", block),) * 2 if last else (("v", block), ("v", halo), ("a", gathered))
        result = call(
            functools.partial(update_kernel, last), "vvvvvvvv", outs,
            tables, near, spread, near_j, partial, adjoint, volume, step,
            scratch=[] if last else sends,
        )
        if last:
            return result[0], result[1]
        adjoint, far, spread = result


def solution(mesh):
    return jax.shard_map(
        on_device,
        mesh=mesh,
        in_specs=(
            P("inst", "cell", None, None),
            P("inst", "cell", None, None),
            P("inst", "cell", None, None, None),
            P("cell", None),
            P("cell", None),
            P("cell", None),
            P("cell"),
            P("cell"),
        ),
        out_specs=(P("inst", "cell", None, None), P("inst", "cell", None, None)),
        check_vma=False,
    )
```

time: 642 us -> 273 us (0.43)
  the two profiles are of different devices: /device:TPU:2 before, /device:TPU:1 now
where the time goes in v1:
time: 273 us; the launch traced here: 270 us
  starting transfers between devices  188 us (69%)
  local copies, waits for them, and re-layouts  41.3 us (15%)
  Pallas kernels  30.2 us (11%)
  waiting for transfers between devices  7.82 us (3%)
    ppermute x16, starting transfers between devices, on_device(): near = lax.ppermute(near, 'cell', near_pairs)  85.3 us
    all_to_all x16, starting transfers between devices, on_device(): spread = lax.all_to_all(spread, 'inst', 0, 0)  68.6 us
    unnamed x56, local copies, waits for them, and re-layouts  41.3 us
    ppermute x16, starting transfers between devices, on_device(): far = lax.ppermute(far, 'cell', far_pairs)  34.6 us
    pallas_call x51, Pallas kernels, call(): pl.pallas_call(kernel, in_specs=[spaces[c] for c in ins], out_specs=[spac...  30.2 us
    ppermute x16, waiting for transfers between devices, on_device(): near = lax.ppermute(near, 'cell', near_pairs)  7.74 us
  transfers between devices with their start and end apart: 48, of which 15 were waited for; matrix products, arithmetic and copies ran while one was open for 0% of the time, Pallas kernels for 4%

profile of v1, /device:TPU:1, one launch (start us, length us, event | category | flops | bytes accessed | tf_op | source)
XLA Modules:
  0.0 270.0 jit_solution(17059298213164888813)
XLA Ops:
  3.6 4.9 %all-to-all-start = ((f32[4,2,3,8,320]{4,3,2,1,0:T(8,128)}), f32[4,2,3,8,320]{4,3,2,1,0:T(8,128)S(1)}, u32[]{:S(2)}, u32[]{:S(2)}) async-start(f32[4,2,3,8,320]{4,3,2,1,0:T(8,128)} %get-tuple-element.82), calls=%async_computation | async-start | bytes 589824 | tf_op jit(solution)/shard_map/all_to_all | solution.py:197
  8.5 4.8 %collective-permute-start.1 = (f32[2,2,8,320]{3,2,1,0:T(8,128)S(1)}, f32[2,2,8,320]{3,2,1,0:T(8,128)S(1)}, u32[]{:S(2)}, u32[]{:S(2)}) collective-permute-start(f32[2,2,8,320]{3,2,1,0:T(8,128)S(1)} %get-tuple-element.83), channel_id=1, source_target_pairs={{0,127},{1,2},{2,1},{3,4},{4,3},{5,6},{6,5},{7,8},{8,7},{9,10},{10... | collective-permute-start | bytes 122888 | tf_op jit(solution)/shard_map/ppermute | solution.py:198
  21.0 11.3 %collective-permute-start = (f32[2,2,8,320]{3,2,1,0:T(8,128)S(1)}, f32[2,2,8,320]{3,2,1,0:T(8,128)S(1)}, u32[]{:S(2)}, u32[]{:S(2)}) collective-permute-start(f32[2,2,8,320]{3,2,1,0:T(8,128)S(1)} %get-tuple-element.81), channel_id=1, source_target_pairs={{0,1},{1,0},{2,3},{3,2},{4,5},{5,4},{6,7},{7,6},{8,9},{9,8},{10,11... | collective-permute-start | bytes 122888 | tf_op jit(solution)/shard_map/ppermute | solution.py:202
  48.4 4.2 %all-to-all-start.2 = ((f32[4,2,3,8,320]{4,3,2,1,0:T(8,128)}), f32[4,2,3,8,320]{4,3,2,1,0:T(8,128)S(1)}, u32[]{:S(2)}, u32[]{:S(2)}) async-start(f32[4,2,3,8,320]{4,3,2,1,0:T(8,128)} %get-tuple-element.92), calls=%async_computation.2 | async-start | bytes 589824 | tf_op jit(solution)/shard_map/all_to_all | solution.py:197
  58.2 5.7 %collective-permute-start.4 = (f32[2,2,8,320]{3,2,1,0:T(8,128)S(1)}, f32[2,2,8,320]{3,2,1,0:T(8,128)S(1)}, u32[]{:S(2)}, u32[]{:S(2)}) collective-permute-start(f32[2,2,8,320]{3,2,1,0:T(8,128)S(1)} %get-tuple-element.91), channel_id=1, source_target_pairs={{0,1},{1,0},{2,3},{3,2},{4,5},{5,4},{6,7},{7,6},{8,9},{9,8},{10,11... | collective-permute-start | bytes 122888 | tf_op jit(solution)/shard_map/ppermute | solution.py:202
  65.9 4.2 %all-to-all-start.3 = ((f32[4,2,3,8,320]{4,3,2,1,0:T(8,128)}), f32[4,2,3,8,320]{4,3,2,1,0:T(8,128)S(1)}, u32[]{:S(2)}, u32[]{:S(2)}) async-start(f32[4,2,3,8,320]{4,3,2,1,0:T(8,128)} %get-tuple-element.97), calls=%async_computation.3 | async-start | bytes 589824 | tf_op jit(solution)/shard_map/all_to_all | solution.py:197
  74.6 4.3 %collective-permute-start.6 = (f32[2,2,8,320]{3,2,1,0:T(8,128)S(1)}, f32[2,2,8,320]{3,2,1,0:T(8,128)S(1)}, u32[]{:S(2)}, u32[]{:S(2)}) collective-permute-start(f32[2,2,8,320]{3,2,1,0:T(8,128)S(1)} %get-tuple-element.96), channel_id=1, source_target_pairs={{0,1},{1,0},{2,3},{3,2},{4,5},{5,4},{6,7},{7,6},{8,9},{9,8},{10,11... | collective-permute-start | bytes 122888 | tf_op jit(solution)/shard_map/ppermute | solution.py:202
  80.9 4.2 %all-to-all-start.4 = ((f32[4,2,3,8,320]{4,3,2,1,0:T(8,128)}), f32[4,2,3,8,320]{4,3,2,1,0:T(8,128)S(1)}, u32[]{:S(2)}, u32[]{:S(2)}) async-start(f32[4,2,3,8,320]{4,3,2,1,0:T(8,128)} %get-tuple-element.102), calls=%async_computation.4 | async-start | bytes 589824 | tf_op jit(solution)/shard_map/all_to_all | solution.py:197
  89.6 5.9 %collective-permute-start.8 = (f32[2,2,8,320]{3,2,1,0:T(8,128)S(1)}, f32[2,2,8,320]{3,2,1,0:T(8,128)S(1)}, u32[]{:S(2)}, u32[]{:S(2)}) collective-permute-start(f32[2,2,8,320]{3,2,1,0:T(8,128)S(1)} %get-tuple-element.101), channel_id=1, source_target_pairs={{0,1},{1,0},{2,3},{3,2},{4,5},{5,4},{6,7},{7,6},{8,9},{9,8},{10,11... | collective-permute-start | bytes 122888 | tf_op jit(solution)/shard_map/ppermute | solution.py:202
  97.4 4.2 %all-to-all-start.5 = ((f32[4,2,3,8,320]{4,3,2,1,0:T(8,128)}), f32[4,2,3,8,320]{4,3,2,1,0:T(8,128)S(1)}, u32[]{:S(2)}, u32[]{:S(2)}) async-start(f32[4,2,3,8,320]{4,3,2,1,0:T(8,128)} %get-tuple-element.107), calls=%async_computation.5 | async-start | bytes 589824 | tf_op jit(solution)/shard_map/all_to_all | solution.py:197
  106.2 4.3 %collective-permute-start.10 = (f32[2,2,8,320]{3,2,1,0:T(8,128)S(1)}, f32[2,2,8,320]{3,2,1,0:T(8,128)S(1)}, u32[]{:S(2)}, u32[]{:S(2)}) collective-permute-start(f32[2,2,8,320]{3,2,1,0:T(8,128)S(1)} %get-tuple-element.106), channel_id=1, source_target_pairs={{0,1},{1,0},{2,3},{3,2},{4,5},{5,4},{6,7},{7,6},{8,9},{9,8},{10,11... | collective-permute-start | bytes 122888 | tf_op jit(solution)/shard_map/ppermute | solution.py:202
  112.4 4.2 %all-to-all-start.6 = ((f32[4,2,3,8,320]{4,3,2,1,0:T(8,128)}), f32[4,2,3,8,320]{4,3,2,1,0:T(8,128)S(1)}, u32[]{:S(2)}, u32[]{:S(2)}) async-start(f32[4,2,3,8,320]{4,3,2,1,0:T(8,128)} %get-tuple-element.112), calls=%async_computation.6 | async-start | bytes 589824 | tf_op jit(solution)/shard_map/all_to_all | solution.py:197
  121.2 5.9 %collective-permute-start.12 = (f32[2,2,8,320]{3,2,1,0:T(8,128)S(1)}, f32[2,2,8,320]{3,2,1,0:T(8,128)S(1)}, u32[]{:S(2)}, u32[]{:S(2)}) collective-permute-start(f32[2,2,8,320]{3,2,1,0:T(8,128)S(1)} %get-tuple-element.111), channel_id=1, source_target_pairs={{0,1},{1,0},{2,3},{3,2},{4,5},{5,4},{6,7},{7,6},{8,9},{9,8},{10,11... | collective-permute-start | bytes 122888 | tf_op jit(solution)/shard_map/ppermute | solution.py:202
  129.0 4.2 %all-to-all-start.7 = ((f32[4,2,3,8,320]{4,3,2,1,0:T(8,128)}), f32[4,2,3,8,320]{4,3,2,1,0:T(8,128)S(1)}, u32[]{:S(2)}, u32[]{:S(2)}) async-start(f32[4,2,3,8,320]{4,3,2,1,0:T(8,128)} %get-tuple-element.117), calls=%async_computation.7 | async-start | bytes 589824 | tf_op jit(solution)/shard_map/all_to_all | solution.py:197
  137.7 4.3 %collective-permute-start.14 = (f32[2,2,8,320]{3,2,1,0:T(8,128)S(1)}, f32[2,2,8,320]{3,2,1,0:T(8,128)S(1)}, u32[]{:S(2)}, u32[]{:S(2)}) collective-permute-start(f32[2,2,8,320]{3,2,1,0:T(8,128)S(1)} %get-tuple-element.116), channel_id=1, source_target_pairs={{0,1},{1,0},{2,3},{3,2},{4,5},{5,4},{6,7},{7,6},{8,9},{9,8},{10,11... | collective-permute-start | bytes 122888 | tf_op jit(solution)/shard_map/ppermute | solution.py:202
  144.0 4.2 %all-to-all-start.8 = ((f32[4,2,3,8,320]{4,3,2,1,0:T(8,128)}), f32[4,2,3,8,320]{4,3,2,1,0:T(8,128)S(1)}, u32[]{:S(2)}, u32[]{:S(2)}) async-start(f32[4,2,3,8,320]{4,3,2,1,0:T(8,128)} %get-tuple-element.122), calls=%async_computation.8 | async-start | bytes 589824 | tf_op jit(solution)/shard_map/all_to_all | solution.py:197
  152.7 5.9 %collective-permute-start.16 = (f32[2,2,8,320]{3,2,1,0:T(8,128)S(1)}, f32[2,2,8,320]{3,2,1,0:T(8,128)S(1)}, u32[]{:S(2)}, u32[]{:S(2)}) collective-permute-start(f32[2,2,8,320]{3,2,1,0:T(8,128)S(1)} %get-tuple-element.121), channel_id=1, source_target_pairs={{0,1},{1,0},{2,3},{3,2},{4,5},{5,4},{6,7},{7,6},{8,9},{9,8},{10,11... | collective-permute-start | bytes 122888 | tf_op jit(solution)/shard_map/ppermute | solution.py:202
  169.3 4.3 %collective-permute-start.18 = (f32[2,2,8,320]{3,2,1,0:T(8,128)S(1)}, f32[2,2,8,320]{3,2,1,0:T(8,128)S(1)}, u32[]{:S(2)}, u32[]{:S(2)}) collective-permute-start(f32[2,2,8,320]{3,2,1,0:T(8,128)S(1)} %get-tuple-element.126), channel_id=1, source_target_pairs={{0,1},{1,0},{2,3},{3,2},{4,5},{5,4},{6,7},{7,6},{8,9},{9,8},{10,11... | collective-permute-start | bytes 122888 | tf_op jit(solution)/shard_map/ppermute | solution.py:202
  184.2 6.0 %collective-permute-start.20 = (f32[2,2,8,320]{3,2,1,0:T(8,128)S(1)}, f32[2,2,8,320]{3,2,1,0:T(8,128)S(1)}, u32[]{:S(2)}, u32[]{:S(2)}) collective-permute-start(f32[2,2,8,320]{3,2,1,0:T(8,128)S(1)} %get-tuple-element.131), channel_id=1, source_target_pairs={{0,1},{1,0},{2,3},{3,2},{4,5},{5,4},{6,7},{7,6},{8,9},{9,8},{10,11... | collective-permute-start | bytes 122888 | tf_op jit(solution)/shard_map/ppermute | solution.py:202
  200.8 4.3 %collective-permute-start.22 = (f32[2,2,8,320]{3,2,1,0:T(8,128)S(1)}, f32[2,2,8,320]{3,2,1,0:T(8,128)S(1)}, u32[]{:S(2)}, u32[]{:S(2)}) collective-permute-start(f32[2,2,8,320]{3,2,1,0:T(8,128)S(1)} %get-tuple-element.136), channel_id=1, source_target_pairs={{0,1},{1,0},{2,3},{3,2},{4,5},{5,4},{6,7},{7,6},{8,9},{9,8},{10,11... | collective-permute-start | bytes 122888 | tf_op jit(solution)/shard_map/ppermute | solution.py:202
  215.8 5.9 %collective-permute-start.24 = (f32[2,2,8,320]{3,2,1,0:T(8,128)S(1)}, f32[2,2,8,320]{3,2,1,0:T(8,128)S(1)}, u32[]{:S(2)}, u32[]{:S(2)}) collective-permute-start(f32[2,2,8,320]{3,2,1,0:T(8,128)S(1)} %get-tuple-element.141), channel_id=1, source_target_pairs={{0,1},{1,0},{2,3},{3,2},{4,5},{5,4},{6,7},{7,6},{8,9},{9,8},{10,11... | collective-permute-start | bytes 122888 | tf_op jit(solution)/shard_map/ppermute | solution.py:202
  232.4 4.3 %collective-permute-start.26 = (f32[2,2,8,320]{3,2,1,0:T(8,128)S(1)}, f32[2,2,8,320]{3,2,1,0:T(8,128)S(1)}, u32[]{:S(2)}, u32[]{:S(2)}) collective-permute-start(f32[2,2,8,320]{3,2,1,0:T(8,128)S(1)} %get-tuple-element.146), channel_id=1, source_target_pairs={{0,1},{1,0},{2,3},{3,2},{4,5},{5,4},{6,7},{7,6},{8,9},{9,8},{10,11... | collective-permute-start | bytes 122888 | tf_op jit(solution)/shard_map/ppermute | solution.py:202
  247.3 5.9 %collective-permute-start.28 = (f32[2,2,8,320]{3,2,1,0:T(8,128)S(1)}, f32[2,2,8,320]{3,2,1,0:T(8,128)S(1)}, u32[]{:S(2)}, u32[]{:S(2)}) collective-permute-start(f32[2,2,8,320]{3,2,1,0:T(8,128)S(1)} %get-tuple-element.151), channel_id=1, source_target_pairs={{0,1},{1,0},{2,3},{3,2},{4,5},{5,4},{6,7},{7,6},{8,9},{9,8},{10,11... | collective-permute-start | bytes 122888 | tf_op jit(solution)/shard_map/ppermute | solution.py:202
  263.9 4.3 %collective-permute-start.30 = (f32[2,2,8,320]{3,2,1,0:T(8,128)S(1)}, f32[2,2,8,320]{3,2,1,0:T(8,128)S(1)}, u32[]{:S(2)}, u32[]{:S(2)}) collective-permute-start(f32[2,2,8,320]{3,2,1,0:T(8,128)S(1)} %get-tuple-element.156), channel_id=1, source_target_pairs={{0,1},{1,0},{2,3},{3,2},{4,5},{5,4},{6,7},{7,6},{8,9},{9,8},{10,11... | collective-permute-start | bytes 122888 | tf_op jit(solution)/shard_map/ppermute | solution.py:202
  (180 shorter events, 146.3 us)
Async XLA Ops:
  3.6 29.8 %all-to-all-start = ((f32[4,2,3,8,320]{4,3,2,1,0:T(8,128)}), f32[4,2,3,8,320]{4,3,2,1,0:T(8,128)S(1)}, u32[]{:S(2)}, u32[]{:S(2)}) async-start(f32[4,2,3,8,320]{4,3,2,1,0:T(8,128)} %get-tuple-element.82), calls=%async_computation | async-start | bytes 589824 | tf_op jit(solution)/shard_map/all_to_all | solution.py:197
  8.5 24.6 %collective-permute-start.1 = (f32[2,2,8,320]{3,2,1,0:T(8,128)S(1)}, f32[2,2,8,320]{3,2,1,0:T(8,128)S(1)}, u32[]{:S(2)}, u32[]{:S(2)}) collective-permute-start(f32[2,2,8,320]{3,2,1,0:T(8,128)S(1)} %get-tuple-element.83), channel_id=1, source_target_pairs={{0,127},{1,2},{2,1},{3,4},{4,3},{5,6},{6,5},{7,8},{8,7},{9,10},{10... | collective-permute-start | bytes 122888 | tf_op jit(solution)/shard_map/ppermute | solution.py:198
  21.0 12.3 %collective-permute-start = (f32[2,2,8,320]{3,2,1,0:T(8,128)S(1)}, f32[2,2,8,320]{3,2,1,0:T(8,128)S(1)}, u32[]{:S(2)}, u32[]{:S(2)}) collective-permute-start(f32[2,2,8,320]{3,2,1,0:T(8,128)S(1)} %get-tuple-element.81), channel_id=1, source_target_pairs={{0,1},{1,0},{2,3},{3,2},{4,5},{5,4},{6,7},{7,6},{8,9},{9,8},{10,11... | collective-permute-start | bytes 122888 | tf_op jit(solution)/shard_map/ppermute | solution.py:202
  34.5 12.8 %all-to-all-start.1 = ((f32[4,2,3,8,320]{4,3,2,1,0:T(8,128)}), f32[4,2,3,8,320]{4,3,2,1,0:T(8,128)S(1)}, u32[]{:S(2)}, u32[]{:S(2)}) async-start(f32[4,2,3,8,320]{4,3,2,1,0:T(8,128)} %get-tuple-element.87), calls=%async_computation.1 | async-start | bytes 589824 | tf_op jit(solution)/shard_map/all_to_all | solution.py:197
  48.4 16.4 %all-to-all-start.2 = ((f32[4,2,3,8,320]{4,3,2,1,0:T(8,128)}), f32[4,2,3,8,320]{4,3,2,1,0:T(8,128)S(1)}, u32[]{:S(2)}, u32[]{:S(2)}) async-start(f32[4,2,3,8,320]{4,3,2,1,0:T(8,128)} %get-tuple-element.92), calls=%async_computation.2 | async-start | bytes 589824 | tf_op jit(solution)/shard_map/all_to_all | solution.py:197
  52.6 11.3 %collective-permute-start.5 = (f32[2,2,8,320]{3,2,1,0:T(8,128)S(1)}, f32[2,2,8,320]{3,2,1,0:T(8,128)S(1)}, u32[]{:S(2)}, u32[]{:S(2)}) collective-permute-start(f32[2,2,8,320]{3,2,1,0:T(8,128)S(1)} %get-tuple-element.93), channel_id=1, source_target_pairs={{0,127},{1,2},{2,1},{3,4},{4,3},{5,6},{6,5},{7,8},{8,7},{9,10},{10... | collective-permute-start | bytes 122888 | tf_op jit(solution)/shard_map/ppermute | solution.py:198
  65.9 13.9 %all-to-all-start.3 = ((f32[4,2,3,8,320]{4,3,2,1,0:T(8,128)}), f32[4,2,3,8,320]{4,3,2,1,0:T(8,128)S(1)}, u32[]{:S(2)}, u32[]{:S(2)}) async-start(f32[4,2,3,8,320]{4,3,2,1,0:T(8,128)} %get-tuple-element.97), calls=%async_computation.3 | async-start | bytes 589824 | tf_op jit(solution)/shard_map/all_to_all | solution.py:197
  80.9 15.5 %all-to-all-start.4 = ((f32[4,2,3,8,320]{4,3,2,1,0:T(8,128)}), f32[4,2,3,8,320]{4,3,2,1,0:T(8,128)S(1)}, u32[]{:S(2)}, u32[]{:S(2)}) async-start(f32[4,2,3,8,320]{4,3,2,1,0:T(8,128)} %get-tuple-element.102), calls=%async_computation.4 | async-start | bytes 589824 | tf_op jit(solution)/shard_map/all_to_all | solution.py:197
  85.1 10.4 %collective-permute-start.9 = (f32[2,2,8,320]{3,2,1,0:T(8,128)S(1)}, f32[2,2,8,320]{3,2,1,0:T(8,128)S(1)}, u32[]{:S(2)}, u32[]{:S(2)}) collective-permute-start(f32[2,2,8,320]{3,2,1,0:T(8,128)S(1)} %get-tuple-element.103), channel_id=1, source_target_pairs={{0,127},{1,2},{2,1},{3,4},{4,3},{5,6},{6,5},{7,8},{8,7},{9,10},{10... | collective-permute-start | bytes 122888 | tf_op jit(solution)/shard_map/ppermute | solution.py:198
  97.4 13.9 %all-to-all-start.5 = ((f32[4,2,3,8,320]{4,3,2,1,0:T(8,128)}), f32[4,2,3,8,320]{4,3,2,1,0:T(8,128)S(1)}, u32[]{:S(2)}, u32[]{:S(2)}) async-start(f32[4,2,3,8,320]{4,3,2,1,0:T(8,128)} %get-tuple-element.107), calls=%async_computation.5 | async-start | bytes 589824 | tf_op jit(solution)/shard_map/all_to_all | solution.py:197
  112.4 15.5 %all-to-all-start.6 = ((f32[4,2,3,8,320]{4,3,2,1,0:T(8,128)}), f32[4,2,3,8,320]{4,3,2,1,0:T(8,128)S(1)}, u32[]{:S(2)}, u32[]{:S(2)}) async-start(f32[4,2,3,8,320]{4,3,2,1,0:T(8,128)} %get-tuple-element.112), calls=%async_computation.6 | async-start | bytes 589824 | tf_op jit(solution)/shard_map/all_to_all | solution.py:197
  116.7 10.4 %collective-permute-start.13 = (f32[2,2,8,320]{3,2,1,0:T(8,128)S(1)}, f32[2,2,8,320]{3,2,1,0:T(8,128)S(1)}, u32[]{:S(2)}, u32[]{:S(2)}) collective-permute-start(f32[2,2,8,320]{3,2,1,0:T(8,128)S(1)} %get-tuple-element.113), channel_id=1, source_target_pairs={{0,127},{1,2},{2,1},{3,4},{4,3},{5,6},{6,5},{7,8},{8,7},{9,10},{10... | collective-permute-start | bytes 122888 | tf_op jit(solution)/shard_map/ppermute | solution.py:198
  129.0 13.9 %all-to-all-start.7 = ((f32[4,2,3,8,320]{4,3,2,1,0:T(8,128)}), f32[4,2,3,8,320]{4,3,2,1,0:T(8,128)S(1)}, u32[]{:S(2)}, u32[]{:S(2)}) async-start(f32[4,2,3,8,320]{4,3,2,1,0:T(8,128)} %get-tuple-element.117), calls=%async_computation.7 | async-start | bytes 589824 | tf_op jit(solution)/shard_map/all_to_all | solution.py:197
  144.0 15.5 %all-to-all-start.8 = ((f32[4,2,3,8,320]{4,3,2,1,0:T(8,128)}), f32[4,2,3,8,320]{4,3,2,1,0:T(8,128)S(1)}, u32[]{:S(2)}, u32[]{:S(2)}) async-start(f32[4,2,3,8,320]{4,3,2,1,0:T(8,128)} %get-tuple-element.122), calls=%async_computation.8 | async-start | bytes 589824 | tf_op jit(solution)/shard_map/all_to_all | solution.py:197
  148.2 10.4 %collective-permute-start.17 = (f32[2,2,8,320]{3,2,1,0:T(8,128)S(1)}, f32[2,2,8,320]{3,2,1,0:T(8,128)S(1)}, u32[]{:S(2)}, u32[]{:S(2)}) collective-permute-start(f32[2,2,8,320]{3,2,1,0:T(8,128)S(1)} %get-tuple-element.123), channel_id=1, source_target_pairs={{0,127},{1,2},{2,1},{3,4},{4,3},{5,6},{6,5},{7,8},{8,7},{9,10},{10... | collective-permute-start | bytes 122888 | tf_op jit(solution)/shard_map/ppermute | solution.py:198
  160.5 13.9 %all-to-all-start.9 = ((f32[4,2,3,8,320]{4,3,2,1,0:T(8,128)}), f32[4,2,3,8,320]{4,3,2,1,0:T(8,128)S(1)}, u32[]{:S(2)}, u32[]{:S(2)}) async-start(f32[4,2,3,8,320]{4,3,2,1,0:T(8,128)} %get-tuple-element.127), calls=%async_computation.9 | async-start | bytes 589824 | tf_op jit(solution)/shard_map/all_to_all | solution.py:197
  175.5 15.5 %all-to-all-start.10 = ((f32[4,2,3,8,320]{4,3,2,1,0:T(8,128)}), f32[4,2,3,8,320]{4,3,2,1,0:T(8,128)S(1)}, u32[]{:S(2)}, u32[]{:S(2)}) async-start(f32[4,2,3,8,320]{4,3,2,1,0:T(8,128)} %get-tuple-element.132), calls=%async_computation.10 | async-start | bytes 589824 | tf_op jit(solution)/shard_map/all_to_all | solution.py:197
  179.8 10.5 %collective-permute-start.21 = (f32[2,2,8,320]{3,2,1,0:T(8,128)S(1)}, f32[2,2,8,320]{3,2,1,0:T(8,128)S(1)}, u32[]{:S(2)}, u32[]{:S(2)}) collective-permute-start(f32[2,2,8,320]{3,2,1,0:T(8,128)S(1)} %get-tuple-element.133), channel_id=1, source_target_pairs={{0,127},{1,2},{2,1},{3,4},{4,3},{5,6},{6,5},{7,8},{8,7},{9,10},{10... | collective-permute-start | bytes 122888 | tf_op jit(solution)/shard_map/ppermute | solution.py:198
  192.1 13.9 %all-to-all-start.11 = ((f32[4,2,3,8,320]{4,3,2,1,0:T(8,128)}), f32[4,2,3,8,320]{4,3,2,1,0:T(8,128)S(1)}, u32[]{:S(2)}, u32[]{:S(2)}) async-start(f32[4,2,3,8,320]{4,3,2,1,0:T(8,128)} %get-tuple-element.137), calls=%async_computation.11 | async-start | bytes 589824 | tf_op jit(solution)/shard_map/all_to_all | solution.py:197
  207.1 15.5 %all-to-all-start.12 = ((f32[4,2,3,8,320]{4,3,2,1,0:T(8,128)}), f32[4,2,3,8,320]{4,3,2,1,0:T(8,128)S(1)}, u32[]{:S(2)}, u32[]{:S(2)}) async-start(f32[4,2,3,8,320]{4,3,2,1,0:T(8,128)} %get-tuple-element.142), calls=%async_computation.12 | async-start | bytes 589824 | tf_op jit(solution)/shard_map/all_to_all | solution.py:197
  223.6 13.9 %all-to-all-start.13 = ((f32[4,2,3,8,320]{4,3,2,1,0:T(8,128)}), f32[4,2,3,8,320]{4,3,2,1,0:T(8,128)S(1)}, u32[]{:S(2)}, u32[]{:S(2)}) async-start(f32[4,2,3,8,320]{4,3,2,1,0:T(8,128)} %get-tuple-element.147), calls=%async_computation.13 | async-start | bytes 589824 | tf_op jit(solution)/shard_map/all_to_all | solution.py:197
  238.6 15.5 %all-to-all-start.14 = ((f32[4,2,3,8,320]{4,3,2,1,0:T(8,128)}), f32[4,2,3,8,320]{4,3,2,1,0:T(8,128)S(1)}, u32[]{:S(2)}, u32[]{:S(2)}) async-start(f32[4,2,3,8,320]{4,3,2,1,0:T(8,128)} %get-tuple-element.152), calls=%async_computation.14 | async-start | bytes 589824 | tf_op jit(solution)/shard_map/all_to_all | solution.py:197
  242.9 10.4 %collective-permute-start.29 = (f32[2,2,8,320]{3,2,1,0:T(8,128)S(1)}, f32[2,2,8,320]{3,2,1,0:T(8,128)S(1)}, u32[]{:S(2)}, u32[]{:S(2)}) collective-permute-start(f32[2,2,8,320]{3,2,1,0:T(8,128)S(1)} %get-tuple-element.153), channel_id=1, source_target_pairs={{0,127},{1,2},{2,1},{3,4},{4,3},{5,6},{6,5},{7,8},{8,7},{9,10},{10... | collective-permute-start | bytes 122888 | tf_op jit(solution)/shard_map/ppermute | solution.py:198
  255.2 13.9 %all-to-all-start.15 = ((f32[4,2,3,8,320]{4,3,2,1,0:T(8,128)}), f32[4,2,3,8,320]{4,3,2,1,0:T(8,128)S(1)}, u32[]{:S(2)}, u32[]{:S(2)}) async-start(f32[4,2,3,8,320]{4,3,2,1,0:T(8,128)} %get-tuple-element.157), calls=%async_computation.15 | async-start | bytes 589824 | tf_op jit(solution)/shard_map/all_to_all | solution.py:197
  (52 other events, 264.1 us)

commit v2 on v1

v2 whole, which is shorter than its diff:
```python
import functools
import math

import jax
import jax.numpy as jnp
import numpy as np
from jax import lax
from jax.experimental import pallas as pl
from jax.experimental.pallas import tpu as pltpu
from jax.sharding import PartitionSpec as P

NT = 8
ITERS = 16
SCALE = 0.15
REACH = 2
INST = 2
NEAR_PICK, FAR_PICK, LIVE, NEAR_SEND, FAR_SEND, SAME, CROSS, TABLE = 0, 3, 6, 9, 13, 17, 21, 32
VMEM = pl.BlockSpec(memory_space=pltpu.VMEM)
HBM = pl.BlockSpec(memory_space=pltpu.HBM)
SMEM = pl.BlockSpec(memory_space=pltpu.SMEM)


def time_matrix():
    out = np.zeros((NT, NT))
    for j in range(NT):
        for i in range(NT):
            if i != j and (j - i) % NT != NT // 2:
                angle = math.pi * (j - i) / NT
                out[j, i] = 0.5 * (-1.0) ** (j - i) * math.cos(angle) / math.sin(angle)
    return out.astype(np.float32)


def swapped(block):
    return pltpu.roll(block, block.shape[1] // 2, 1)


def product(block, matrix):
    rows, lanes = block.shape
    width = lanes // 2
    parts = []
    for half in (block[:, :width], swapped(block)[:, :width]):
        for _ in range(3):
            part = half.astype(jnp.bfloat16).astype(jnp.float32)
            parts.append(part)
            half = half - part
    stacked = jnp.concatenate(parts, axis=0).astype(jnp.bfloat16)
    out = jnp.dot(stacked, matrix, preferred_element_type=jnp.float32)
    first, second = (
        out[n : n + rows] + out[n + rows : n + 2 * rows] + out[n + 2 * rows : n + 3 * rows]
        for n in (0, 3 * rows)
    )
    lane = lax.broadcasted_iota(jnp.int32, (rows, lanes), 1)
    return jnp.where(lane < width, first, second)


def chosen(mask_ref, row, yes, no):
    return jnp.where(mask_ref[pl.ds(row, 1), :] > 0.0, yes, no)


def listed(tables_ref, first, entry, blocks_ref):
    row = first + 2 * entry
    middle = chosen(tables_ref, row, blocks_ref[1], blocks_ref[0])
    return chosen(tables_ref, row + 1, blocks_ref[2], middle)


def tables_kernel(place_ref, slots_ref, lists_ref, pad_ref, weights_ref, tables_ref):
    lanes = tables_ref.shape[1]
    side = place_ref[0]
    first = INST * place_ref[1]
    rows = slots_ref.shape[0]
    lane = lax.broadcasted_iota(jnp.int32, (1, lanes), 1)

    def put(row, left, right):
        tables_ref[pl.ds(row, 1), :] = jnp.where(lane < lanes // 2, left, right)

    def flag(row, holds):
        value = jnp.where(holds, 1.0, 0.0).astype(jnp.float32)
        put(row, value, value)

    for r in range(rows):
        flag(NEAR_PICK + r, slots_ref[r, REACH - side] == 1 + (REACH + rows) * (1 - side))
        flag(FAR_PICK + r, slots_ref[r, 1 + side] == 1 + (REACH + rows) * side)
        flag(LIVE + r, r < rows - pad_ref[0])
    for e in range(REACH):
        for v in (1, 2):
            flag(NEAR_SEND + 2 * e + v - 1, lists_ref[REACH - REACH * side + e] == v)
            flag(FAR_SEND + 2 * e + v - 1, lists_ref[REACH * side + e] == v)
    for p in range(NT // INST):
        put(SAME + p, weights_ref[2 * p, first], weights_ref[2 * p + 1, first + 1])
        put(CROSS + p, weights_ref[2 * p, first + 1], weights_ref[2 * p + 1, first])


def send_copies(block_ref, peers_ref, sems, r):
    return [
        pltpu.make_async_copy(block_ref.at[r], peers_ref.at[p, r], sems.at[r, p])
        for p in range(peers_ref.shape[0])
    ]


def begin_kernel(place_ref, lists_ref, adjoint_ref, near_ref, far_ref, peers_ref, sems):
    side = place_ref[0]
    rows = adjoint_ref.shape[0]
    copies = [c for r in range(rows) for c in send_copies(adjoint_ref, peers_ref, sems, r)]
    for copy in copies:
        copy.start()
    for e in range(REACH):
        near_ref[e] = adjoint_ref[lists_ref[REACH - REACH * side + e]]
        far_ref[e] = adjoint_ref[lists_ref[REACH * side + e]]
    for copy in copies:
        copy.wait()


def here_kernel(tables_ref, adjoint_ref, near_ref, own_j_ref, near_j_ref, source_ref, out_ref):
    other = 1 - lax.rem(lax.axis_index("cell"), 2)
    for r in range(adjoint_ref.shape[0]):
        own = product(adjoint_ref[r], own_j_ref[r])
        block = chosen(tables_ref, NEAR_PICK + r, near_ref[other, 1], near_ref[other, 0])
        out_ref[r] = source_ref[r] - (own + product(block, near_j_ref[r]))


def update_kernel(
    last, tables_ref, far_ref, far_j_ref, peers_ref, partial_ref, adjoint_ref, volume_ref,
    step_ref, *outs
):
    rows, _, lanes = adjoint_ref.shape
    width = lanes // 2
    copies = []
    for r in range(rows):
        block = chosen(tables_ref, FAR_PICK + r, far_ref[1], far_ref[0])
        flux = product(block, far_j_ref[r])
        same = cross = None
        for p in range(peers_ref.shape[0]):
            one = tables_ref[pl.ds(SAME + p, 1), :] * peers_ref[p, r]
            two = tables_ref[pl.ds(CROSS + p, 1), :] * peers_ref[p, r]
            same, cross = (one, two) if same is None else (same + one, cross + two)
        coupled = same + swapped(cross)
        scale = SCALE * volume_ref[pl.ds(r, 1), :]
        live = tables_ref[pl.ds(LIVE + r, 1), :]
        residual = live * (partial_ref[r] - flux - scale * coupled)
        new = adjoint_ref[r] + step_ref[pl.ds(r, 1), :] * residual
        if last:
            for value, out_ref in zip((new, residual), outs):
                out_ref[0, r] = value[:, :width]
                out_ref[1, r] = swapped(value)[:, :width]
            continue
        outs[0][r] = new
        started = send_copies(outs[0], outs[3], outs[4], r)
        for copy in started:
            copy.start()
        copies += started
    if not last:
        for e in range(REACH):
            outs[1][e] = listed(tables_ref, NEAR_SEND, e, outs[0])
            outs[2][e] = listed(tables_ref, FAR_SEND, e, outs[0])
    for copy in copies:
        copy.wait()


def call(kernel, ins, outs, *args, scratch=(), cost=None):
    spaces = {"s": SMEM, "v": VMEM, "a": HBM}
    return pl.pallas_call(
        kernel,
        in_specs=[spaces[c] for c in ins],
        out_specs=[spaces[c] for c, _ in outs],
        out_shape=[jax.ShapeDtypeStruct(*o) for _, o in outs],
        scratch_shapes=list(scratch),
        compiler_params=pltpu.CompilerParams(vmem_limit_bytes=4 << 20),
        cost_estimate=cost and pl.CostEstimate(flops=cost, bytes_accessed=0, transcendentals=0),
    )(*args)


def side_by_side(blocks):
    return jnp.concatenate([blocks[0], blocks[1]], axis=-1)


def on_device(adjoint, source, jacobian, volume, step, slots, lists, pads):
    shape = adjoint.shape
    _, rows, objectives, width = shape
    peers = lax.axis_size("inst")
    cells = lax.axis_size("cell")
    near_groups = [[i, i + 1] for i in range(0, cells, 2)]
    far_pairs = [(i, (i + 1 if i % 2 else i - 1) % cells) for i in range(cells)]
    side = lax.rem(lax.axis_index("cell"), 2).astype(jnp.int32)
    place = jnp.stack([side, lax.axis_index("inst").astype(jnp.int32)])
    f32 = jnp.float32
    lanes = 2 * width
    block = ((rows, objectives, lanes), f32)
    halo = ((REACH, objectives, lanes), f32)
    gathered = ((peers,) + block[0], f32)
    sends = [pltpu.SemaphoreType.DMA((rows, peers))]
    listed_out = (("v", halo), ("v", halo), ("a", gathered))
    adjoint = side_by_side(adjoint)
    near, far, spread = call(
        begin_kernel, "ssv", listed_out, place, lists, adjoint, scratch=sends
    )
    tables = call(
        tables_kernel, "sssss", (("v", ((TABLE, lanes), f32)),), place, slots, lists, pads,
        jnp.asarray(time_matrix()),
    )[0]
    source = side_by_side(source)
    volume = jnp.concatenate([volume, volume], axis=-1)
    step = jnp.concatenate([step, step], axis=-1)
    own_j, near_j, far_j = (
        side_by_side(lax.dynamic_index_in_dim(jacobian, k, axis=2, keepdims=False))
        for k in (0, REACH - side, 1 + side)
    )
    for sweep in range(ITERS):
        last = sweep == ITERS - 1
        spread = lax.all_to_all(spread, "inst", 0, 0)
        far = lax.ppermute(far, "cell", far_pairs)
        near = lax.all_gather(near, "cell", axis_index_groups=near_groups)
        partial = call(
            here_kernel, "vvvvvv", (("v", block),), tables, adjoint, near, own_j, near_j, source
        )[0]
        result = call(
            functools.partial(update_kernel, last), "vvvvvvvv",
            (("v", (shape, f32)),) * 2 if last else (("v", block),) + listed_out,
            tables, far, far_j, spread, partial, adjoint, volume, step,
            scratch=[] if last else sends,
        )
        if last:
            return result[0], result[1]
        adjoint, near, far, spread = result


def solution(mesh):
    return jax.shard_map(
        on_device,
        mesh=mesh,
        in_specs=(
            P("inst", "cell", None, None),
            P("inst", "cell", None, None),
            P("inst", "cell", None, None, None),
            P("cell", None),
            P("cell", None),
            P("cell", None),
            P("cell"),
            P("cell"),
        ),
        out_specs=(P("inst", "cell", None, None), P("inst", "cell", None, None)),
        check_vma=False,
    )
```

time: 273 us -> 254 us (0.930)
  the two profiles are of different devices: /device:TPU:1 before, /device:TPU:2 now
where the time goes in v2:
time: 254 us; the launch traced here: 251 us
  starting transfers between devices  141 us (56%)
  Pallas kernels  30.8 us (12%)
  blocking collectives  30 us (12%)
  local copies, waits for them, and re-layouts  24.3 us (10%)
  waiting for transfers between devices  21.4 us (8%)
    all_to_all x16, starting transfers between devices, on_device(): spread = lax.all_to_all(spread, 'inst', 0, 0)  77 us
    ppermute x16, starting transfers between devices, on_device(): far = lax.ppermute(far, 'cell', far_pairs)  64.2 us
    pallas_call x34, Pallas kernels, call(): pl.pallas_call(kernel, in_specs=[spaces[c] for c in ins], out_specs=[spac...  30.8 us
    all_gather x16, blocking collectives, on_device(): near = lax.all_gather(near, 'cell', axis_index_groups=near_groups)  30 us
    ppermute x16, waiting for transfers between devices, on_device(): far = lax.ppermute(far, 'cell', far_pairs)  21.4 us
    unnamed x44, local copies, waits for them, and re-layouts  20 us
  transfers between devices with their start and end apart: 32, of which 15 were waited for; matrix products, arithmetic and copies ran while one was open for 2% of the time, Pallas kernels for 4%

profile of v2, /device:TPU:2, one launch (start us, length us, event | category | flops | bytes accessed | tf_op | source)
XLA Modules:
  0.0 251.1 jit_solution(17124849584310353063)
XLA Ops:
  3.6 13.3 %collective-permute-start = (f32[2,8,640]{2,1,0:T(8,128)S(1)}, f32[2,8,640]{2,1,0:T(8,128)S(1)}, u32[]{:S(2)}, u32[]{:S(2)}) collective-permute-start(f32[2,8,640]{2,1,0:T(8,128)S(1)} %get-tuple-element.65), channel_id=1, source_target_pairs={{0,127},{1,2},{2,1},{3,4},{4,3},{5,6},{6,5},{7,8},{8,7},{9,10},{10... | collective-permute-start | bytes 122888 | tf_op jit(solution)/shard_map/ppermute | solution.py:210
  16.9 4.8 %all-to-all-start = ((f32[4,3,8,640]{3,2,1,0:T(8,128)}), f32[4,3,8,640]{3,2,1,0:T(8,128)S(1)}, u32[]{:S(2)}, u32[]{:S(2)}) async-start(f32[4,3,8,640]{3,2,1,0:T(8,128)} %get-tuple-element.66), calls=%async_computation | async-start | bytes 491520 | tf_op jit(solution)/shard_map/all_to_all | solution.py:209
  31.9 4.8 %all-to-all-start.1 = ((f32[4,3,8,640]{3,2,1,0:T(8,128)}), f32[4,3,8,640]{3,2,1,0:T(8,128)S(1)}, u32[]{:S(2)}, u32[]{:S(2)}) async-start(f32[4,3,8,640]{3,2,1,0:T(8,128)} %get-tuple-element.69), calls=%async_computation.1 | async-start | bytes 491520 | tf_op jit(solution)/shard_map/all_to_all | solution.py:209
  46.5 4.8 %all-to-all-start.2 = ((f32[4,3,8,640]{3,2,1,0:T(8,128)}), f32[4,3,8,640]{3,2,1,0:T(8,128)S(1)}, u32[]{:S(2)}, u32[]{:S(2)}) async-start(f32[4,3,8,640]{3,2,1,0:T(8,128)} %get-tuple-element.73), calls=%async_computation.2 | async-start | bytes 491520 | tf_op jit(solution)/shard_map/all_to_all | solution.py:209
  61.1 4.8 %all-to-all-start.3 = ((f32[4,3,8,640]{3,2,1,0:T(8,128)}), f32[4,3,8,640]{3,2,1,0:T(8,128)S(1)}, u32[]{:S(2)}, u32[]{:S(2)}) async-start(f32[4,3,8,640]{3,2,1,0:T(8,128)} %get-tuple-element.77), calls=%async_computation.3 | async-start | bytes 491520 | tf_op jit(solution)/shard_map/all_to_all | solution.py:209
  75.7 4.8 %all-to-all-start.4 = ((f32[4,3,8,640]{3,2,1,0:T(8,128)}), f32[4,3,8,640]{3,2,1,0:T(8,128)S(1)}, u32[]{:S(2)}, u32[]{:S(2)}) async-start(f32[4,3,8,640]{3,2,1,0:T(8,128)} %get-tuple-element.81), calls=%async_computation.4 | async-start | bytes 491520 | tf_op jit(solution)/shard_map/all_to_all | solution.py:209
  80.6 3.5 %collective-permute-start.4 = (f32[2,8,640]{2,1,0:T(8,128)S(1)}, f32[2,8,640]{2,1,0:T(8,128)S(1)}, u32[]{:S(2)}, u32[]{:S(2)}) collective-permute-start(f32[2,8,640]{2,1,0:T(8,128)S(1)} %get-tuple-element.80), channel_id=1, source_target_pairs={{0,127},{1,2},{2,1},{3,4},{4,3},{5,6},{6,5},{7,8},{8,7},{9,10},{10... | collective-permute-start | bytes 122888 | tf_op jit(solution)/shard_map/ppermute | solution.py:210
  90.4 4.8 %all-to-all-start.5 = ((f32[4,3,8,640]{3,2,1,0:T(8,128)}), f32[4,3,8,640]{3,2,1,0:T(8,128)S(1)}, u32[]{:S(2)}, u32[]{:S(2)}) async-start(f32[4,3,8,640]{3,2,1,0:T(8,128)} %get-tuple-element.85), calls=%async_computation.5 | async-start | bytes 491520 | tf_op jit(solution)/shard_map/all_to_all | solution.py:209
  105.0 4.8 %all-to-all-start.6 = ((f32[4,3,8,640]{3,2,1,0:T(8,128)}), f32[4,3,8,640]{3,2,1,0:T(8,128)S(1)}, u32[]{:S(2)}, u32[]{:S(2)}) async-start(f32[4,3,8,640]{3,2,1,0:T(8,128)} %get-tuple-element.89), calls=%async_computation.6 | async-start | bytes 491520 | tf_op jit(solution)/shard_map/all_to_all | solution.py:209
  119.6 4.8 %all-to-all-start.7 = ((f32[4,3,8,640]{3,2,1,0:T(8,128)}), f32[4,3,8,640]{3,2,1,0:T(8,128)S(1)}, u32[]{:S(2)}, u32[]{:S(2)}) async-start(f32[4,3,8,640]{3,2,1,0:T(8,128)} %get-tuple-element.93), calls=%async_computation.7 | async-start | bytes 491520 | tf_op jit(solution)/shard_map/all_to_all | solution.py:209
  134.2 4.8 %all-to-all-start.8 = ((f32[4,3,8,640]{3,2,1,0:T(8,128)}), f32[4,3,8,640]{3,2,1,0:T(8,128)S(1)}, u32[]{:S(2)}, u32[]{:S(2)}) async-start(f32[4,3,8,640]{3,2,1,0:T(8,128)} %get-tuple-element.97), calls=%async_computation.8 | async-start | bytes 491520 | tf_op jit(solution)/shard_map/all_to_all | solution.py:209
  139.0 3.5 %collective-permute-start.8 = (f32[2,8,640]{2,1,0:T(8,128)S(1)}, f32[2,8,640]{2,1,0:T(8,128)S(1)}, u32[]{:S(2)}, u32[]{:S(2)}) collective-permute-start(f32[2,8,640]{2,1,0:T(8,128)S(1)} %get-tuple-element.96), channel_id=1, source_target_pairs={{0,127},{1,2},{2,1},{3,4},{4,3},{5,6},{6,5},{7,8},{8,7},{9,10},{10... | collective-permute-start | bytes 122888 | tf_op jit(solution)/shard_map/ppermute | solution.py:210
  148.8 4.8 %all-to-all-start.9 = ((f32[4,3,8,640]{3,2,1,0:T(8,128)}), f32[4,3,8,640]{3,2,1,0:T(8,128)S(1)}, u32[]{:S(2)}, u32[]{:S(2)}) async-start(f32[4,3,8,640]{3,2,1,0:T(8,128)} %get-tuple-element.101), calls=%async_computation.9 | async-start | bytes 491520 | tf_op jit(solution)/shard_map/all_to_all | solution.py:209
  153.6 3.5 %collective-permute-start.9 = (f32[2,8,640]{2,1,0:T(8,128)S(1)}, f32[2,8,640]{2,1,0:T(8,128)S(1)}, u32[]{:S(2)}, u32[]{:S(2)}) collective-permute-start(f32[2,8,640]{2,1,0:T(8,128)S(1)} %get-tuple-element.100), channel_id=1, source_target_pairs={{0,127},{1,2},{2,1},{3,4},{4,3},{5,6},{6,5},{7,8},{8,7},{9,10},{10... | collective-permute-start | bytes 122888 | tf_op jit(solution)/shard_map/ppermute | solution.py:210
  163.4 4.8 %all-to-all-start.10 = ((f32[4,3,8,640]{3,2,1,0:T(8,128)}), f32[4,3,8,640]{3,2,1,0:T(8,128)S(1)}, u32[]{:S(2)}, u32[]{:S(2)}) async-start(f32[4,3,8,640]{3,2,1,0:T(8,128)} %get-tuple-element.105), calls=%async_computation.10 | async-start | bytes 491520 | tf_op jit(solution)/shard_map/all_to_all | solution.py:209
  168.3 3.7 %collective-permute-start.10 = (f32[2,8,640]{2,1,0:T(8,128)S(1)}, f32[2,8,640]{2,1,0:T(8,128)S(1)}, u32[]{:S(2)}, u32[]{:S(2)}) collective-permute-start(f32[2,8,640]{2,1,0:T(8,128)S(1)} %get-tuple-element.104), channel_id=1, source_target_pairs={{0,127},{1,2},{2,1},{3,4},{4,3},{5,6},{6,5},{7,8},{8,7},{9,10},{10... | collective-permute-start | bytes 122888 | tf_op jit(solution)/shard_map/ppermute | solution.py:210
  178.1 4.8 %all-to-all-start.11 = ((f32[4,3,8,640]{3,2,1,0:T(8,128)}), f32[4,3,8,640]{3,2,1,0:T(8,128)S(1)}, u32[]{:S(2)}, u32[]{:S(2)}) async-start(f32[4,3,8,640]{3,2,1,0:T(8,128)} %get-tuple-element.109), calls=%async_computation.11 | async-start | bytes 491520 | tf_op jit(solution)/shard_map/all_to_all | solution.py:209
  192.7 4.8 %all-to-all-start.12 = ((f32[4,3,8,640]{3,2,1,0:T(8,128)}), f32[4,3,8,640]{3,2,1,0:T(8,128)S(1)}, u32[]{:S(2)}, u32[]{:S(2)}) async-start(f32[4,3,8,640]{3,2,1,0:T(8,128)} %get-tuple-element.113), calls=%async_computation.12 | async-start | bytes 491520 | tf_op jit(solution)/shard_map/all_to_all | solution.py:209
  197.5 3.5 %collective-permute-start.12 = (f32[2,8,640]{2,1,0:T(8,128)S(1)}, f32[2,8,640]{2,1,0:T(8,128)S(1)}, u32[]{:S(2)}, u32[]{:S(2)}) collective-permute-start(f32[2,8,640]{2,1,0:T(8,128)S(1)} %get-tuple-element.112), channel_id=1, source_target_pairs={{0,127},{1,2},{2,1},{3,4},{4,3},{5,6},{6,5},{7,8},{8,7},{9,10},{10... | collective-permute-start | bytes 122888 | tf_op jit(solution)/shard_map/ppermute | solution.py:210
  207.3 4.8 %all-to-all-start.13 = ((f32[4,3,8,640]{3,2,1,0:T(8,128)}), f32[4,3,8,640]{3,2,1,0:T(8,128)S(1)}, u32[]{:S(2)}, u32[]{:S(2)}) async-start(f32[4,3,8,640]{3,2,1,0:T(8,128)} %get-tuple-element.117), calls=%async_computation.13 | async-start | bytes 491520 | tf_op jit(solution)/shard_map/all_to_all | solution.py:209
  221.9 4.8 %all-to-all-start.14 = ((f32[4,3,8,640]{3,2,1,0:T(8,128)}), f32[4,3,8,640]{3,2,1,0:T(8,128)S(1)}, u32[]{:S(2)}, u32[]{:S(2)}) async-start(f32[4,3,8,640]{3,2,1,0:T(8,128)} %get-tuple-element.121), calls=%async_computation.14 | async-start | bytes 491520 | tf_op jit(solution)/shard_map/all_to_all | solution.py:209
  226.7 3.5 %collective-permute-start.14 = (f32[2,8,640]{2,1,0:T(8,128)S(1)}, f32[2,8,640]{2,1,0:T(8,128)S(1)}, u32[]{:S(2)}, u32[]{:S(2)}) collective-permute-start(f32[2,8,640]{2,1,0:T(8,128)S(1)} %get-tuple-element.120), channel_id=1, source_target_pairs={{0,127},{1,2},{2,1},{3,4},{4,3},{5,6},{6,5},{7,8},{8,7},{9,10},{10... | collective-permute-start | bytes 122888 | tf_op jit(solution)/shard_map/ppermute | solution.py:210
  236.5 4.8 %all-to-all-start.15 = ((f32[4,3,8,640]{3,2,1,0:T(8,128)}), f32[4,3,8,640]{3,2,1,0:T(8,128)S(1)}, u32[]{:S(2)}, u32[]{:S(2)}) async-start(f32[4,3,8,640]{3,2,1,0:T(8,128)} %get-tuple-element.125), calls=%async_computation.15 | async-start | bytes 491520 | tf_op jit(solution)/shard_map/all_to_all | solution.py:209
  241.3 3.5 %collective-permute-start.15 = (f32[2,8,640]{2,1,0:T(8,128)S(1)}, f32[2,8,640]{2,1,0:T(8,128)S(1)}, u32[]{:S(2)}, u32[]{:S(2)}) collective-permute-start(f32[2,8,640]{2,1,0:T(8,128)S(1)} %get-tuple-element.124), channel_id=1, source_target_pairs={{0,127},{1,2},{2,1},{3,4},{4,3},{5,6},{6,5},{7,8},{8,7},{9,10},{10... | collective-permute-start | bytes 122888 | tf_op jit(solution)/shard_map/ppermute | solution.py:210
  (143 shorter events, 134.4 us)
Async XLA Ops:
  3.6 27.1 %collective-permute-start = (f32[2,8,640]{2,1,0:T(8,128)S(1)}, f32[2,8,640]{2,1,0:T(8,128)S(1)}, u32[]{:S(2)}, u32[]{:S(2)}) collective-permute-start(f32[2,8,640]{2,1,0:T(8,128)S(1)} %get-tuple-element.65), channel_id=1, source_target_pairs={{0,127},{1,2},{2,1},{3,4},{4,3},{5,6},{6,5},{7,8},{8,7},{9,10},{10... | collective-permute-start | bytes 122888 | tf_op jit(solution)/shard_map/ppermute | solution.py:210
  16.9 13.8 %all-to-all-start = ((f32[4,3,8,640]{3,2,1,0:T(8,128)}), f32[4,3,8,640]{3,2,1,0:T(8,128)S(1)}, u32[]{:S(2)}, u32[]{:S(2)}) async-start(f32[4,3,8,640]{3,2,1,0:T(8,128)} %get-tuple-element.66), calls=%async_computation | async-start | bytes 491520 | tf_op jit(solution)/shard_map/all_to_all | solution.py:209
  31.9 13.4 %all-to-all-start.1 = ((f32[4,3,8,640]{3,2,1,0:T(8,128)}), f32[4,3,8,640]{3,2,1,0:T(8,128)S(1)}, u32[]{:S(2)}, u32[]{:S(2)}) async-start(f32[4,3,8,640]{3,2,1,0:T(8,128)} %get-tuple-element.69), calls=%async_computation.1 | async-start | bytes 491520 | tf_op jit(solution)/shard_map/all_to_all | solution.py:209
  36.7 8.6 %collective-permute-start.1 = (f32[2,8,640]{2,1,0:T(8,128)S(1)}, f32[2,8,640]{2,1,0:T(8,128)S(1)}, u32[]{:S(2)}, u32[]{:S(2)}) collective-permute-start(f32[2,8,640]{2,1,0:T(8,128)S(1)} %get-tuple-element.68), channel_id=1, source_target_pairs={{0,127},{1,2},{2,1},{3,4},{4,3},{5,6},{6,5},{7,8},{8,7},{9,10},{10... | collective-permute-start | bytes 122888 | tf_op jit(solution)/shard_map/ppermute | solution.py:210
  46.5 13.4 %all-to-all-start.2 = ((f32[4,3,8,640]{3,2,1,0:T(8,128)}), f32[4,3,8,640]{3,2,1,0:T(8,128)S(1)}, u32[]{:S(2)}, u32[]{:S(2)}) async-start(f32[4,3,8,640]{3,2,1,0:T(8,128)} %get-tuple-element.73), calls=%async_computation.2 | async-start | bytes 491520 | tf_op jit(solution)/shard_map/all_to_all | solution.py:209
  51.3 8.6 %collective-permute-start.2 = (f32[2,8,640]{2,1,0:T(8,128)S(1)}, f32[2,8,640]{2,1,0:T(8,128)S(1)}, u32[]{:S(2)}, u32[]{:S(2)}) collective-permute-start(f32[2,8,640]{2,1,0:T(8,128)S(1)} %get-tuple-element.72), channel_id=1, source_target_pairs={{0,127},{1,2},{2,1},{3,4},{4,3},{5,6},{6,5},{7,8},{8,7},{9,10},{10... | collective-permute-start | bytes 122888 | tf_op jit(solution)/shard_map/ppermute | solution.py:210
  61.1 13.4 %all-to-all-start.3 = ((f32[4,3,8,640]{3,2,1,0:T(8,128)}), f32[4,3,8,640]{3,2,1,0:T(8,128)S(1)}, u32[]{:S(2)}, u32[]{:S(2)}) async-start(f32[4,3,8,640]{3,2,1,0:T(8,128)} %get-tuple-element.77), calls=%async_computation.3 | async-start | bytes 491520 | tf_op jit(solution)/shard_map/all_to_all | solution.py:209
  65.9 8.6 %collective-permute-start.3 = (f32[2,8,640]{2,1,0:T(8,128)S(1)}, f32[2,8,640]{2,1,0:T(8,128)S(1)}, u32[]{:S(2)}, u32[]{:S(2)}) collective-permute-start(f32[2,8,640]{2,1,0:T(8,128)S(1)} %get-tuple-element.76), channel_id=1, source_target_pairs={{0,127},{1,2},{2,1},{3,4},{4,3},{5,6},{6,5},{7,8},{8,7},{9,10},{10... | collective-permute-start | bytes 122888 | tf_op jit(solution)/shard_map/ppermute | solution.py:210
  75.7 13.4 %all-to-all-start.4 = ((f32[4,3,8,640]{3,2,1,0:T(8,128)}), f32[4,3,8,640]{3,2,1,0:T(8,128)S(1)}, u32[]{:S(2)}, u32[]{:S(2)}) async-start(f32[4,3,8,640]{3,2,1,0:T(8,128)} %get-tuple-element.81), calls=%async_computation.4 | async-start | bytes 491520 | tf_op jit(solution)/shard_map/all_to_all | solution.py:209
  80.6 8.6 %collective-permute-start.4 = (f32[2,8,640]{2,1,0:T(8,128)S(1)}, f32[2,8,640]{2,1,0:T(8,128)S(1)}, u32[]{:S(2)}, u32[]{:S(2)}) collective-permute-start(f32[2,8,640]{2,1,0:T(8,128)S(1)} %get-tuple-element.80), channel_id=1, source_target_pairs={{0,127},{1,2},{2,1},{3,4},{4,3},{5,6},{6,5},{7,8},{8,7},{9,10},{10... | collective-permute-start | bytes 122888 | tf_op jit(solution)/shard_map/ppermute | solution.py:210
  90.4 13.4 %all-to-all-start.5 = ((f32[4,3,8,640]{3,2,1,0:T(8,128)}), f32[4,3,8,640]{3,2,1,0:T(8,128)S(1)}, u32[]{:S(2)}, u32[]{:S(2)}) async-start(f32[4,3,8,640]{3,2,1,0:T(8,128)} %get-tuple-element.85), calls=%async_computation.5 | async-start | bytes 491520 | tf_op jit(solution)/shard_map/all_to_all | solution.py:209
  105.0 13.4 %all-to-all-start.6 = ((f32[4,3,8,640]{3,2,1,0:T(8,128)}), f32[4,3,8,640]{3,2,1,0:T(8,128)S(1)}, u32[]{:S(2)}, u32[]{:S(2)}) async-start(f32[4,3,8,640]{3,2,1,0:T(8,128)} %get-tuple-element.89), calls=%async_computation.6 | async-start | bytes 491520 | tf_op jit(solution)/shard_map/all_to_all | solution.py:209
  119.6 13.4 %all-to-all-start.7 = ((f32[4,3,8,640]{3,2,1,0:T(8,128)}), f32[4,3,8,640]{3,2,1,0:T(8,128)S(1)}, u32[]{:S(2)}, u32[]{:S(2)}) async-start(f32[4,3,8,640]{3,2,1,0:T(8,128)} %get-tuple-element.93), calls=%async_computation.7 | async-start | bytes 491520 | tf_op jit(solution)/shard_map/all_to_all | solution.py:209
  134.2 13.4 %all-to-all-start.8 = ((f32[4,3,8,640]{3,2,1,0:T(8,128)}), f32[4,3,8,640]{3,2,1,0:T(8,128)S(1)}, u32[]{:S(2)}, u32[]{:S(2)}) async-start(f32[4,3,8,640]{3,2,1,0:T(8,128)} %get-tuple-element.97), calls=%async_computation.8 | async-start | bytes 491520 | tf_op jit(solution)/shard_map/all_to_all | solution.py:209
  139.0 8.6 %collective-permute-start.8 = (f32[2,8,640]{2,1,0:T(8,128)S(1)}, f32[2,8,640]{2,1,0:T(8,128)S(1)}, u32[]{:S(2)}, u32[]{:S(2)}) collective-permute-start(f32[2,8,640]{2,1,0:T(8,128)S(1)} %get-tuple-element.96), channel_id=1, source_target_pairs={{0,127},{1,2},{2,1},{3,4},{4,3},{5,6},{6,5},{7,8},{8,7},{9,10},{10... | collective-permute-start | bytes 122888 | tf_op jit(solution)/shard_map/ppermute | solution.py:210
  148.8 13.4 %all-to-all-start.9 = ((f32[4,3,8,640]{3,2,1,0:T(8,128)}), f32[4,3,8,640]{3,2,1,0:T(8,128)S(1)}, u32[]{:S(2)}, u32[]{:S(2)}) async-start(f32[4,3,8,640]{3,2,1,0:T(8,128)} %get-tuple-element.101), calls=%async_computation.9 | async-start | bytes 491520 | tf_op jit(solution)/shard_map/all_to_all | solution.py:209
  153.6 8.6 %collective-permute-start.9 = (f32[2,8,640]{2,1,0:T(8,128)S(1)}, f32[2,8,640]{2,1,0:T(8,128)S(1)}, u32[]{:S(2)}, u32[]{:S(2)}) collective-permute-start(f32[2,8,640]{2,1,0:T(8,128)S(1)} %get-tuple-element.100), channel_id=1, source_target_pairs={{0,127},{1,2},{2,1},{3,4},{4,3},{5,6},{6,5},{7,8},{8,7},{9,10},{10... | collective-permute-start | bytes 122888 | tf_op jit(solution)/shard_map/ppermute | solution.py:210
  163.4 13.4 %all-to-all-start.10 = ((f32[4,3,8,640]{3,2,1,0:T(8,128)}), f32[4,3,8,640]{3,2,1,0:T(8,128)S(1)}, u32[]{:S(2)}, u32[]{:S(2)}) async-start(f32[4,3,8,640]{3,2,1,0:T(8,128)} %get-tuple-element.105), calls=%async_computation.10 | async-start | bytes 491520 | tf_op jit(solution)/shard_map/all_to_all | solution.py:209
  178.1 13.4 %all-to-all-start.11 = ((f32[4,3,8,640]{3,2,1,0:T(8,128)}), f32[4,3,8,640]{3,2,1,0:T(8,128)S(1)}, u32[]{:S(2)}, u32[]{:S(2)}) async-start(f32[4,3,8,640]{3,2,1,0:T(8,128)} %get-tuple-element.109), calls=%async_computation.11 | async-start | bytes 491520 | tf_op jit(solution)/shard_map/all_to_all | solution.py:209
  192.7 13.4 %all-to-all-start.12 = ((f32[4,3,8,640]{3,2,1,0:T(8,128)}), f32[4,3,8,640]{3,2,1,0:T(8,128)S(1)}, u32[]{:S(2)}, u32[]{:S(2)}) async-start(f32[4,3,8,640]{3,2,1,0:T(8,128)} %get-tuple-element.113), calls=%async_computation.12 | async-start | bytes 491520 | tf_op jit(solution)/shard_map/all_to_all | solution.py:209
  207.3 13.4 %all-to-all-start.13 = ((f32[4,3,8,640]{3,2,1,0:T(8,128)}), f32[4,3,8,640]{3,2,1,0:T(8,128)S(1)}, u32[]{:S(2)}, u32[]{:S(2)}) async-start(f32[4,3,8,640]{3,2,1,0:T(8,128)} %get-tuple-element.117), calls=%async_computation.13 | async-start | bytes 491520 | tf_op jit(solution)/shard_map/all_to_all | solution.py:209
  221.9 13.4 %all-to-all-start.14 = ((f32[4,3,8,640]{3,2,1,0:T(8,128)}), f32[4,3,8,640]{3,2,1,0:T(8,128)S(1)}, u32[]{:S(2)}, u32[]{:S(2)}) async-start(f32[4,3,8,640]{3,2,1,0:T(8,128)} %get-tuple-element.121), calls=%async_computation.14 | async-start | bytes 491520 | tf_op jit(solution)/shard_map/all_to_all | solution.py:209
  226.7 8.6 %collective-permute-start.14 = (f32[2,8,640]{2,1,0:T(8,128)S(1)}, f32[2,8,640]{2,1,0:T(8,128)S(1)}, u32[]{:S(2)}, u32[]{:S(2)}) collective-permute-start(f32[2,8,640]{2,1,0:T(8,128)S(1)} %get-tuple-element.120), channel_id=1, source_target_pairs={{0,127},{1,2},{2,1},{3,4},{4,3},{5,6},{6,5},{7,8},{8,7},{9,10},{10... | collective-permute-start | bytes 122888 | tf_op jit(solution)/shard_map/ppermute | solution.py:210
  236.5 13.4 %all-to-all-start.15 = ((f32[4,3,8,640]{3,2,1,0:T(8,128)}), f32[4,3,8,640]{3,2,1,0:T(8,128)S(1)}, u32[]{:S(2)}, u32[]{:S(2)}) async-start(f32[4,3,8,640]{3,2,1,0:T(8,128)} %get-tuple-element.125), calls=%async_computation.15 | async-start | bytes 491520 | tf_op jit(solution)/shard_map/all_to_all | solution.py:209
  (30 other events, 100.6 us)

commit v3 on v2

--- a/solution.py
+++ b/solution.py
@@ -49,8 +49,7 @@
         out[n : n + rows] + out[n + rows : n + 2 * rows] + out[n + 2 * rows : n + 3 * rows]
         for n in (0, 3 * rows)
     )
-    lane = lax.broadcasted_iota(jnp.int32, (rows, lanes), 1)
-    return jnp.where(lane < width, first, second)
+    return jnp.where(lane_of((rows, lanes)) < width, first, second)
 
 
 def chosen(mask_ref, row, yes, no):
@@ -63,12 +62,20 @@
     return chosen(tables_ref, row + 1, blocks_ref[2], middle)
 
 
-def tables_kernel(place_ref, slots_ref, lists_ref, pad_ref, weights_ref, tables_ref):
+def tables_kernel(
+    slots_ref, lists_ref, pad_ref, weights_ref, source_ref, volume_ref, step_ref,
+    tables_ref, source_out, volume_out, step_out, held
+):
     lanes = tables_ref.shape[1]
-    side = place_ref[0]
-    first = INST * place_ref[1]
+    side = lax.rem(lax.axis_index("cell"), 2)
+    first = INST * lax.axis_index("inst")
     rows = slots_ref.shape[0]
-    lane = lax.broadcasted_iota(jnp.int32, (1, lanes), 1)
+    lane = lane_of((1, lanes))
+    for r in range(rows):
+        source_out[r] = side_by_side(held, source_ref[0, r], source_ref[1, r])
+        for value_ref, out_ref in ((volume_ref, volume_out), (step_ref, step_out)):
+            value = jnp.broadcast_to(value_ref[pl.ds(r, 1), :], source_ref.shape[2:])
+            out_ref[pl.ds(r, 1), :] = side_by_side(held, value, value)[:1]
 
     def put(row, left, right):
         tables_ref[pl.ds(row, 1), :] = jnp.where(lane < lanes // 2, left, right)
@@ -90,24 +97,55 @@
         put(CROSS + p, weights_ref[2 * p, first + 1], weights_ref[2 * p + 1, first])
 
 
-def send_copies(block_ref, peers_ref, sems, r):
-    return [
-        pltpu.make_async_copy(block_ref.at[r], peers_ref.at[p, r], sems.at[r, p])
-        for p in range(peers_ref.shape[0])
-    ]
-
-
-def begin_kernel(place_ref, lists_ref, adjoint_ref, near_ref, far_ref, peers_ref, sems):
-    side = place_ref[0]
-    rows = adjoint_ref.shape[0]
-    copies = [c for r in range(rows) for c in send_copies(adjoint_ref, peers_ref, sems, r)]
-    for copy in copies:
-        copy.start()
+def send_copy(held, peers_ref, sems, r):
+    return pltpu.make_async_copy(held.at[:, r], peers_ref.at[:, r], sems.at[r])
+
+
+def lane_of(shape):
+    return lax.broadcasted_iota(jnp.int32, shape, len(shape) - 1)
+
+
+def side_by_side(held, left, right):
+    width = held.shape[1] // 2
+    held[:, :width] = right
+    moved = swapped(held[...])
+    held[:, :width] = left
+    return jnp.where(lane_of(held.shape) < width, held[...], moved)
+
+
+def begin_kernel(
+    lists_ref, adjoint_ref, adjoint_out, near_ref, far_ref, peers_ref, held, copied, sems
+):
+    side = lax.rem(lax.axis_index("cell"), 2)
+    copies = []
+    for r in range(adjoint_out.shape[0]):
+        new = side_by_side(held, adjoint_ref[0, r], adjoint_ref[1, r])
+        adjoint_out[r] = new
+        for p in range(copied.shape[0]):
+            copied[p, r] = new
+        copies.append(send_copy(copied, peers_ref, sems, r))
+        copies[-1].start()
     for e in range(REACH):
-        near_ref[e] = adjoint_ref[lists_ref[REACH - REACH * side + e]]
-        far_ref[e] = adjoint_ref[lists_ref[REACH * side + e]]
+        near_ref[e] = adjoint_out[lists_ref[REACH - REACH * side + e]]
+        far_ref[e] = adjoint_out[lists_ref[REACH * side + e]]
     for copy in copies:
         copy.wait()
+
+
+def pack_kernel(jacobian_ref, own_ref, near_ref, far_ref, held):
+    rows = jacobian_ref.shape[1]
+    side = lax.rem(lax.axis_index("cell"), 2)
+    height = held.shape[0]
+    for k, out_ref in ((0, own_ref), (REACH - side, near_ref), (1 + side, far_ref)):
+        for r in range(rows):
+
+            @pl.loop(0, out_ref.shape[1] // height)
+            def _(n):
+                some = pl.ds(pl.multiple_of(n * height, height), height)
+                left, right = (
+                    jacobian_ref[t, r, k, some, :].astype(jnp.float32) for t in range(INST)
+                )
+                out_ref[r, some, :] = side_by_side(held, left, right).astype(out_ref.dtype)
 
 
 def here_kernel(tables_ref, adjoint_ref, near_ref, own_j_ref, near_j_ref, source_ref, out_ref):
@@ -144,10 +182,10 @@
                 out_ref[1, r] = swapped(value)[:, :width]
             continue
         outs[0][r] = new
-        started = send_copies(outs[0], outs[3], outs[4], r)
-        for copy in started:
-            copy.start()
-        copies += started
+        for p in range(peers_ref.shape[0]):
+            outs[4][p, r] = new
+        copies.append(send_copy(outs[4], outs[3], outs[5], r))
+        copies[-1].start()
     if not last:
         for e in range(REACH):
             outs[1][e] = listed(tables_ref, NEAR_SEND, e, outs[0])
@@ -156,7 +194,7 @@
         copy.wait()
 
 
-def call(kernel, ins, outs, *args, scratch=(), cost=None):
+def call(kernel, ins, outs, *args, scratch=()):
     spaces = {"s": SMEM, "v": VMEM, "a": HBM}
     return pl.pallas_call(
         kernel,
@@ -165,12 +203,7 @@
         out_shape=[jax.ShapeDtypeStruct(*o) for _, o in outs],
         scratch_shapes=list(scratch),
         compiler_params=pltpu.CompilerParams(vmem_limit_bytes=4 << 20),
-        cost_estimate=cost and pl.CostEstimate(flops=cost, bytes_accessed=0, transcendentals=0),
     )(*args)
-
-
-def side_by_side(blocks):
-    return jnp.concatenate([blocks[0], blocks[1]], axis=-1)
 
 
 def on_device(adjoint, source, jacobian, volume, step, slots, lists, pads):
@@ -180,29 +213,25 @@
     cells = lax.axis_size("cell")
     near_groups = [[i, i + 1] for i in range(0, cells, 2)]
     far_pairs = [(i, (i + 1 if i % 2 else i - 1) % cells) for i in range(cells)]
-    side = lax.rem(lax.axis_index("cell"), 2).astype(jnp.int32)
-    place = jnp.stack([side, lax.axis_index("inst").astype(jnp.int32)])
     f32 = jnp.float32
     lanes = 2 * width
     block = ((rows, objectives, lanes), f32)
     halo = ((REACH, objectives, lanes), f32)
     gathered = ((peers,) + block[0], f32)
-    sends = [pltpu.SemaphoreType.DMA((rows, peers))]
-    listed_out = (("v", halo), ("v", halo), ("a", gathered))
-    adjoint = side_by_side(adjoint)
-    near, far, spread = call(
-        begin_kernel, "ssv", listed_out, place, lists, adjoint, scratch=sends
-    )
-    tables = call(
-        tables_kernel, "sssss", (("v", ((TABLE, lanes), f32)),), place, slots, lists, pads,
-        jnp.asarray(time_matrix()),
-    )[0]
-    source = side_by_side(source)
-    volume = jnp.concatenate([volume, volume], axis=-1)
-    step = jnp.concatenate([step, step], axis=-1)
-    own_j, near_j, far_j = (
-        side_by_side(lax.dynamic_index_in_dim(jacobian, k, axis=2, keepdims=False))
-        for k in (0, REACH - side, 1 + side)
+    sends = [pltpu.VMEM(*gathered), pltpu.SemaphoreType.DMA((rows,))]
+    listed_out = (("v", block), ("v", halo), ("v", halo), ("a", gathered))
+    held = pltpu.VMEM(block[0][1:], f32)
+    adjoint, near, far, spread = call(
+        begin_kernel, "sv", listed_out, lists, adjoint, scratch=[held] + sends
+    )
+    cells_out = ("v", ((rows, lanes), f32))
+    tables, source, volume, step = call(
+        tables_kernel, "ssssvvv", (("v", ((TABLE, lanes), f32)), ("v", block)) + (cells_out,) * 2,
+        slots, lists, pads, jnp.asarray(time_matrix()), source, volume, step, scratch=[held],
+    )
+    own_j, near_j, far_j = call(
+        pack_kernel, "v", (("v", ((rows, width, lanes), jacobian.dtype)),) * 3, jacobian,
+        scratch=[pltpu.VMEM((64, lanes), f32)],
     )
     for sweep in range(ITERS):
         last = sweep == ITERS - 1
@@ -214,7 +243,7 @@
         )[0]
         result = call(
             functools.partial(update_kernel, last), "vvvvvvvv",
-            (("v", (shape, f32)),) * 2 if last else (("v", block),) + listed_out,
+            (("v", (shape, f32)),) * 2 if last else listed_out,
             tables, far, far_j, spread, partial, adjoint, volume, step,
             scratch=[] if last else sends,
         )

time: 254 us -> 253 us (level)
  Pallas kernels: 30.8 us -> 33.7 us
    ppermute x16, starting transfers between devices: 64.2 us -> 59.5 us  [on_device(): far = lax.ppermute(far, 'cell', far_pairs)]
    all_to_all x16, starting transfers between devices: 77 us -> 81.4 us  [on_device(): spread = lax.all_to_all(spread, 'inst', 0, 0)]
    squeeze x3 -> x0, local copies, waits for them, and re-layouts: 4.29 us -> none  [side_by_side(): return jnp.concatenate([blocks[0], blocks[1]], axis=-1)]
    unnamed x44 -> x50, local copies, waits for them, and re-layouts: 20 us -> 23.1 us
    pallas_call x34 -> x35, Pallas kernels: 30.8 us -> 33.7 us  [call(): pl.pallas_call(kernel, in_specs=[spaces[c] for c in ins], out_specs=[spac...]
  transfers between devices with their start and end apart: 32 -> 32, of which waited for: 15 -> 15; matrix products, arithmetic and copies ran while one was open for 2% -> 0% of each run, Pallas kernels for 4% -> 6%
where the time goes in v3:
time: 253 us; the launch traced here: 251 us
  starting transfers between devices  141 us (56%)
  Pallas kernels  33.7 us (13%)
  blocking collectives  30 us (12%)
  local copies, waits for them, and re-layouts  23.1 us (9%)
  waiting for transfers between devices  21.2 us (8%)
    all_to_all x16, starting transfers between devices, on_device(): spread = lax.all_to_all(spread, 'inst', 0, 0)  81.4 us
    ppermute x16, starting transfers between devices, on_device(): far = lax.ppermute(far, 'cell', far_pairs)  59.5 us
    pallas_call x35, Pallas kernels, call(): pl.pallas_call(kernel, in_specs=[spaces[c] for c in ins], out_specs=[spac...  33.7 us
    all_gather x16, blocking collectives, on_device(): near = lax.all_gather(near, 'cell', axis_index_groups=near_groups)  30 us
    unnamed x50, local copies, waits for them, and re-layouts  23.1 us
    ppermute x16, waiting for transfers between devices, on_device(): far = lax.ppermute(far, 'cell', far_pairs)  21.1 us
  transfers between devices with their start and end apart: 32, of which 15 were waited for; matrix products, arithmetic and copies ran while one was open for 0% of the time, Pallas kernels for 6%

profile of v3, /device:TPU:2, one launch (start us, length us, event | category | flops | bytes accessed | tf_op | source)
XLA Modules:
  0.0 250.7 jit_solution(12941790458092527462)
XLA Ops:
  3.5 9.3 %all-to-all-start = ((f32[4,3,8,640]{3,2,1,0:T(8,128)}), f32[4,3,8,640]{3,2,1,0:T(8,128)S(1)}, u32[]{:S(2)}, u32[]{:S(2)}) async-start(f32[4,3,8,640]{3,2,1,0:T(8,128)} %get-tuple-element.76), calls=%async_computation | async-start | bytes 491520 | tf_op jit(solution)/shard_map/all_to_all | solution.py:238
  12.8 8.3 %collective-permute-start = (f32[2,8,640]{2,1,0:T(8,128)S(1)}, f32[2,8,640]{2,1,0:T(8,128)S(1)}, u32[]{:S(2)}, u32[]{:S(2)}) collective-permute-start(f32[2,8,640]{2,1,0:T(8,128)S(1)} %get-tuple-element.74), channel_id=1, source_target_pairs={{0,127},{1,2},{2,1},{3,4},{4,3},{5,6},{6,5},{7,8},{8,7},{9,10},{10... | collective-permute-start | bytes 122888 | tf_op jit(solution)/shard_map/ppermute | solution.py:239
  24.0 4.1 %shard_map.106 = (bf16[3,320,640]{2,1,0:T(8,128)(2,1)S(1)}, bf16[3,320,640]{2,1,0:T(8,128)(2,1)S(1)}, bf16[3,320,640]{2,1,0:T(8,128)(2,1)S(1)}) custom-call(bf16[2,3,3,320,320]{4,3,2,1,0:T(8,128)(2,1)S(1)} %copy-done.16), custom_call_target="tpu_custom_call" | custom-call | tf_op jit(solution)/shard_map/pallas_call | solution.py:199
  32.6 4.8 %all-to-all-start.1 = ((f32[4,3,8,640]{3,2,1,0:T(8,128)}), f32[4,3,8,640]{3,2,1,0:T(8,128)S(1)}, u32[]{:S(2)}, u32[]{:S(2)}) async-start(f32[4,3,8,640]{3,2,1,0:T(8,128)} %get-tuple-element.85), calls=%async_computation.1 | async-start | bytes 491520 | tf_op jit(solution)/shard_map/all_to_all | solution.py:238
  47.2 4.8 %all-to-all-start.2 = ((f32[4,3,8,640]{3,2,1,0:T(8,128)}), f32[4,3,8,640]{3,2,1,0:T(8,128)S(1)}, u32[]{:S(2)}, u32[]{:S(2)}) async-start(f32[4,3,8,640]{3,2,1,0:T(8,128)} %get-tuple-element.89), calls=%async_computation.2 | async-start | bytes 491520 | tf_op jit(solution)/shard_map/all_to_all | solution.py:238
  61.7 4.8 %all-to-all-start.3 = ((f32[4,3,8,640]{3,2,1,0:T(8,128)}), f32[4,3,8,640]{3,2,1,0:T(8,128)S(1)}, u32[]{:S(2)}, u32[]{:S(2)}) async-start(f32[4,3,8,640]{3,2,1,0:T(8,128)} %get-tuple-element.93), calls=%async_computation.3 | async-start | bytes 491520 | tf_op jit(solution)/shard_map/all_to_all | solution.py:238
  66.5 3.5 %collective-permute-start.3 = (f32[2,8,640]{2,1,0:T(8,128)S(1)}, f32[2,8,640]{2,1,0:T(8,128)S(1)}, u32[]{:S(2)}, u32[]{:S(2)}) collective-permute-start(f32[2,8,640]{2,1,0:T(8,128)S(1)} %get-tuple-element.92), channel_id=1, source_target_pairs={{0,127},{1,2},{2,1},{3,4},{4,3},{5,6},{6,5},{7,8},{8,7},{9,10},{10... | collective-permute-start | bytes 122888 | tf_op jit(solution)/shard_map/ppermute | solution.py:239
  76.2 4.8 %all-to-all-start.4 = ((f32[4,3,8,640]{3,2,1,0:T(8,128)}), f32[4,3,8,640]{3,2,1,0:T(8,128)S(1)}, u32[]{:S(2)}, u32[]{:S(2)}) async-start(f32[4,3,8,640]{3,2,1,0:T(8,128)} %get-tuple-element.97), calls=%async_computation.4 | async-start | bytes 491520 | tf_op jit(solution)/shard_map/all_to_all | solution.py:238
  81.0 3.5 %collective-permute-start.4 = (f32[2,8,640]{2,1,0:T(8,128)S(1)}, f32[2,8,640]{2,1,0:T(8,128)S(1)}, u32[]{:S(2)}, u32[]{:S(2)}) collective-permute-start(f32[2,8,640]{2,1,0:T(8,128)S(1)} %get-tuple-element.96), channel_id=1, source_target_pairs={{0,127},{1,2},{2,1},{3,4},{4,3},{5,6},{6,5},{7,8},{8,7},{9,10},{10... | collective-permute-start | bytes 122888 | tf_op jit(solution)/shard_map/ppermute | solution.py:239
  90.8 4.8 %all-to-all-start.5 = ((f32[4,3,8,640]{3,2,1,0:T(8,128)}), f32[4,3,8,640]{3,2,1,0:T(8,128)S(1)}, u32[]{:S(2)}, u32[]{:S(2)}) async-start(f32[4,3,8,640]{3,2,1,0:T(8,128)} %get-tuple-element.101), calls=%async_computation.5 | async-start | bytes 491520 | tf_op jit(solution)/shard_map/all_to_all | solution.py:238
  95.6 3.5 %collective-permute-start.5 = (f32[2,8,640]{2,1,0:T(8,128)S(1)}, f32[2,8,640]{2,1,0:T(8,128)S(1)}, u32[]{:S(2)}, u32[]{:S(2)}) collective-permute-start(f32[2,8,640]{2,1,0:T(8,128)S(1)} %get-tuple-element.100), channel_id=1, source_target_pairs={{0,127},{1,2},{2,1},{3,4},{4,3},{5,6},{6,5},{7,8},{8,7},{9,10},{10... | collective-permute-start | bytes 122888 | tf_op jit(solution)/shard_map/ppermute | solution.py:239
  105.3 4.8 %all-to-all-start.6 = ((f32[4,3,8,640]{3,2,1,0:T(8,128)}), f32[4,3,8,640]{3,2,1,0:T(8,128)S(1)}, u32[]{:S(2)}, u32[]{:S(2)}) async-start(f32[4,3,8,640]{3,2,1,0:T(8,128)} %get-tuple-element.105), calls=%async_computation.6 | async-start | bytes 491520 | tf_op jit(solution)/shard_map/all_to_all | solution.py:238
  110.1 3.5 %collective-permute-start.6 = (f32[2,8,640]{2,1,0:T(8,128)S(1)}, f32[2,8,640]{2,1,0:T(8,128)S(1)}, u32[]{:S(2)}, u32[]{:S(2)}) collective-permute-start(f32[2,8,640]{2,1,0:T(8,128)S(1)} %get-tuple-element.104), channel_id=1, source_target_pairs={{0,127},{1,2},{2,1},{3,4},{4,3},{5,6},{6,5},{7,8},{8,7},{9,10},{10... | collective-permute-start | bytes 122888 | tf_op jit(solution)/shard_map/ppermute | solution.py:239
  119.8 4.8 %all-to-all-start.7 = ((f32[4,3,8,640]{3,2,1,0:T(8,128)}), f32[4,3,8,640]{3,2,1,0:T(8,128)S(1)}, u32[]{:S(2)}, u32[]{:S(2)}) async-start(f32[4,3,8,640]{3,2,1,0:T(8,128)} %get-tuple-element.109), calls=%async_computation.7 | async-start | bytes 491520 | tf_op jit(solution)/shard_map/all_to_all | solution.py:238
  134.4 4.8 %all-to-all-start.8 = ((f32[4,3,8,640]{3,2,1,0:T(8,128)}), f32[4,3,8,640]{3,2,1,0:T(8,128)S(1)}, u32[]{:S(2)}, u32[]{:S(2)}) async-start(f32[4,3,8,640]{3,2,1,0:T(8,128)} %get-tuple-element.113), calls=%async_computation.8 | async-start | bytes 491520 | tf_op jit(solution)/shard_map/all_to_all | solution.py:238
  148.9 4.8 %all-to-all-start.9 = ((f32[4,3,8,640]{3,2,1,0:T(8,128)}), f32[4,3,8,640]{3,2,1,0:T(8,128)S(1)}, u32[]{:S(2)}, u32[]{:S(2)}) async-start(f32[4,3,8,640]{3,2,1,0:T(8,128)} %get-tuple-element.117), calls=%async_computation.9 | async-start | bytes 491520 | tf_op jit(solution)/shard_map/all_to_all | solution.py:238
  163.4 4.8 %all-to-all-start.10 = ((f32[4,3,8,640]{3,2,1,0:T(8,128)}), f32[4,3,8,640]{3,2,1,0:T(8,128)S(1)}, u32[]{:S(2)}, u32[]{:S(2)}) async-start(f32[4,3,8,640]{3,2,1,0:T(8,128)} %get-tuple-element.121), calls=%async_computation.10 | async-start | bytes 491520 | tf_op jit(solution)/shard_map/all_to_all | solution.py:238
  178.0 4.8 %all-to-all-start.11 = ((f32[4,3,8,640]{3,2,1,0:T(8,128)}), f32[4,3,8,640]{3,2,1,0:T(8,128)S(1)}, u32[]{:S(2)}, u32[]{:S(2)}) async-start(f32[4,3,8,640]{3,2,1,0:T(8,128)} %get-tuple-element.125), calls=%async_computation.11 | async-start | bytes 491520 | tf_op jit(solution)/shard_map/all_to_all | solution.py:238
  192.5 4.8 %all-to-all-start.12 = ((f32[4,3,8,640]{3,2,1,0:T(8,128)}), f32[4,3,8,640]{3,2,1,0:T(8,128)S(1)}, u32[]{:S(2)}, u32[]{:S(2)}) async-start(f32[4,3,8,640]{3,2,1,0:T(8,128)} %get-tuple-element.129), calls=%async_computation.12 | async-start | bytes 491520 | tf_op jit(solution)/shard_map/all_to_all | solution.py:238
  197.3 3.7 %collective-permute-start.12 = (f32[2,8,640]{2,1,0:T(8,128)S(1)}, f32[2,8,640]{2,1,0:T(8,128)S(1)}, u32[]{:S(2)}, u32[]{:S(2)}) collective-permute-start(f32[2,8,640]{2,1,0:T(8,128)S(1)} %get-tuple-element.128), channel_id=1, source_target_pairs={{0,127},{1,2},{2,1},{3,4},{4,3},{5,6},{6,5},{7,8},{8,7},{9,10},{10... | collective-permute-start | bytes 122888 | tf_op jit(solution)/shard_map/ppermute | solution.py:239
  207.0 4.8 %all-to-all-start.13 = ((f32[4,3,8,640]{3,2,1,0:T(8,128)}), f32[4,3,8,640]{3,2,1,0:T(8,128)S(1)}, u32[]{:S(2)}, u32[]{:S(2)}) async-start(f32[4,3,8,640]{3,2,1,0:T(8,128)} %get-tuple-element.133), calls=%async_computation.13 | async-start | bytes 491520 | tf_op jit(solution)/shard_map/all_to_all | solution.py:238
  221.6 4.8 %all-to-all-start.14 = ((f32[4,3,8,640]{3,2,1,0:T(8,128)}), f32[4,3,8,640]{3,2,1,0:T(8,128)S(1)}, u32[]{:S(2)}, u32[]{:S(2)}) async-start(f32[4,3,8,640]{3,2,1,0:T(8,128)} %get-tuple-element.137), calls=%async_computation.14 | async-start | bytes 491520 | tf_op jit(solution)/shard_map/all_to_all | solution.py:238
  226.4 3.5 %collective-permute-start.14 = (f32[2,8,640]{2,1,0:T(8,128)S(1)}, f32[2,8,640]{2,1,0:T(8,128)S(1)}, u32[]{:S(2)}, u32[]{:S(2)}) collective-permute-start(f32[2,8,640]{2,1,0:T(8,128)S(1)} %get-tuple-element.136), channel_id=1, source_target_pairs={{0,127},{1,2},{2,1},{3,4},{4,3},{5,6},{6,5},{7,8},{8,7},{9,10},{10... | collective-permute-start | bytes 122888 | tf_op jit(solution)/shard_map/ppermute | solution.py:239
  236.1 4.8 %all-to-all-start.15 = ((f32[4,3,8,640]{3,2,1,0:T(8,128)}), f32[4,3,8,640]{3,2,1,0:T(8,128)S(1)}, u32[]{:S(2)}, u32[]{:S(2)}) async-start(f32[4,3,8,640]{3,2,1,0:T(8,128)} %get-tuple-element.141), calls=%async_computation.15 | async-start | bytes 491520 | tf_op jit(solution)/shard_map/all_to_all | solution.py:238
  (141 shorter events, 134.0 us)
Async XLA Ops:
  3.5 28.0 %all-to-all-start = ((f32[4,3,8,640]{3,2,1,0:T(8,128)}), f32[4,3,8,640]{3,2,1,0:T(8,128)S(1)}, u32[]{:S(2)}, u32[]{:S(2)}) async-start(f32[4,3,8,640]{3,2,1,0:T(8,128)} %get-tuple-element.76), calls=%async_computation | async-start | bytes 491520 | tf_op jit(solution)/shard_map/all_to_all | solution.py:238
  12.8 18.7 %collective-permute-start = (f32[2,8,640]{2,1,0:T(8,128)S(1)}, f32[2,8,640]{2,1,0:T(8,128)S(1)}, u32[]{:S(2)}, u32[]{:S(2)}) collective-permute-start(f32[2,8,640]{2,1,0:T(8,128)S(1)} %get-tuple-element.74), channel_id=1, source_target_pairs={{0,127},{1,2},{2,1},{3,4},{4,3},{5,6},{6,5},{7,8},{8,7},{9,10},{10... | collective-permute-start | bytes 122888 | tf_op jit(solution)/shard_map/ppermute | solution.py:239
  32.6 13.4 %all-to-all-start.1 = ((f32[4,3,8,640]{3,2,1,0:T(8,128)}), f32[4,3,8,640]{3,2,1,0:T(8,128)S(1)}, u32[]{:S(2)}, u32[]{:S(2)}) async-start(f32[4,3,8,640]{3,2,1,0:T(8,128)} %get-tuple-element.85), calls=%async_computation.1 | async-start | bytes 491520 | tf_op jit(solution)/shard_map/all_to_all | solution.py:238
  37.4 8.6 %collective-permute-start.1 = (f32[2,8,640]{2,1,0:T(8,128)S(1)}, f32[2,8,640]{2,1,0:T(8,128)S(1)}, u32[]{:S(2)}, u32[]{:S(2)}) collective-permute-start(f32[2,8,640]{2,1,0:T(8,128)S(1)} %get-tuple-element.84), channel_id=1, source_target_pairs={{0,127},{1,2},{2,1},{3,4},{4,3},{5,6},{6,5},{7,8},{8,7},{9,10},{10... | collective-permute-start | bytes 122888 | tf_op jit(solution)/shard_map/ppermute | solution.py:239
  47.2 13.4 %all-to-all-start.2 = ((f32[4,3,8,640]{3,2,1,0:T(8,128)}), f32[4,3,8,640]{3,2,1,0:T(8,128)S(1)}, u32[]{:S(2)}, u32[]{:S(2)}) async-start(f32[4,3,8,640]{3,2,1,0:T(8,128)} %get-tuple-element.89), calls=%async_computation.2 | async-start | bytes 491520 | tf_op jit(solution)/shard_map/all_to_all | solution.py:238
  52.0 8.6 %collective-permute-start.2 = (f32[2,8,640]{2,1,0:T(8,128)S(1)}, f32[2,8,640]{2,1,0:T(8,128)S(1)}, u32[]{:S(2)}, u32[]{:S(2)}) collective-permute-start(f32[2,8,640]{2,1,0:T(8,128)S(1)} %get-tuple-element.88), channel_id=1, source_target_pairs={{0,127},{1,2},{2,1},{3,4},{4,3},{5,6},{6,5},{7,8},{8,7},{9,10},{10... | collective-permute-start | bytes 122888 | tf_op jit(solution)/shard_map/ppermute | solution.py:239
  61.7 13.4 %all-to-all-start.3 = ((f32[4,3,8,640]{3,2,1,0:T(8,128)}), f32[4,3,8,640]{3,2,1,0:T(8,128)S(1)}, u32[]{:S(2)}, u32[]{:S(2)}) async-start(f32[4,3,8,640]{3,2,1,0:T(8,128)} %get-tuple-element.93), calls=%async_computation.3 | async-start | bytes 491520 | tf_op jit(solution)/shard_map/all_to_all | solution.py:238
  76.2 13.4 %all-to-all-start.4 = ((f32[4,3,8,640]{3,2,1,0:T(8,128)}), f32[4,3,8,640]{3,2,1,0:T(8,128)S(1)}, u32[]{:S(2)}, u32[]{:S(2)}) async-start(f32[4,3,8,640]{3,2,1,0:T(8,128)} %get-tuple-element.97), calls=%async_computation.4 | async-start | bytes 491520 | tf_op jit(solution)/shard_map/all_to_all | solution.py:238
  81.0 8.6 %collective-permute-start.4 = (f32[2,8,640]{2,1,0:T(8,128)S(1)}, f32[2,8,640]{2,1,0:T(8,128)S(1)}, u32[]{:S(2)}, u32[]{:S(2)}) collective-permute-start(f32[2,8,640]{2,1,0:T(8,128)S(1)} %get-tuple-element.96), channel_id=1, source_target_pairs={{0,127},{1,2},{2,1},{3,4},{4,3},{5,6},{6,5},{7,8},{8,7},{9,10},{10... | collective-permute-start | bytes 122888 | tf_op jit(solution)/shard_map/ppermute | solution.py:239
  90.8 13.4 %all-to-all-start.5 = ((f32[4,3,8,640]{3,2,1,0:T(8,128)}), f32[4,3,8,640]{3,2,1,0:T(8,128)S(1)}, u32[]{:S(2)}, u32[]{:S(2)}) async-start(f32[4,3,8,640]{3,2,1,0:T(8,128)} %get-tuple-element.101), calls=%async_computation.5 | async-start | bytes 491520 | tf_op jit(solution)/shard_map/all_to_all | solution.py:238
  105.3 13.4 %all-to-all-start.6 = ((f32[4,3,8,640]{3,2,1,0:T(8,128)}), f32[4,3,8,640]{3,2,1,0:T(8,128)S(1)}, u32[]{:S(2)}, u32[]{:S(2)}) async-start(f32[4,3,8,640]{3,2,1,0:T(8,128)} %get-tuple-element.105), calls=%async_computation.6 | async-start | bytes 491520 | tf_op jit(solution)/shard_map/all_to_all | solution.py:238
  119.8 13.4 %all-to-all-start.7 = ((f32[4,3,8,640]{3,2,1,0:T(8,128)}), f32[4,3,8,640]{3,2,1,0:T(8,128)S(1)}, u32[]{:S(2)}, u32[]{:S(2)}) async-start(f32[4,3,8,640]{3,2,1,0:T(8,128)} %get-tuple-element.109), calls=%async_computation.7 | async-start | bytes 491520 | tf_op jit(solution)/shard_map/all_to_all | solution.py:238
  124.6 8.6 %collective-permute-start.7 = (f32[2,8,640]{2,1,0:T(8,128)S(1)}, f32[2,8,640]{2,1,0:T(8,128)S(1)}, u32[]{:S(2)}, u32[]{:S(2)}) collective-permute-start(f32[2,8,640]{2,1,0:T(8,128)S(1)} %get-tuple-element.108), channel_id=1, source_target_pairs={{0,127},{1,2},{2,1},{3,4},{4,3},{5,6},{6,5},{7,8},{8,7},{9,10},{10... | collective-permute-start | bytes 122888 | tf_op jit(solution)/shard_map/ppermute | solution.py:239
  134.4 13.4 %all-to-all-start.8 = ((f32[4,3,8,640]{3,2,1,0:T(8,128)}), f32[4,3,8,640]{3,2,1,0:T(8,128)S(1)}, u32[]{:S(2)}, u32[]{:S(2)}) async-start(f32[4,3,8,640]{3,2,1,0:T(8,128)} %get-tuple-element.113), calls=%async_computation.8 | async-start | bytes 491520 | tf_op jit(solution)/shard_map/all_to_all | solution.py:238
  148.9 13.4 %all-to-all-start.9 = ((f32[4,3,8,640]{3,2,1,0:T(8,128)}), f32[4,3,8,640]{3,2,1,0:T(8,128)S(1)}, u32[]{:S(2)}, u32[]{:S(2)}) async-start(f32[4,3,8,640]{3,2,1,0:T(8,128)} %get-tuple-element.117), calls=%async_computation.9 | async-start | bytes 491520 | tf_op jit(solution)/shard_map/all_to_all | solution.py:238
  153.7 8.6 %collective-permute-start.9 = (f32[2,8,640]{2,1,0:T(8,128)S(1)}, f32[2,8,640]{2,1,0:T(8,128)S(1)}, u32[]{:S(2)}, u32[]{:S(2)}) collective-permute-start(f32[2,8,640]{2,1,0:T(8,128)S(1)} %get-tuple-element.116), channel_id=1, source_target_pairs={{0,127},{1,2},{2,1},{3,4},{4,3},{5,6},{6,5},{7,8},{8,7},{9,10},{10... | collective-permute-start | bytes 122888 | tf_op jit(solution)/shard_map/ppermute | solution.py:239
  163.4 13.4 %all-to-all-start.10 = ((f32[4,3,8,640]{3,2,1,0:T(8,128)}), f32[4,3,8,640]{3,2,1,0:T(8,128)S(1)}, u32[]{:S(2)}, u32[]{:S(2)}) async-start(f32[4,3,8,640]{3,2,1,0:T(8,128)} %get-tuple-element.121), calls=%async_computation.10 | async-start | bytes 491520 | tf_op jit(solution)/shard_map/all_to_all | solution.py:238
  168.2 8.6 %collective-permute-start.10 = (f32[2,8,640]{2,1,0:T(8,128)S(1)}, f32[2,8,640]{2,1,0:T(8,128)S(1)}, u32[]{:S(2)}, u32[]{:S(2)}) collective-permute-start(f32[2,8,640]{2,1,0:T(8,128)S(1)} %get-tuple-element.120), channel_id=1, source_target_pairs={{0,127},{1,2},{2,1},{3,4},{4,3},{5,6},{6,5},{7,8},{8,7},{9,10},{10... | collective-permute-start | bytes 122888 | tf_op jit(solution)/shard_map/ppermute | solution.py:239
  178.0 13.4 %all-to-all-start.11 = ((f32[4,3,8,640]{3,2,1,0:T(8,128)}), f32[4,3,8,640]{3,2,1,0:T(8,128)S(1)}, u32[]{:S(2)}, u32[]{:S(2)}) async-start(f32[4,3,8,640]{3,2,1,0:T(8,128)} %get-tuple-element.125), calls=%async_computation.11 | async-start | bytes 491520 | tf_op jit(solution)/shard_map/all_to_all | solution.py:238
  192.5 13.4 %all-to-all-start.12 = ((f32[4,3,8,640]{3,2,1,0:T(8,128)}), f32[4,3,8,640]{3,2,1,0:T(8,128)S(1)}, u32[]{:S(2)}, u32[]{:S(2)}) async-start(f32[4,3,8,640]{3,2,1,0:T(8,128)} %get-tuple-element.129), calls=%async_computation.12 | async-start | bytes 491520 | tf_op jit(solution)/shard_map/all_to_all | solution.py:238
  207.0 13.4 %all-to-all-start.13 = ((f32[4,3,8,640]{3,2,1,0:T(8,128)}), f32[4,3,8,640]{3,2,1,0:T(8,128)S(1)}, u32[]{:S(2)}, u32[]{:S(2)}) async-start(f32[4,3,8,640]{3,2,1,0:T(8,128)} %get-tuple-element.133), calls=%async_computation.13 | async-start | bytes 491520 | tf_op jit(solution)/shard_map/all_to_all | solution.py:238
  221.6 13.4 %all-to-all-start.14 = ((f32[4,3,8,640]{3,2,1,0:T(8,128)}), f32[4,3,8,640]{3,2,1,0:T(8,128)S(1)}, u32[]{:S(2)}, u32[]{:S(2)}) async-start(f32[4,3,8,640]{3,2,1,0:T(8,128)} %get-tuple-element.137), calls=%async_computation.14 | async-start | bytes 491520 | tf_op jit(solution)/shard_map/all_to_all | solution.py:238
  236.1 13.4 %all-to-all-start.15 = ((f32[4,3,8,640]{3,2,1,0:T(8,128)}), f32[4,3,8,640]{3,2,1,0:T(8,128)S(1)}, u32[]{:S(2)}, u32[]{:S(2)}) async-start(f32[4,3,8,640]{3,2,1,0:T(8,128)} %get-tuple-element.141), calls=%async_computation.15 | async-start | bytes 491520 | tf_op jit(solution)/shard_map/all_to_all | solution.py:238
  240.9 8.6 %collective-permute-start.15 = (f32[2,8,640]{2,1,0:T(8,128)S(1)}, f32[2,8,640]{2,1,0:T(8,128)S(1)}, u32[]{:S(2)}, u32[]{:S(2)}) collective-permute-start(f32[2,8,640]{2,1,0:T(8,128)S(1)} %get-tuple-element.140), channel_id=1, source_target_pairs={{0,127},{1,2},{2,1},{3,4},{4,3},{5,6},{6,5},{7,8},{8,7},{9,10},{10... | collective-permute-start | bytes 122888 | tf_op jit(solution)/shard_map/ppermute | solution.py:239
  (33 other events, 120.4 us)

commit v4 on v3

--- a/solution.py
+++ b/solution.py
@@ -14,6 +14,7 @@
 SCALE = 0.15
 REACH = 2
 INST = 2
+TILE = 128
 NEAR_PICK, FAR_PICK, LIVE, NEAR_SEND, FAR_SEND, SAME, CROSS, TABLE = 0, 3, 6, 9, 13, 17, 21, 32
 VMEM = pl.BlockSpec(memory_space=pltpu.VMEM)
 HBM = pl.BlockSpec(memory_space=pltpu.HBM)
@@ -30,15 +31,51 @@
     return out.astype(np.float32)
 
 
+def cut_of(width):
+    return width - width % TILE
+
+
+def lane_of(shape):
+    return lax.broadcasted_iota(jnp.int32, shape, len(shape) - 1)
+
+
+def in_left(shape):
+    width = shape[-1] // 2
+    cut, lane = cut_of(width), lane_of(shape)
+    return (lane < cut) | ((lane >= 2 * cut) & (lane < cut + width))
+
+
+def left_of(block):
+    width = block.shape[1] // 2
+    cut = cut_of(width)
+    return jnp.concatenate([block[:, :cut], block[:, 2 * cut : cut + width]], axis=1)
+
+
 def swapped(block):
-    return pltpu.roll(block, block.shape[1] // 2, 1)
+    width = block.shape[1] // 2
+    cut = cut_of(width)
+    tail = pltpu.roll(block[:, 2 * cut :], width - cut, 1)
+    return jnp.concatenate([block[:, cut : 2 * cut], block[:, :cut], tail], axis=1)
+
+
+def tail_beside(held, left, right):
+    size = left.shape[1]
+    held[:, :size] = right
+    moved = pltpu.roll(held[...], size, 1)
+    held[:, :size] = left
+    return jnp.where(lane_of(held.shape) < size, held[...], moved)
+
+
+def side_by_side(held, left, right):
+    cut = cut_of(left.shape[1])
+    tail = tail_beside(held, left[:, cut:], right[:, cut:])
+    return jnp.concatenate([left[:, :cut], right[:, :cut], tail], axis=1)
 
 
 def product(block, matrix):
     rows, lanes = block.shape
-    width = lanes // 2
     parts = []
-    for half in (block[:, :width], swapped(block)[:, :width]):
+    for half in (left_of(block), left_of(swapped(block))):
         for _ in range(3):
             part = half.astype(jnp.bfloat16).astype(jnp.float32)
             parts.append(part)
@@ -49,7 +86,7 @@
         out[n : n + rows] + out[n + rows : n + 2 * rows] + out[n + 2 * rows : n + 3 * rows]
         for n in (0, 3 * rows)
     )
-    return jnp.where(lane_of((rows, lanes)) < width, first, second)
+    return jnp.where(in_left((rows, lanes)), first, second)
 
 
 def chosen(mask_ref, row, yes, no):
@@ -70,7 +107,7 @@
     side = lax.rem(lax.axis_index("cell"), 2)
     first = INST * lax.axis_index("inst")
     rows = slots_ref.shape[0]
-    lane = lane_of((1, lanes))
+    is_left = in_left((1, lanes))
     for r in range(rows):
         source_out[r] = side_by_side(held, source_ref[0, r], source_ref[1, r])
         for value_ref, out_ref in ((volume_ref, volume_out), (step_ref, step_out)):
@@ -78,7 +115,7 @@
             out_ref[pl.ds(r, 1), :] = side_by_side(held, value, value)[:1]
 
     def put(row, left, right):
-        tables_ref[pl.ds(row, 1), :] = jnp.where(lane < lanes // 2, left, right)
+        tables_ref[pl.ds(row, 1), :] = jnp.where(is_left, left, right)
 
     def flag(row, holds):
         value = jnp.where(holds, 1.0, 0.0).astype(jnp.float32)
@@ -101,22 +138,7 @@
     return pltpu.make_async_copy(held.at[:, r], peers_ref.at[:, r], sems.at[r])
 
 
-def lane_of(shape):
-    return lax.broadcasted_iota(jnp.int32, shape, len(shape) - 1)
-
-
-def side_by_side(held, left, right):
-    width = held.shape[1] // 2
-    held[:, :width] = right
-    moved = swapped(held[...])
-    held[:, :width] = left
-    return jnp.where(lane_of(held.shape) < width, held[...], moved)
-
-
-def begin_kernel(
-    lists_ref, adjoint_ref, adjoint_out, near_ref, far_ref, peers_ref, held, copied, sems
-):
-    side = lax.rem(lax.axis_index("cell"), 2)
+def begin_kernel(adjoint_ref, adjoint_out, peers_ref, held, copied, sems):
     copies = []
     for r in range(adjoint_out.shape[0]):
         new = side_by_side(held, adjoint_ref[0, r], adjoint_ref[1, r])
@@ -125,27 +147,29 @@
             copied[p, r] = new
         copies.append(send_copy(copied, peers_ref, sems, r))
         copies[-1].start()
-    for e in range(REACH):
-        near_ref[e] = adjoint_out[lists_ref[REACH - REACH * side + e]]
-        far_ref[e] = adjoint_out[lists_ref[REACH * side + e]]
     for copy in copies:
         copy.wait()
 
 
+def lists_kernel(lists_ref, adjoint_ref, near_ref, far_ref):
+    side = lax.rem(lax.axis_index("cell"), 2)
+    for e in range(REACH):
+        near_ref[e] = adjoint_ref[lists_ref[REACH - REACH * side + e]]
+        far_ref[e] = adjoint_ref[lists_ref[REACH * side + e]]
+
+
 def pack_kernel(jacobian_ref, own_ref, near_ref, far_ref, held):
-    rows = jacobian_ref.shape[1]
+    rows, width = jacobian_ref.shape[1], jacobian_ref.shape[-1]
     side = lax.rem(lax.axis_index("cell"), 2)
-    height = held.shape[0]
+    cut = cut_of(width)
     for k, out_ref in ((0, own_ref), (REACH - side, near_ref), (1 + side, far_ref)):
         for r in range(rows):
-
-            @pl.loop(0, out_ref.shape[1] // height)
-            def _(n):
-                some = pl.ds(pl.multiple_of(n * height, height), height)
-                left, right = (
-                    jacobian_ref[t, r, k, some, :].astype(jnp.float32) for t in range(INST)
-                )
-                out_ref[r, some, :] = side_by_side(held, left, right).astype(out_ref.dtype)
+            for t in range(INST):
+                out_ref[r, :, t * cut : (t + 1) * cut] = jacobian_ref[t, r, k, :, :cut]
+            left, right = (
+                jacobian_ref[t, r, k, :, cut:].astype(jnp.float32) for t in range(INST)
+            )
+            out_ref[r, :, 2 * cut :] = tail_beside(held, left, right).astype(out_ref.dtype)
 
 
 def here_kernel(tables_ref, adjoint_ref, near_ref, own_j_ref, near_j_ref, source_ref, out_ref):
@@ -160,8 +184,7 @@
     last, tables_ref, far_ref, far_j_ref, peers_ref, partial_ref, adjoint_ref, volume_ref,
     step_ref, *outs
 ):
-    rows, _, lanes = adjoint_ref.shape
-    width = lanes // 2
+    rows = adjoint_ref.shape[0]
     copies = []
     for r in range(rows):
         block = chosen(tables_ref, FAR_PICK + r, far_ref[1], far_ref[0])
@@ -178,8 +201,8 @@
         new = adjoint_ref[r] + step_ref[pl.ds(r, 1), :] * residual
         if last:
             for value, out_ref in zip((new, residual), outs):
-                out_ref[0, r] = value[:, :width]
-                out_ref[1, r] = swapped(value)[:, :width]
+                out_ref[0, r] = left_of(value)
+                out_ref[1, r] = left_of(swapped(value))
             continue
         outs[0][r] = new
         for p in range(peers_ref.shape[0]):
@@ -220,10 +243,11 @@
     gathered = ((peers,) + block[0], f32)
     sends = [pltpu.VMEM(*gathered), pltpu.SemaphoreType.DMA((rows,))]
     listed_out = (("v", block), ("v", halo), ("v", halo), ("a", gathered))
-    held = pltpu.VMEM(block[0][1:], f32)
-    adjoint, near, far, spread = call(
-        begin_kernel, "sv", listed_out, lists, adjoint, scratch=[held] + sends
-    )
+    held = pltpu.VMEM((objectives, TILE), f32)
+    adjoint, spread = call(
+        begin_kernel, "v", (("v", block), ("a", gathered)), adjoint, scratch=[held] + sends
+    )
+    near, far = call(lists_kernel, "sv", (("v", halo),) * 2, lists, adjoint)
     cells_out = ("v", ((rows, lanes), f32))
     tables, source, volume, step = call(
         tables_kernel, "ssssvvv", (("v", ((TABLE, lanes), f32)), ("v", block)) + (cells_out,) * 2,
@@ -231,7 +255,7 @@
     )
     own_j, near_j, far_j = call(
         pack_kernel, "v", (("v", ((rows, width, lanes), jacobian.dtype)),) * 3, jacobian,
-        scratch=[pltpu.VMEM((64, lanes), f32)],
+        scratch=[pltpu.VMEM((width, TILE), f32)],
     )
     for sweep in range(ITERS):
         last = sweep == ITERS - 1

time: 253 us -> 250 us (0.988)
  Pallas kernels: 33.7 us -> 29.9 us
    pallas_call x35 -> x36, Pallas kernels: 33.7 us -> 29.9 us  [call(): pl.pallas_call(kernel, in_specs=[spaces[c] for c in ins], out_specs=[spac...]
  transfers between devices with their start and end apart: 32 -> 32, of which waited for: 15 -> 15; matrix products, arithmetic and copies ran while one was open for 0% -> 0% of each run, Pallas kernels for 6% -> 5%
where the time goes in v4:
time: 250 us; the launch traced here: 247 us
  starting transfers between devices  141 us (56%)
  Pallas kernels  29.9 us (12%)
  blocking collectives  29.8 us (12%)
  local copies, waits for them, and re-layouts  23.3 us (9%)
  waiting for transfers between devices  21.6 us (9%)
    all_to_all x16, starting transfers between devices, on_device(): spread = lax.all_to_all(spread, 'inst', 0, 0)  81.4 us
    ppermute x16, starting transfers between devices, on_device(): far = lax.ppermute(far, 'cell', far_pairs)  59.2 us
    pallas_call x36, Pallas kernels, call(): pl.pallas_call(kernel, in_specs=[spaces[c] for c in ins], out_specs=[spac...  29.9 us
    all_gather x16, blocking collectives, on_device(): near = lax.all_gather(near, 'cell', axis_index_groups=near_groups)  29.8 us
    unnamed x50, local copies, waits for them, and re-layouts  23.3 us
    ppermute x16, waiting for transfers between devices, on_device(): far = lax.ppermute(far, 'cell', far_pairs)  21.6 us
  transfers between devices with their start and end apart: 32, of which 15 were waited for; matrix products, arithmetic and copies ran while one was open for 0% of the time, Pallas kernels for 5%

profile of v4, /device:TPU:2, one launch (start us, length us, event | category | flops | bytes accessed | tf_op | source)
XLA Modules:
  0.0 247.1 jit_solution(3375415946804047836)
XLA Ops:
  2.3 9.3 %all-to-all-start = ((f32[4,3,8,640]{3,2,1,0:T(8,128)}), f32[4,3,8,640]{3,2,1,0:T(8,128)S(1)}, u32[]{:S(2)}, u32[]{:S(2)}) async-start(f32[4,3,8,640]{3,2,1,0:T(8,128)} %get-tuple-element.77), calls=%async_computation | async-start | bytes 491520 | tf_op jit(solution)/shard_map/all_to_all | solution.py:262
  12.8 8.3 %collective-permute-start = (f32[2,8,640]{2,1,0:T(8,128)S(1)}, f32[2,8,640]{2,1,0:T(8,128)S(1)}, u32[]{:S(2)}, u32[]{:S(2)}) collective-permute-start(f32[2,8,640]{2,1,0:T(8,128)S(1)} %get-tuple-element.75), channel_id=1, source_target_pairs={{0,127},{1,2},{2,1},{3,4},{4,3},{5,6},{6,5},{7,8},{8,7},{9,10},{10... | collective-permute-start | bytes 122888 | tf_op jit(solution)/shard_map/ppermute | solution.py:263
  29.3 4.8 %all-to-all-start.1 = ((f32[4,3,8,640]{3,2,1,0:T(8,128)}), f32[4,3,8,640]{3,2,1,0:T(8,128)S(1)}, u32[]{:S(2)}, u32[]{:S(2)}) async-start(f32[4,3,8,640]{3,2,1,0:T(8,128)} %get-tuple-element.85), calls=%async_computation.1 | async-start | bytes 491520 | tf_op jit(solution)/shard_map/all_to_all | solution.py:262
  43.9 4.8 %all-to-all-start.2 = ((f32[4,3,8,640]{3,2,1,0:T(8,128)}), f32[4,3,8,640]{3,2,1,0:T(8,128)S(1)}, u32[]{:S(2)}, u32[]{:S(2)}) async-start(f32[4,3,8,640]{3,2,1,0:T(8,128)} %get-tuple-element.89), calls=%async_computation.2 | async-start | bytes 491520 | tf_op jit(solution)/shard_map/all_to_all | solution.py:262
  58.4 4.8 %all-to-all-start.3 = ((f32[4,3,8,640]{3,2,1,0:T(8,128)}), f32[4,3,8,640]{3,2,1,0:T(8,128)S(1)}, u32[]{:S(2)}, u32[]{:S(2)}) async-start(f32[4,3,8,640]{3,2,1,0:T(8,128)} %get-tuple-element.93), calls=%async_computation.3 | async-start | bytes 491520 | tf_op jit(solution)/shard_map/all_to_all | solution.py:262
  63.2 3.5 %collective-permute-start.3 = (f32[2,8,640]{2,1,0:T(8,128)S(1)}, f32[2,8,640]{2,1,0:T(8,128)S(1)}, u32[]{:S(2)}, u32[]{:S(2)}) collective-permute-start(f32[2,8,640]{2,1,0:T(8,128)S(1)} %get-tuple-element.92), channel_id=1, source_target_pairs={{0,127},{1,2},{2,1},{3,4},{4,3},{5,6},{6,5},{7,8},{8,7},{9,10},{10... | collective-permute-start | bytes 122888 | tf_op jit(solution)/shard_map/ppermute | solution.py:263
  72.9 4.8 %all-to-all-start.4 = ((f32[4,3,8,640]{3,2,1,0:T(8,128)}), f32[4,3,8,640]{3,2,1,0:T(8,128)S(1)}, u32[]{:S(2)}, u32[]{:S(2)}) async-start(f32[4,3,8,640]{3,2,1,0:T(8,128)} %get-tuple-element.97), calls=%async_computation.4 | async-start | bytes 491520 | tf_op jit(solution)/shard_map/all_to_all | solution.py:262
  87.4 4.8 %all-to-all-start.5 = ((f32[4,3,8,640]{3,2,1,0:T(8,128)}), f32[4,3,8,640]{3,2,1,0:T(8,128)S(1)}, u32[]{:S(2)}, u32[]{:S(2)}) async-start(f32[4,3,8,640]{3,2,1,0:T(8,128)} %get-tuple-element.101), calls=%async_computation.5 | async-start | bytes 491520 | tf_op jit(solution)/shard_map/all_to_all | solution.py:262
  92.2 3.5 %collective-permute-start.5 = (f32[2,8,640]{2,1,0:T(8,128)S(1)}, f32[2,8,640]{2,1,0:T(8,128)S(1)}, u32[]{:S(2)}, u32[]{:S(2)}) collective-permute-start(f32[2,8,640]{2,1,0:T(8,128)S(1)} %get-tuple-element.100), channel_id=1, source_target_pairs={{0,127},{1,2},{2,1},{3,4},{4,3},{5,6},{6,5},{7,8},{8,7},{9,10},{10... | collective-permute-start | bytes 122888 | tf_op jit(solution)/shard_map/ppermute | solution.py:263
  101.9 4.8 %all-to-all-start.6 = ((f32[4,3,8,640]{3,2,1,0:T(8,128)}), f32[4,3,8,640]{3,2,1,0:T(8,128)S(1)}, u32[]{:S(2)}, u32[]{:S(2)}) async-start(f32[4,3,8,640]{3,2,1,0:T(8,128)} %get-tuple-element.105), calls=%async_computation.6 | async-start | bytes 491520 | tf_op jit(solution)/shard_map/all_to_all | solution.py:262
  116.4 4.8 %all-to-all-start.7 = ((f32[4,3,8,640]{3,2,1,0:T(8,128)}), f32[4,3,8,640]{3,2,1,0:T(8,128)S(1)}, u32[]{:S(2)}, u32[]{:S(2)}) async-start(f32[4,3,8,640]{3,2,1,0:T(8,128)} %get-tuple-element.109), calls=%async_computation.7 | async-start | bytes 491520 | tf_op jit(solution)/shard_map/all_to_all | solution.py:262
  121.2 3.5 %collective-permute-start.7 = (f32[2,8,640]{2,1,0:T(8,128)S(1)}, f32[2,8,640]{2,1,0:T(8,128)S(1)}, u32[]{:S(2)}, u32[]{:S(2)}) collective-permute-start(f32[2,8,640]{2,1,0:T(8,128)S(1)} %get-tuple-element.108), channel_id=1, source_target_pairs={{0,127},{1,2},{2,1},{3,4},{4,3},{5,6},{6,5},{7,8},{8,7},{9,10},{10... | collective-permute-start | bytes 122888 | tf_op jit(solution)/shard_map/ppermute | solution.py:263
  130.9 4.8 %all-to-all-start.8 = ((f32[4,3,8,640]{3,2,1,0:T(8,128)}), f32[4,3,8,640]{3,2,1,0:T(8,128)S(1)}, u32[]{:S(2)}, u32[]{:S(2)}) async-start(f32[4,3,8,640]{3,2,1,0:T(8,128)} %get-tuple-element.113), calls=%async_computation.8 | async-start | bytes 491520 | tf_op jit(solution)/shard_map/all_to_all | solution.py:262
  145.5 4.8 %all-to-all-start.9 = ((f32[4,3,8,640]{3,2,1,0:T(8,128)}), f32[4,3,8,640]{3,2,1,0:T(8,128)S(1)}, u32[]{:S(2)}, u32[]{:S(2)}) async-start(f32[4,3,8,640]{3,2,1,0:T(8,128)} %get-tuple-element.117), calls=%async_computation.9 | async-start | bytes 491520 | tf_op jit(solution)/shard_map/all_to_all | solution.py:262
  150.3 3.5 %collective-permute-start.9 = (f32[2,8,640]{2,1,0:T(8,128)S(1)}, f32[2,8,640]{2,1,0:T(8,128)S(1)}, u32[]{:S(2)}, u32[]{:S(2)}) collective-permute-start(f32[2,8,640]{2,1,0:T(8,128)S(1)} %get-tuple-element.116), channel_id=1, source_target_pairs={{0,127},{1,2},{2,1},{3,4},{4,3},{5,6},{6,5},{7,8},{8,7},{9,10},{10... | collective-permute-start | bytes 122888 | tf_op jit(solution)/shard_map/ppermute | solution.py:263
  160.0 4.8 %all-to-all-start.10 = ((f32[4,3,8,640]{3,2,1,0:T(8,128)}), f32[4,3,8,640]{3,2,1,0:T(8,128)S(1)}, u32[]{:S(2)}, u32[]{:S(2)}) async-start(f32[4,3,8,640]{3,2,1,0:T(8,128)} %get-tuple-element.121), calls=%async_computation.10 | async-start | bytes 491520 | tf_op jit(solution)/shard_map/all_to_all | solution.py:262
  174.5 4.8 %all-to-all-start.11 = ((f32[4,3,8,640]{3,2,1,0:T(8,128)}), f32[4,3,8,640]{3,2,1,0:T(8,128)S(1)}, u32[]{:S(2)}, u32[]{:S(2)}) async-start(f32[4,3,8,640]{3,2,1,0:T(8,128)} %get-tuple-element.125), calls=%async_computation.11 | async-start | bytes 491520 | tf_op jit(solution)/shard_map/all_to_all | solution.py:262
  179.3 3.5 %collective-permute-start.11 = (f32[2,8,640]{2,1,0:T(8,128)S(1)}, f32[2,8,640]{2,1,0:T(8,128)S(1)}, u32[]{:S(2)}, u32[]{:S(2)}) collective-permute-start(f32[2,8,640]{2,1,0:T(8,128)S(1)} %get-tuple-element.124), channel_id=1, source_target_pairs={{0,127},{1,2},{2,1},{3,4},{4,3},{5,6},{6,5},{7,8},{8,7},{9,10},{10... | collective-permute-start | bytes 122888 | tf_op jit(solution)/shard_map/ppermute | solution.py:263
  189.0 4.8 %all-to-all-start.12 = ((f32[4,3,8,640]{3,2,1,0:T(8,128)}), f32[4,3,8,640]{3,2,1,0:T(8,128)S(1)}, u32[]{:S(2)}, u32[]{:S(2)}) async-start(f32[4,3,8,640]{3,2,1,0:T(8,128)} %get-tuple-element.129), calls=%async_computation.12 | async-start | bytes 491520 | tf_op jit(solution)/shard_map/all_to_all | solution.py:262
  203.5 4.8 %all-to-all-start.13 = ((f32[4,3,8,640]{3,2,1,0:T(8,128)}), f32[4,3,8,640]{3,2,1,0:T(8,128)S(1)}, u32[]{:S(2)}, u32[]{:S(2)}) async-start(f32[4,3,8,640]{3,2,1,0:T(8,128)} %get-tuple-element.133), calls=%async_computation.13 | async-start | bytes 491520 | tf_op jit(solution)/shard_map/all_to_all | solution.py:262
  208.3 3.5 %collective-permute-start.13 = (f32[2,8,640]{2,1,0:T(8,128)S(1)}, f32[2,8,640]{2,1,0:T(8,128)S(1)}, u32[]{:S(2)}, u32[]{:S(2)}) collective-permute-start(f32[2,8,640]{2,1,0:T(8,128)S(1)} %get-tuple-element.132), channel_id=1, source_target_pairs={{0,127},{1,2},{2,1},{3,4},{4,3},{5,6},{6,5},{7,8},{8,7},{9,10},{10... | collective-permute-start | bytes 122888 | tf_op jit(solution)/shard_map/ppermute | solution.py:263
  218.0 4.8 %all-to-all-start.14 = ((f32[4,3,8,640]{3,2,1,0:T(8,128)}), f32[4,3,8,640]{3,2,1,0:T(8,128)S(1)}, u32[]{:S(2)}, u32[]{:S(2)}) async-start(f32[4,3,8,640]{3,2,1,0:T(8,128)} %get-tuple-element.137), calls=%async_computation.14 | async-start | bytes 491520 | tf_op jit(solution)/shard_map/all_to_all | solution.py:262
  232.5 4.8 %all-to-all-start.15 = ((f32[4,3,8,640]{3,2,1,0:T(8,128)}), f32[4,3,8,640]{3,2,1,0:T(8,128)S(1)}, u32[]{:S(2)}, u32[]{:S(2)}) async-start(f32[4,3,8,640]{3,2,1,0:T(8,128)} %get-tuple-element.141), calls=%async_computation.15 | async-start | bytes 491520 | tf_op jit(solution)/shard_map/all_to_all | solution.py:262
  237.4 3.5 %collective-permute-start.15 = (f32[2,8,640]{2,1,0:T(8,128)S(1)}, f32[2,8,640]{2,1,0:T(8,128)S(1)}, u32[]{:S(2)}, u32[]{:S(2)}) collective-permute-start(f32[2,8,640]{2,1,0:T(8,128)S(1)} %get-tuple-element.140), channel_id=1, source_target_pairs={{0,127},{1,2},{2,1},{3,4},{4,3},{5,6},{6,5},{7,8},{8,7},{9,10},{10... | collective-permute-start | bytes 122888 | tf_op jit(solution)/shard_map/ppermute | solution.py:263
  (142 shorter events, 131.3 us)
Async XLA Ops:
  2.3 25.9 %all-to-all-start = ((f32[4,3,8,640]{3,2,1,0:T(8,128)}), f32[4,3,8,640]{3,2,1,0:T(8,128)S(1)}, u32[]{:S(2)}, u32[]{:S(2)}) async-start(f32[4,3,8,640]{3,2,1,0:T(8,128)} %get-tuple-element.77), calls=%async_computation | async-start | bytes 491520 | tf_op jit(solution)/shard_map/all_to_all | solution.py:262
  12.8 15.4 %collective-permute-start = (f32[2,8,640]{2,1,0:T(8,128)S(1)}, f32[2,8,640]{2,1,0:T(8,128)S(1)}, u32[]{:S(2)}, u32[]{:S(2)}) collective-permute-start(f32[2,8,640]{2,1,0:T(8,128)S(1)} %get-tuple-element.75), channel_id=1, source_target_pairs={{0,127},{1,2},{2,1},{3,4},{4,3},{5,6},{6,5},{7,8},{8,7},{9,10},{10... | collective-permute-start | bytes 122888 | tf_op jit(solution)/shard_map/ppermute | solution.py:263
  29.3 13.4 %all-to-all-start.1 = ((f32[4,3,8,640]{3,2,1,0:T(8,128)}), f32[4,3,8,640]{3,2,1,0:T(8,128)S(1)}, u32[]{:S(2)}, u32[]{:S(2)}) async-start(f32[4,3,8,640]{3,2,1,0:T(8,128)} %get-tuple-element.85), calls=%async_computation.1 | async-start | bytes 491520 | tf_op jit(solution)/shard_map/all_to_all | solution.py:262
  34.2 8.6 %collective-permute-start.1 = (f32[2,8,640]{2,1,0:T(8,128)S(1)}, f32[2,8,640]{2,1,0:T(8,128)S(1)}, u32[]{:S(2)}, u32[]{:S(2)}) collective-permute-start(f32[2,8,640]{2,1,0:T(8,128)S(1)} %get-tuple-element.84), channel_id=1, source_target_pairs={{0,127},{1,2},{2,1},{3,4},{4,3},{5,6},{6,5},{7,8},{8,7},{9,10},{10... | collective-permute-start | bytes 122888 | tf_op jit(solution)/shard_map/ppermute | solution.py:263
  43.9 13.4 %all-to-all-start.2 = ((f32[4,3,8,640]{3,2,1,0:T(8,128)}), f32[4,3,8,640]{3,2,1,0:T(8,128)S(1)}, u32[]{:S(2)}, u32[]{:S(2)}) async-start(f32[4,3,8,640]{3,2,1,0:T(8,128)} %get-tuple-element.89), calls=%async_computation.2 | async-start | bytes 491520 | tf_op jit(solution)/shard_map/all_to_all | solution.py:262
  48.7 8.6 %collective-permute-start.2 = (f32[2,8,640]{2,1,0:T(8,128)S(1)}, f32[2,8,640]{2,1,0:T(8,128)S(1)}, u32[]{:S(2)}, u32[]{:S(2)}) collective-permute-start(f32[2,8,640]{2,1,0:T(8,128)S(1)} %get-tuple-element.88), channel_id=1, source_target_pairs={{0,127},{1,2},{2,1},{3,4},{4,3},{5,6},{6,5},{7,8},{8,7},{9,10},{10... | collective-permute-start | bytes 122888 | tf_op jit(solution)/shard_map/ppermute | solution.py:263
  58.4 13.4 %all-to-all-start.3 = ((f32[4,3,8,640]{3,2,1,0:T(8,128)}), f32[4,3,8,640]{3,2,1,0:T(8,128)S(1)}, u32[]{:S(2)}, u32[]{:S(2)}) async-start(f32[4,3,8,640]{3,2,1,0:T(8,128)} %get-tuple-element.93), calls=%async_computation.3 | async-start | bytes 491520 | tf_op jit(solution)/shard_map/all_to_all | solution.py:262
  72.9 13.4 %all-to-all-start.4 = ((f32[4,3,8,640]{3,2,1,0:T(8,128)}), f32[4,3,8,640]{3,2,1,0:T(8,128)S(1)}, u32[]{:S(2)}, u32[]{:S(2)}) async-start(f32[4,3,8,640]{3,2,1,0:T(8,128)} %get-tuple-element.97), calls=%async_computation.4 | async-start | bytes 491520 | tf_op jit(solution)/shard_map/all_to_all | solution.py:262
  87.4 13.4 %all-to-all-start.5 = ((f32[4,3,8,640]{3,2,1,0:T(8,128)}), f32[4,3,8,640]{3,2,1,0:T(8,128)S(1)}, u32[]{:S(2)}, u32[]{:S(2)}) async-start(f32[4,3,8,640]{3,2,1,0:T(8,128)} %get-tuple-element.101), calls=%async_computation.5 | async-start | bytes 491520 | tf_op jit(solution)/shard_map/all_to_all | solution.py:262
  92.2 8.6 %collective-permute-start.5 = (f32[2,8,640]{2,1,0:T(8,128)S(1)}, f32[2,8,640]{2,1,0:T(8,128)S(1)}, u32[]{:S(2)}, u32[]{:S(2)}) collective-permute-start(f32[2,8,640]{2,1,0:T(8,128)S(1)} %get-tuple-element.100), channel_id=1, source_target_pairs={{0,127},{1,2},{2,1},{3,4},{4,3},{5,6},{6,5},{7,8},{8,7},{9,10},{10... | collective-permute-start | bytes 122888 | tf_op jit(solution)/shard_map/ppermute | solution.py:263
  101.9 13.4 %all-to-all-start.6 = ((f32[4,3,8,640]{3,2,1,0:T(8,128)}), f32[4,3,8,640]{3,2,1,0:T(8,128)S(1)}, u32[]{:S(2)}, u32[]{:S(2)}) async-start(f32[4,3,8,640]{3,2,1,0:T(8,128)} %get-tuple-element.105), calls=%async_computation.6 | async-start | bytes 491520 | tf_op jit(solution)/shard_map/all_to_all | solution.py:262
  106.7 8.6 %collective-permute-start.6 = (f32[2,8,640]{2,1,0:T(8,128)S(1)}, f32[2,8,640]{2,1,0:T(8,128)S(1)}, u32[]{:S(2)}, u32[]{:S(2)}) collective-permute-start(f32[2,8,640]{2,1,0:T(8,128)S(1)} %get-tuple-element.104), channel_id=1, source_target_pairs={{0,127},{1,2},{2,1},{3,4},{4,3},{5,6},{6,5},{7,8},{8,7},{9,10},{10... | collective-permute-start | bytes 122888 | tf_op jit(solution)/shard_map/ppermute | solution.py:263
  116.4 13.4 %all-to-all-start.7 = ((f32[4,3,8,640]{3,2,1,0:T(8,128)}), f32[4,3,8,640]{3,2,1,0:T(8,128)S(1)}, u32[]{:S(2)}, u32[]{:S(2)}) async-start(f32[4,3,8,640]{3,2,1,0:T(8,128)} %get-tuple-element.109), calls=%async_computation.7 | async-start | bytes 491520 | tf_op jit(solution)/shard_map/all_to_all | solution.py:262
  130.9 13.4 %all-to-all-start.8 = ((f32[4,3,8,640]{3,2,1,0:T(8,128)}), f32[4,3,8,640]{3,2,1,0:T(8,128)S(1)}, u32[]{:S(2)}, u32[]{:S(2)}) async-start(f32[4,3,8,640]{3,2,1,0:T(8,128)} %get-tuple-element.113), calls=%async_computation.8 | async-start | bytes 491520 | tf_op jit(solution)/shard_map/all_to_all | solution.py:262
  145.5 13.4 %all-to-all-start.9 = ((f32[4,3,8,640]{3,2,1,0:T(8,128)}), f32[4,3,8,640]{3,2,1,0:T(8,128)S(1)}, u32[]{:S(2)}, u32[]{:S(2)}) async-start(f32[4,3,8,640]{3,2,1,0:T(8,128)} %get-tuple-element.117), calls=%async_computation.9 | async-start | bytes 491520 | tf_op jit(solution)/shard_map/all_to_all | solution.py:262
  150.3 8.6 %collective-permute-start.9 = (f32[2,8,640]{2,1,0:T(8,128)S(1)}, f32[2,8,640]{2,1,0:T(8,128)S(1)}, u32[]{:S(2)}, u32[]{:S(2)}) collective-permute-start(f32[2,8,640]{2,1,0:T(8,128)S(1)} %get-tuple-element.116), channel_id=1, source_target_pairs={{0,127},{1,2},{2,1},{3,4},{4,3},{5,6},{6,5},{7,8},{8,7},{9,10},{10... | collective-permute-start | bytes 122888 | tf_op jit(solution)/shard_map/ppermute | solution.py:263
  160.0 13.4 %all-to-all-start.10 = ((f32[4,3,8,640]{3,2,1,0:T(8,128)}), f32[4,3,8,640]{3,2,1,0:T(8,128)S(1)}, u32[]{:S(2)}, u32[]{:S(2)}) async-start(f32[4,3,8,640]{3,2,1,0:T(8,128)} %get-tuple-element.121), calls=%async_computation.10 | async-start | bytes 491520 | tf_op jit(solution)/shard_map/all_to_all | solution.py:262
  174.5 13.4 %all-to-all-start.11 = ((f32[4,3,8,640]{3,2,1,0:T(8,128)}), f32[4,3,8,640]{3,2,1,0:T(8,128)S(1)}, u32[]{:S(2)}, u32[]{:S(2)}) async-start(f32[4,3,8,640]{3,2,1,0:T(8,128)} %get-tuple-element.125), calls=%async_computation.11 | async-start | bytes 491520 | tf_op jit(solution)/shard_map/all_to_all | solution.py:262
  189.0 13.4 %all-to-all-start.12 = ((f32[4,3,8,640]{3,2,1,0:T(8,128)}), f32[4,3,8,640]{3,2,1,0:T(8,128)S(1)}, u32[]{:S(2)}, u32[]{:S(2)}) async-start(f32[4,3,8,640]{3,2,1,0:T(8,128)} %get-tuple-element.129), calls=%async_computation.12 | async-start | bytes 491520 | tf_op jit(solution)/shard_map/all_to_all | solution.py:262
  193.8 8.6 %collective-permute-start.12 = (f32[2,8,640]{2,1,0:T(8,128)S(1)}, f32[2,8,640]{2,1,0:T(8,128)S(1)}, u32[]{:S(2)}, u32[]{:S(2)}) collective-permute-start(f32[2,8,640]{2,1,0:T(8,128)S(1)} %get-tuple-element.128), channel_id=1, source_target_pairs={{0,127},{1,2},{2,1},{3,4},{4,3},{5,6},{6,5},{7,8},{8,7},{9,10},{10... | collective-permute-start | bytes 122888 | tf_op jit(solution)/shard_map/ppermute | solution.py:263
  203.5 13.4 %all-to-all-start.13 = ((f32[4,3,8,640]{3,2,1,0:T(8,128)}), f32[4,3,8,640]{3,2,1,0:T(8,128)S(1)}, u32[]{:S(2)}, u32[]{:S(2)}) async-start(f32[4,3,8,640]{3,2,1,0:T(8,128)} %get-tuple-element.133), calls=%async_computation.13 | async-start | bytes 491520 | tf_op jit(solution)/shard_map/all_to_all | solution.py:262
  218.0 13.4 %all-to-all-start.14 = ((f32[4,3,8,640]{3,2,1,0:T(8,128)}), f32[4,3,8,640]{3,2,1,0:T(8,128)S(1)}, u32[]{:S(2)}, u32[]{:S(2)}) async-start(f32[4,3,8,640]{3,2,1,0:T(8,128)} %get-tuple-element.137), calls=%async_computation.14 | async-start | bytes 491520 | tf_op jit(solution)/shard_map/all_to_all | solution.py:262
  232.5 13.4 %all-to-all-start.15 = ((f32[4,3,8,640]{3,2,1,0:T(8,128)}), f32[4,3,8,640]{3,2,1,0:T(8,128)S(1)}, u32[]{:S(2)}, u32[]{:S(2)}) async-start(f32[4,3,8,640]{3,2,1,0:T(8,128)} %get-tuple-element.141), calls=%async_computation.15 | async-start | bytes 491520 | tf_op jit(solution)/shard_map/all_to_all | solution.py:262
  237.4 8.6 %collective-permute-start.15 = (f32[2,8,640]{2,1,0:T(8,128)S(1)}, f32[2,8,640]{2,1,0:T(8,128)S(1)}, u32[]{:S(2)}, u32[]{:S(2)}) collective-permute-start(f32[2,8,640]{2,1,0:T(8,128)S(1)} %get-tuple-element.140), channel_id=1, source_target_pairs={{0,127},{1,2},{2,1},{3,4},{4,3},{5,6},{6,5},{7,8},{8,7},{9,10},{10... | collective-permute-start | bytes 122888 | tf_op jit(solution)/shard_map/ppermute | solution.py:263
  (33 other events, 100.8 us)

commit v5 on v4

--- a/solution.py
+++ b/solution.py
@@ -134,21 +134,15 @@
         put(CROSS + p, weights_ref[2 * p, first + 1], weights_ref[2 * p + 1, first])
 
 
-def send_copy(held, peers_ref, sems, r):
-    return pltpu.make_async_copy(held.at[:, r], peers_ref.at[:, r], sems.at[r])
-
-
-def begin_kernel(adjoint_ref, adjoint_out, peers_ref, held, copied, sems):
-    copies = []
+def begin_kernel(adjoint_ref, adjoint_out, peers_ref, tail, held, sem):
     for r in range(adjoint_out.shape[0]):
-        new = side_by_side(held, adjoint_ref[0, r], adjoint_ref[1, r])
+        new = side_by_side(tail, adjoint_ref[0, r], adjoint_ref[1, r])
         adjoint_out[r] = new
-        for p in range(copied.shape[0]):
-            copied[p, r] = new
-        copies.append(send_copy(copied, peers_ref, sems, r))
-        copies[-1].start()
-    for copy in copies:
-        copy.wait()
+        for p in range(held.shape[0]):
+            held[p, r] = new
+    copy = pltpu.make_async_copy(held, peers_ref, sem)
+    copy.start()
+    copy.wait()
 
 
 def lists_kernel(lists_ref, adjoint_ref, near_ref, far_ref):
@@ -172,23 +166,15 @@
             out_ref[r, :, 2 * cut :] = tail_beside(held, left, right).astype(out_ref.dtype)
 
 
-def here_kernel(tables_ref, adjoint_ref, near_ref, own_j_ref, near_j_ref, source_ref, out_ref):
+def here_kernel(
+    tables_ref, adjoint_ref, near_ref, peers_ref, own_j_ref, near_j_ref, source_ref, volume_ref,
+    out_ref
+):
     other = 1 - lax.rem(lax.axis_index("cell"), 2)
     for r in range(adjoint_ref.shape[0]):
         own = product(adjoint_ref[r], own_j_ref[r])
         block = chosen(tables_ref, NEAR_PICK + r, near_ref[other, 1], near_ref[other, 0])
-        out_ref[r] = source_ref[r] - (own + product(block, near_j_ref[r]))
-
-
-def update_kernel(
-    last, tables_ref, far_ref, far_j_ref, peers_ref, partial_ref, adjoint_ref, volume_ref,
-    step_ref, *outs
-):
-    rows = adjoint_ref.shape[0]
-    copies = []
-    for r in range(rows):
-        block = chosen(tables_ref, FAR_PICK + r, far_ref[1], far_ref[0])
-        flux = product(block, far_j_ref[r])
+        near = product(block, near_j_ref[r])
         same = cross = None
         for p in range(peers_ref.shape[0]):
             one = tables_ref[pl.ds(SAME + p, 1), :] * peers_ref[p, r]
@@ -196,25 +182,40 @@
             same, cross = (one, two) if same is None else (same + one, cross + two)
         coupled = same + swapped(cross)
         scale = SCALE * volume_ref[pl.ds(r, 1), :]
+        out_ref[r] = source_ref[r] - (own + near) - scale * coupled
+
+
+def update_kernel(
+    last, tables_ref, far_ref, far_j_ref, partial_ref, adjoint_ref, step_ref, *outs
+):
+    rows = adjoint_ref.shape[0]
+    fluxes = [
+        product(chosen(tables_ref, FAR_PICK + r, far_ref[1], far_ref[0]), far_j_ref[r])
+        for r in range(rows)
+    ]
+    residuals, news = [], []
+    for r, flux in enumerate(fluxes):
         live = tables_ref[pl.ds(LIVE + r, 1), :]
-        residual = live * (partial_ref[r] - flux - scale * coupled)
-        new = adjoint_ref[r] + step_ref[pl.ds(r, 1), :] * residual
-        if last:
-            for value, out_ref in zip((new, residual), outs):
+        residuals.append(live * (partial_ref[r] - flux))
+        news.append(adjoint_ref[r] + step_ref[pl.ds(r, 1), :] * residuals[r])
+    if last:
+        for values, out_ref in zip((news, residuals), outs):
+            for r, value in enumerate(values):
                 out_ref[0, r] = left_of(value)
                 out_ref[1, r] = left_of(swapped(value))
-            continue
-        outs[0][r] = new
-        for p in range(peers_ref.shape[0]):
-            outs[4][p, r] = new
-        copies.append(send_copy(outs[4], outs[3], outs[5], r))
-        copies[-1].start()
-    if not last:
-        for e in range(REACH):
-            outs[1][e] = listed(tables_ref, NEAR_SEND, e, outs[0])
-            outs[2][e] = listed(tables_ref, FAR_SEND, e, outs[0])
-    for copy in copies:
-        copy.wait()
+        return
+    adjoint_out, near_out, far_out, peers_out, held, sem = outs
+    for r, new in enumerate(news):
+        for p in range(held.shape[0]):
+            held[p, r] = new
+    copy = pltpu.make_async_copy(held, peers_out, sem)
+    copy.start()
+    for r, new in enumerate(news):
+        adjoint_out[r] = new
+    for e in range(REACH):
+        near_out[e] = listed(tables_ref, NEAR_SEND, e, news)
+        far_out[e] = listed(tables_ref, FAR_SEND, e, news)
+    copy.wait()
 
 
 def call(kernel, ins, outs, *args, scratch=()):
@@ -241,7 +242,7 @@
     block = ((rows, objectives, lanes), f32)
     halo = ((REACH, objectives, lanes), f32)
     gathered = ((peers,) + block[0], f32)
-    sends = [pltpu.VMEM(*gathered), pltpu.SemaphoreType.DMA((rows,))]
+    sends = [pltpu.VMEM(*gathered), pltpu.SemaphoreType.DMA]
     listed_out = (("v", block), ("v", halo), ("v", halo), ("a", gathered))
     held = pltpu.VMEM((objectives, TILE), f32)
     adjoint, spread = call(
@@ -263,13 +264,13 @@
         far = lax.ppermute(far, "cell", far_pairs)
         near = lax.all_gather(near, "cell", axis_index_groups=near_groups)
         partial = call(
-            here_kernel, "vvvvvv", (("v", block),), tables, adjoint, near, own_j, near_j, source
+            here_kernel, "vvvvvvvv", (("v", block),),
+            tables, adjoint, near, spread, own_j, near_j, source, volume,
         )[0]
         result = call(
-            functools.partial(update_kernel, last), "vvvvvvvv",
+            functools.partial(update_kernel, last), "vvvvvv",
             (("v", (shape, f32)),) * 2 if last else listed_out,
-            tables, far, far_j, spread, partial, adjoint, volume, step,
-            scratch=[] if last else sends,
+            tables, far, far_j, partial, adjoint, step, scratch=[] if last else sends,
         )
         if last:
             return result[0], result[1]

time: 250 us -> 252 us (level)
    unnamed x50 -> x52, local copies, waits for them, and re-layouts: 23.3 us -> 25.4 us
  transfers between devices with their start and end apart: 32 -> 32, of which waited for: 15 -> 16; matrix products, arithmetic and copies ran while one was open for 0% -> 0% of each run, Pallas kernels for 5% -> 5%
where the time goes in v5:
time: 252 us; the launch traced here: 250 us
  starting transfers between devices  141 us (56%)
  Pallas kernels  30.4 us (12%)
  blocking collectives  30 us (12%)
  local copies, waits for them, and re-layouts  25.4 us (10%)
  waiting for transfers between devices  21 us (8%)
    all_to_all x16, starting transfers between devices, on_device(): spread = lax.all_to_all(spread, 'inst', 0, 0)  81.4 us
    ppermute x16, starting transfers between devices, on_device(): far = lax.ppermute(far, 'cell', far_pairs)  59.5 us
    pallas_call x36, Pallas kernels, call(): pl.pallas_call(kernel, in_specs=[spaces[c] for c in ins], out_specs=[spac...  30.4 us
    all_gather x16, blocking collectives, on_device(): near = lax.all_gather(near, 'cell', axis_index_groups=near_groups)  30 us
    unnamed x52, local copies, waits for them, and re-layouts  25.4 us
    ppermute x16, waiting for transfers between devices, on_device(): far = lax.ppermute(far, 'cell', far_pairs)  19.7 us
  transfers between devices with their start and end apart: 32, of which 16 were waited for; matrix products, arithmetic and copies ran while one was open for 0% of the time, Pallas kernels for 5%

profile of v5, /device:TPU:2, one launch (start us, length us, event | category | flops | bytes accessed | tf_op | source)
XLA Modules:
  0.0 249.6 jit_solution(5198717216500523168)
XLA Ops:
  2.3 9.3 %all-to-all-start = ((f32[4,3,8,640]{3,2,1,0:T(8,128)}), f32[4,3,8,640]{3,2,1,0:T(8,128)S(1)}, u32[]{:S(2)}, u32[]{:S(2)}) async-start(f32[4,3,8,640]{3,2,1,0:T(8,128)} %get-tuple-element.78), calls=%async_computation | async-start | bytes 491520 | tf_op jit(solution)/shard_map/all_to_all | solution.py:263
  12.8 8.3 %collective-permute-start = (f32[2,8,640]{2,1,0:T(8,128)S(1)}, f32[2,8,640]{2,1,0:T(8,128)S(1)}, u32[]{:S(2)}, u32[]{:S(2)}) collective-permute-start(f32[2,8,640]{2,1,0:T(8,128)S(1)} %get-tuple-element.75), channel_id=1, source_target_pairs={{0,127},{1,2},{2,1},{3,4},{4,3},{5,6},{6,5},{7,8},{8,7},{9,10},{10... | collective-permute-start | bytes 122888 | tf_op jit(solution)/shard_map/ppermute | solution.py:264
  31.5 4.8 %all-to-all-start.1 = ((f32[4,3,8,640]{3,2,1,0:T(8,128)}), f32[4,3,8,640]{3,2,1,0:T(8,128)S(1)}, u32[]{:S(2)}, u32[]{:S(2)}) async-start(f32[4,3,8,640]{3,2,1,0:T(8,128)} %get-tuple-element.87), calls=%async_computation.1 | async-start | bytes 491520 | tf_op jit(solution)/shard_map/all_to_all | solution.py:263
  46.0 4.8 %all-to-all-start.2 = ((f32[4,3,8,640]{3,2,1,0:T(8,128)}), f32[4,3,8,640]{3,2,1,0:T(8,128)S(1)}, u32[]{:S(2)}, u32[]{:S(2)}) async-start(f32[4,3,8,640]{3,2,1,0:T(8,128)} %get-tuple-element.91), calls=%async_computation.2 | async-start | bytes 491520 | tf_op jit(solution)/shard_map/all_to_all | solution.py:263
  60.6 4.8 %all-to-all-start.3 = ((f32[4,3,8,640]{3,2,1,0:T(8,128)}), f32[4,3,8,640]{3,2,1,0:T(8,128)S(1)}, u32[]{:S(2)}, u32[]{:S(2)}) async-start(f32[4,3,8,640]{3,2,1,0:T(8,128)} %get-tuple-element.95), calls=%async_computation.3 | async-start | bytes 491520 | tf_op jit(solution)/shard_map/all_to_all | solution.py:263
  65.4 3.5 %collective-permute-start.3 = (f32[2,8,640]{2,1,0:T(8,128)S(1)}, f32[2,8,640]{2,1,0:T(8,128)S(1)}, u32[]{:S(2)}, u32[]{:S(2)}) collective-permute-start(f32[2,8,640]{2,1,0:T(8,128)S(1)} %get-tuple-element.92), channel_id=1, source_target_pairs={{0,127},{1,2},{2,1},{3,4},{4,3},{5,6},{6,5},{7,8},{8,7},{9,10},{10... | collective-permute-start | bytes 122888 | tf_op jit(solution)/shard_map/ppermute | solution.py:264
  75.1 4.8 %all-to-all-start.4 = ((f32[4,3,8,640]{3,2,1,0:T(8,128)}), f32[4,3,8,640]{3,2,1,0:T(8,128)S(1)}, u32[]{:S(2)}, u32[]{:S(2)}) async-start(f32[4,3,8,640]{3,2,1,0:T(8,128)} %get-tuple-element.99), calls=%async_computation.4 | async-start | bytes 491520 | tf_op jit(solution)/shard_map/all_to_all | solution.py:263
  79.9 3.5 %collective-permute-start.4 = (f32[2,8,640]{2,1,0:T(8,128)S(1)}, f32[2,8,640]{2,1,0:T(8,128)S(1)}, u32[]{:S(2)}, u32[]{:S(2)}) collective-permute-start(f32[2,8,640]{2,1,0:T(8,128)S(1)} %get-tuple-element.96), channel_id=1, source_target_pairs={{0,127},{1,2},{2,1},{3,4},{4,3},{5,6},{6,5},{7,8},{8,7},{9,10},{10... | collective-permute-start | bytes 122888 | tf_op jit(solution)/shard_map/ppermute | solution.py:264
  89.6 4.8 %all-to-all-start.5 = ((f32[4,3,8,640]{3,2,1,0:T(8,128)}), f32[4,3,8,640]{3,2,1,0:T(8,128)S(1)}, u32[]{:S(2)}, u32[]{:S(2)}) async-start(f32[4,3,8,640]{3,2,1,0:T(8,128)} %get-tuple-element.103), calls=%async_computation.5 | async-start | bytes 491520 | tf_op jit(solution)/shard_map/all_to_all | solution.py:263
  104.2 4.8 %all-to-all-start.6 = ((f32[4,3,8,640]{3,2,1,0:T(8,128)}), f32[4,3,8,640]{3,2,1,0:T(8,128)S(1)}, u32[]{:S(2)}, u32[]{:S(2)}) async-start(f32[4,3,8,640]{3,2,1,0:T(8,128)} %get-tuple-element.107), calls=%async_computation.6 | async-start | bytes 491520 | tf_op jit(solution)/shard_map/all_to_all | solution.py:263
  109.0 3.5 %collective-permute-start.6 = (f32[2,8,640]{2,1,0:T(8,128)S(1)}, f32[2,8,640]{2,1,0:T(8,128)S(1)}, u32[]{:S(2)}, u32[]{:S(2)}) collective-permute-start(f32[2,8,640]{2,1,0:T(8,128)S(1)} %get-tuple-element.104), channel_id=1, source_target_pairs={{0,127},{1,2},{2,1},{3,4},{4,3},{5,6},{6,5},{7,8},{8,7},{9,10},{10... | collective-permute-start | bytes 122888 | tf_op jit(solution)/shard_map/ppermute | solution.py:264
  118.7 4.8 %all-to-all-start.7 = ((f32[4,3,8,640]{3,2,1,0:T(8,128)}), f32[4,3,8,640]{3,2,1,0:T(8,128)S(1)}, u32[]{:S(2)}, u32[]{:S(2)}) async-start(f32[4,3,8,640]{3,2,1,0:T(8,128)} %get-tuple-element.111), calls=%async_computation.7 | async-start | bytes 491520 | tf_op jit(solution)/shard_map/all_to_all | solution.py:263
  133.3 4.8 %all-to-all-start.8 = ((f32[4,3,8,640]{3,2,1,0:T(8,128)}), f32[4,3,8,640]{3,2,1,0:T(8,128)S(1)}, u32[]{:S(2)}, u32[]{:S(2)}) async-start(f32[4,3,8,640]{3,2,1,0:T(8,128)} %get-tuple-element.115), calls=%async_computation.8 | async-start | bytes 491520 | tf_op jit(solution)/shard_map/all_to_all | solution.py:263
  138.1 3.5 %collective-permute-start.8 = (f32[2,8,640]{2,1,0:T(8,128)S(1)}, f32[2,8,640]{2,1,0:T(8,128)S(1)}, u32[]{:S(2)}, u32[]{:S(2)}) collective-permute-start(f32[2,8,640]{2,1,0:T(8,128)S(1)} %get-tuple-element.112), channel_id=1, source_target_pairs={{0,127},{1,2},{2,1},{3,4},{4,3},{5,6},{6,5},{7,8},{8,7},{9,10},{10... | collective-permute-start | bytes 122888 | tf_op jit(solution)/shard_map/ppermute | solution.py:264
  147.8 4.8 %all-to-all-start.9 = ((f32[4,3,8,640]{3,2,1,0:T(8,128)}), f32[4,3,8,640]{3,2,1,0:T(8,128)S(1)}, u32[]{:S(2)}, u32[]{:S(2)}) async-start(f32[4,3,8,640]{3,2,1,0:T(8,128)} %get-tuple-element.119), calls=%async_computation.9 | async-start | bytes 491520 | tf_op jit(solution)/shard_map/all_to_all | solution.py:263
  162.3 4.8 %all-to-all-start.10 = ((f32[4,3,8,640]{3,2,1,0:T(8,128)}), f32[4,3,8,640]{3,2,1,0:T(8,128)S(1)}, u32[]{:S(2)}, u32[]{:S(2)}) async-start(f32[4,3,8,640]{3,2,1,0:T(8,128)} %get-tuple-element.123), calls=%async_computation.10 | async-start | bytes 491520 | tf_op jit(solution)/shard_map/all_to_all | solution.py:263
  167.1 3.5 %collective-permute-start.10 = (f32[2,8,640]{2,1,0:T(8,128)S(1)}, f32[2,8,640]{2,1,0:T(8,128)S(1)}, u32[]{:S(2)}, u32[]{:S(2)}) collective-permute-start(f32[2,8,640]{2,1,0:T(8,128)S(1)} %get-tuple-element.120), channel_id=1, source_target_pairs={{0,127},{1,2},{2,1},{3,4},{4,3},{5,6},{6,5},{7,8},{8,7},{9,10},{10... | collective-permute-start | bytes 122888 | tf_op jit(solution)/shard_map/ppermute | solution.py:264
  176.9 4.8 %all-to-all-start.11 = ((f32[4,3,8,640]{3,2,1,0:T(8,128)}), f32[4,3,8,640]{3,2,1,0:T(8,128)S(1)}, u32[]{:S(2)}, u32[]{:S(2)}) async-start(f32[4,3,8,640]{3,2,1,0:T(8,128)} %get-tuple-element.127), calls=%async_computation.11 | async-start | bytes 491520 | tf_op jit(solution)/shard_map/all_to_all | solution.py:263
  191.4 4.8 %all-to-all-start.12 = ((f32[4,3,8,640]{3,2,1,0:T(8,128)}), f32[4,3,8,640]{3,2,1,0:T(8,128)S(1)}, u32[]{:S(2)}, u32[]{:S(2)}) async-start(f32[4,3,8,640]{3,2,1,0:T(8,128)} %get-tuple-element.131), calls=%async_computation.12 | async-start | bytes 491520 | tf_op jit(solution)/shard_map/all_to_all | solution.py:263
  196.2 3.7 %collective-permute-start.12 = (f32[2,8,640]{2,1,0:T(8,128)S(1)}, f32[2,8,640]{2,1,0:T(8,128)S(1)}, u32[]{:S(2)}, u32[]{:S(2)}) collective-permute-start(f32[2,8,640]{2,1,0:T(8,128)S(1)} %get-tuple-element.128), channel_id=1, source_target_pairs={{0,127},{1,2},{2,1},{3,4},{4,3},{5,6},{6,5},{7,8},{8,7},{9,10},{10... | collective-permute-start | bytes 122888 | tf_op jit(solution)/shard_map/ppermute | solution.py:264
  205.9 4.8 %all-to-all-start.13 = ((f32[4,3,8,640]{3,2,1,0:T(8,128)}), f32[4,3,8,640]{3,2,1,0:T(8,128)S(1)}, u32[]{:S(2)}, u32[]{:S(2)}) async-start(f32[4,3,8,640]{3,2,1,0:T(8,128)} %get-tuple-element.135), calls=%async_computation.13 | async-start | bytes 491520 | tf_op jit(solution)/shard_map/all_to_all | solution.py:263
  220.5 4.8 %all-to-all-start.14 = ((f32[4,3,8,640]{3,2,1,0:T(8,128)}), f32[4,3,8,640]{3,2,1,0:T(8,128)S(1)}, u32[]{:S(2)}, u32[]{:S(2)}) async-start(f32[4,3,8,640]{3,2,1,0:T(8,128)} %get-tuple-element.139), calls=%async_computation.14 | async-start | bytes 491520 | tf_op jit(solution)/shard_map/all_to_all | solution.py:263
  225.3 3.5 %collective-permute-start.14 = (f32[2,8,640]{2,1,0:T(8,128)S(1)}, f32[2,8,640]{2,1,0:T(8,128)S(1)}, u32[]{:S(2)}, u32[]{:S(2)}) collective-permute-start(f32[2,8,640]{2,1,0:T(8,128)S(1)} %get-tuple-element.136), channel_id=1, source_target_pairs={{0,127},{1,2},{2,1},{3,4},{4,3},{5,6},{6,5},{7,8},{8,7},{9,10},{10... | collective-permute-start | bytes 122888 | tf_op jit(solution)/shard_map/ppermute | solution.py:264
  235.0 4.8 %all-to-all-start.15 = ((f32[4,3,8,640]{3,2,1,0:T(8,128)}), f32[4,3,8,640]{3,2,1,0:T(8,128)S(1)}, u32[]{:S(2)}, u32[]{:S(2)}) async-start(f32[4,3,8,640]{3,2,1,0:T(8,128)} %get-tuple-element.143), calls=%async_computation.15 | async-start | bytes 491520 | tf_op jit(solution)/shard_map/all_to_all | solution.py:263
  (144 shorter events, 133.5 us)
Async XLA Ops:
  2.3 26.1 %all-to-all-start = ((f32[4,3,8,640]{3,2,1,0:T(8,128)}), f32[4,3,8,640]{3,2,1,0:T(8,128)S(1)}, u32[]{:S(2)}, u32[]{:S(2)}) async-start(f32[4,3,8,640]{3,2,1,0:T(8,128)} %get-tuple-element.78), calls=%async_computation | async-start | bytes 491520 | tf_op jit(solution)/shard_map/all_to_all | solution.py:263
  12.8 17.5 %collective-permute-start = (f32[2,8,640]{2,1,0:T(8,128)S(1)}, f32[2,8,640]{2,1,0:T(8,128)S(1)}, u32[]{:S(2)}, u32[]{:S(2)}) collective-permute-start(f32[2,8,640]{2,1,0:T(8,128)S(1)} %get-tuple-element.75), channel_id=1, source_target_pairs={{0,127},{1,2},{2,1},{3,4},{4,3},{5,6},{6,5},{7,8},{8,7},{9,10},{10... | collective-permute-start | bytes 122888 | tf_op jit(solution)/shard_map/ppermute | solution.py:264
  31.5 10.2 %all-to-all-start.1 = ((f32[4,3,8,640]{3,2,1,0:T(8,128)}), f32[4,3,8,640]{3,2,1,0:T(8,128)S(1)}, u32[]{:S(2)}, u32[]{:S(2)}) async-start(f32[4,3,8,640]{3,2,1,0:T(8,128)} %get-tuple-element.87), calls=%async_computation.1 | async-start | bytes 491520 | tf_op jit(solution)/shard_map/all_to_all | solution.py:263
  36.3 8.6 %collective-permute-start.1 = (f32[2,8,640]{2,1,0:T(8,128)S(1)}, f32[2,8,640]{2,1,0:T(8,128)S(1)}, u32[]{:S(2)}, u32[]{:S(2)}) collective-permute-start(f32[2,8,640]{2,1,0:T(8,128)S(1)} %get-tuple-element.84), channel_id=1, source_target_pairs={{0,127},{1,2},{2,1},{3,4},{4,3},{5,6},{6,5},{7,8},{8,7},{9,10},{10... | collective-permute-start | bytes 122888 | tf_op jit(solution)/shard_map/ppermute | solution.py:264
  46.0 10.2 %all-to-all-start.2 = ((f32[4,3,8,640]{3,2,1,0:T(8,128)}), f32[4,3,8,640]{3,2,1,0:T(8,128)S(1)}, u32[]{:S(2)}, u32[]{:S(2)}) async-start(f32[4,3,8,640]{3,2,1,0:T(8,128)} %get-tuple-element.91), calls=%async_computation.2 | async-start | bytes 491520 | tf_op jit(solution)/shard_map/all_to_all | solution.py:263
  50.8 8.6 %collective-permute-start.2 = (f32[2,8,640]{2,1,0:T(8,128)S(1)}, f32[2,8,640]{2,1,0:T(8,128)S(1)}, u32[]{:S(2)}, u32[]{:S(2)}) collective-permute-start(f32[2,8,640]{2,1,0:T(8,128)S(1)} %get-tuple-element.88), channel_id=1, source_target_pairs={{0,127},{1,2},{2,1},{3,4},{4,3},{5,6},{6,5},{7,8},{8,7},{9,10},{10... | collective-permute-start | bytes 122888 | tf_op jit(solution)/shard_map/ppermute | solution.py:264
  60.6 10.2 %all-to-all-start.3 = ((f32[4,3,8,640]{3,2,1,0:T(8,128)}), f32[4,3,8,640]{3,2,1,0:T(8,128)S(1)}, u32[]{:S(2)}, u32[]{:S(2)}) async-start(f32[4,3,8,640]{3,2,1,0:T(8,128)} %get-tuple-element.95), calls=%async_computation.3 | async-start | bytes 491520 | tf_op jit(solution)/shard_map/all_to_all | solution.py:263
  65.4 8.6 %collective-permute-start.3 = (f32[2,8,640]{2,1,0:T(8,128)S(1)}, f32[2,8,640]{2,1,0:T(8,128)S(1)}, u32[]{:S(2)}, u32[]{:S(2)}) collective-permute-start(f32[2,8,640]{2,1,0:T(8,128)S(1)} %get-tuple-element.92), channel_id=1, source_target_pairs={{0,127},{1,2},{2,1},{3,4},{4,3},{5,6},{6,5},{7,8},{8,7},{9,10},{10... | collective-permute-start | bytes 122888 | tf_op jit(solution)/shard_map/ppermute | solution.py:264
  75.1 10.2 %all-to-all-start.4 = ((f32[4,3,8,640]{3,2,1,0:T(8,128)}), f32[4,3,8,640]{3,2,1,0:T(8,128)S(1)}, u32[]{:S(2)}, u32[]{:S(2)}) async-start(f32[4,3,8,640]{3,2,1,0:T(8,128)} %get-tuple-element.99), calls=%async_computation.4 | async-start | bytes 491520 | tf_op jit(solution)/shard_map/all_to_all | solution.py:263
  79.9 8.6 %collective-permute-start.4 = (f32[2,8,640]{2,1,0:T(8,128)S(1)}, f32[2,8,640]{2,1,0:T(8,128)S(1)}, u32[]{:S(2)}, u32[]{:S(2)}) collective-permute-start(f32[2,8,640]{2,1,0:T(8,128)S(1)} %get-tuple-element.96), channel_id=1, source_target_pairs={{0,127},{1,2},{2,1},{3,4},{4,3},{5,6},{6,5},{7,8},{8,7},{9,10},{10... | collective-permute-start | bytes 122888 | tf_op jit(solution)/shard_map/ppermute | solution.py:264
  89.6 10.2 %all-to-all-start.5 = ((f32[4,3,8,640]{3,2,1,0:T(8,128)}), f32[4,3,8,640]{3,2,1,0:T(8,128)S(1)}, u32[]{:S(2)}, u32[]{:S(2)}) async-start(f32[4,3,8,640]{3,2,1,0:T(8,128)} %get-tuple-element.103), calls=%async_computation.5 | async-start | bytes 491520 | tf_op jit(solution)/shard_map/all_to_all | solution.py:263
  104.2 10.2 %all-to-all-start.6 = ((f32[4,3,8,640]{3,2,1,0:T(8,128)}), f32[4,3,8,640]{3,2,1,0:T(8,128)S(1)}, u32[]{:S(2)}, u32[]{:S(2)}) async-start(f32[4,3,8,640]{3,2,1,0:T(8,128)} %get-tuple-element.107), calls=%async_computation.6 | async-start | bytes 491520 | tf_op jit(solution)/shard_map/all_to_all | solution.py:263
  118.7 10.2 %all-to-all-start.7 = ((f32[4,3,8,640]{3,2,1,0:T(8,128)}), f32[4,3,8,640]{3,2,1,0:T(8,128)S(1)}, u32[]{:S(2)}, u32[]{:S(2)}) async-start(f32[4,3,8,640]{3,2,1,0:T(8,128)} %get-tuple-element.111), calls=%async_computation.7 | async-start | bytes 491520 | tf_op jit(solution)/shard_map/all_to_all | solution.py:263
  123.5 8.6 %collective-permute-start.7 = (f32[2,8,640]{2,1,0:T(8,128)S(1)}, f32[2,8,640]{2,1,0:T(8,128)S(1)}, u32[]{:S(2)}, u32[]{:S(2)}) collective-permute-start(f32[2,8,640]{2,1,0:T(8,128)S(1)} %get-tuple-element.108), channel_id=1, source_target_pairs={{0,127},{1,2},{2,1},{3,4},{4,3},{5,6},{6,5},{7,8},{8,7},{9,10},{10... | collective-permute-start | bytes 122888 | tf_op jit(solution)/shard_map/ppermute | solution.py:264
  133.3 10.2 %all-to-all-start.8 = ((f32[4,3,8,640]{3,2,1,0:T(8,128)}), f32[4,3,8,640]{3,2,1,0:T(8,128)S(1)}, u32[]{:S(2)}, u32[]{:S(2)}) async-start(f32[4,3,8,640]{3,2,1,0:T(8,128)} %get-tuple-element.115), calls=%async_computation.8 | async-start | bytes 491520 | tf_op jit(solution)/shard_map/all_to_all | solution.py:263
  138.1 8.6 %collective-permute-start.8 = (f32[2,8,640]{2,1,0:T(8,128)S(1)}, f32[2,8,640]{2,1,0:T(8,128)S(1)}, u32[]{:S(2)}, u32[]{:S(2)}) collective-permute-start(f32[2,8,640]{2,1,0:T(8,128)S(1)} %get-tuple-element.112), channel_id=1, source_target_pairs={{0,127},{1,2},{2,1},{3,4},{4,3},{5,6},{6,5},{7,8},{8,7},{9,10},{10... | collective-permute-start | bytes 122888 | tf_op jit(solution)/shard_map/ppermute | solution.py:264
  147.8 10.2 %all-to-all-start.9 = ((f32[4,3,8,640]{3,2,1,0:T(8,128)}), f32[4,3,8,640]{3,2,1,0:T(8,128)S(1)}, u32[]{:S(2)}, u32[]{:S(2)}) async-start(f32[4,3,8,640]{3,2,1,0:T(8,128)} %get-tuple-element.119), calls=%async_computation.9 | async-start | bytes 491520 | tf_op jit(solution)/shard_map/all_to_all | solution.py:263
  162.3 10.2 %all-to-all-start.10 = ((f32[4,3,8,640]{3,2,1,0:T(8,128)}), f32[4,3,8,640]{3,2,1,0:T(8,128)S(1)}, u32[]{:S(2)}, u32[]{:S(2)}) async-start(f32[4,3,8,640]{3,2,1,0:T(8,128)} %get-tuple-element.123), calls=%async_computation.10 | async-start | bytes 491520 | tf_op jit(solution)/shard_map/all_to_all | solution.py:263
  176.9 10.3 %all-to-all-start.11 = ((f32[4,3,8,640]{3,2,1,0:T(8,128)}), f32[4,3,8,640]{3,2,1,0:T(8,128)S(1)}, u32[]{:S(2)}, u32[]{:S(2)}) async-start(f32[4,3,8,640]{3,2,1,0:T(8,128)} %get-tuple-element.127), calls=%async_computation.11 | async-start | bytes 491520 | tf_op jit(solution)/shard_map/all_to_all | solution.py:263
  191.4 10.4 %all-to-all-start.12 = ((f32[4,3,8,640]{3,2,1,0:T(8,128)}), f32[4,3,8,640]{3,2,1,0:T(8,128)S(1)}, u32[]{:S(2)}, u32[]{:S(2)}) async-start(f32[4,3,8,640]{3,2,1,0:T(8,128)} %get-tuple-element.131), calls=%async_computation.12 | async-start | bytes 491520 | tf_op jit(solution)/shard_map/all_to_all | solution.py:263
  205.9 10.2 %all-to-all-start.13 = ((f32[4,3,8,640]{3,2,1,0:T(8,128)}), f32[4,3,8,640]{3,2,1,0:T(8,128)S(1)}, u32[]{:S(2)}, u32[]{:S(2)}) async-start(f32[4,3,8,640]{3,2,1,0:T(8,128)} %get-tuple-element.135), calls=%async_computation.13 | async-start | bytes 491520 | tf_op jit(solution)/shard_map/all_to_all | solution.py:263
  220.5 10.2 %all-to-all-start.14 = ((f32[4,3,8,640]{3,2,1,0:T(8,128)}), f32[4,3,8,640]{3,2,1,0:T(8,128)S(1)}, u32[]{:S(2)}, u32[]{:S(2)}) async-start(f32[4,3,8,640]{3,2,1,0:T(8,128)} %get-tuple-element.139), calls=%async_computation.14 | async-start | bytes 491520 | tf_op jit(solution)/shard_map/all_to_all | solution.py:263
  235.0 10.2 %all-to-all-start.15 = ((f32[4,3,8,640]{3,2,1,0:T(8,128)}), f32[4,3,8,640]{3,2,1,0:T(8,128)S(1)}, u32[]{:S(2)}, u32[]{:S(2)}) async-start(f32[4,3,8,640]{3,2,1,0:T(8,128)} %get-tuple-element.143), calls=%async_computation.15 | async-start | bytes 491520 | tf_op jit(solution)/shard_map/all_to_all | solution.py:263
  239.8 8.6 %collective-permute-start.15 = (f32[2,8,640]{2,1,0:T(8,128)S(1)}, f32[2,8,640]{2,1,0:T(8,128)S(1)}, u32[]{:S(2)}, u32[]{:S(2)}) collective-permute-start(f32[2,8,640]{2,1,0:T(8,128)S(1)} %get-tuple-element.140), channel_id=1, source_target_pairs={{0,127},{1,2},{2,1},{3,4},{4,3},{5,6},{6,5},{7,8},{8,7},{9,10},{10... | collective-permute-start | bytes 122888 | tf_op jit(solution)/shard_map/ppermute | solution.py:264
  (34 other events, 104.8 us)

commit v6 on v4

--- a/solution.py
+++ b/solution.py
@@ -138,7 +138,10 @@
     return pltpu.make_async_copy(held.at[:, r], peers_ref.at[:, r], sems.at[r])
 
 
-def begin_kernel(adjoint_ref, adjoint_out, peers_ref, held, copied, sems):
+def begin_kernel(
+    lists_ref, adjoint_ref, adjoint_out, near_ref, far_ref, peers_ref, held, copied, sems
+):
+    side = lax.rem(lax.axis_index("cell"), 2)
     copies = []
     for r in range(adjoint_out.shape[0]):
         new = side_by_side(held, adjoint_ref[0, r], adjoint_ref[1, r])
@@ -147,15 +150,11 @@
             copied[p, r] = new
         copies.append(send_copy(copied, peers_ref, sems, r))
         copies[-1].start()
+    for e in range(REACH):
+        near_ref[e] = adjoint_out[lists_ref[REACH - REACH * side + e]]
+        far_ref[e] = adjoint_out[lists_ref[REACH * side + e]]
     for copy in copies:
         copy.wait()
-
-
-def lists_kernel(lists_ref, adjoint_ref, near_ref, far_ref):
-    side = lax.rem(lax.axis_index("cell"), 2)
-    for e in range(REACH):
-        near_ref[e] = adjoint_ref[lists_ref[REACH - REACH * side + e]]
-        far_ref[e] = adjoint_ref[lists_ref[REACH * side + e]]
 
 
 def pack_kernel(jacobian_ref, own_ref, near_ref, far_ref, held):
@@ -244,10 +243,9 @@
     sends = [pltpu.VMEM(*gathered), pltpu.SemaphoreType.DMA((rows,))]
     listed_out = (("v", block), ("v", halo), ("v", halo), ("a", gathered))
     held = pltpu.VMEM((objectives, TILE), f32)
-    adjoint, spread = call(
-        begin_kernel, "v", (("v", block), ("a", gathered)), adjoint, scratch=[held] + sends
-    )
-    near, far = call(lists_kernel, "sv", (("v", halo),) * 2, lists, adjoint)
+    adjoint, near, far, spread = call(
+        begin_kernel, "sv", listed_out, lists, adjoint, scratch=[held] + sends
+    )
     cells_out = ("v", ((rows, lanes), f32))
     tables, source, volume, step = call(
         tables_kernel, "ssssvvv", (("v", ((TABLE, lanes), f32)), ("v", block)) + (cells_out,) * 2,

time: 250 us -> 250 us (level)
    pallas_call x36 -> x35, Pallas kernels: 29.9 us -> 29.7 us  [call(): pl.pallas_call(kernel, in_specs=[spaces[c] for c in ins], out_specs=[spac...]
where the time goes in v6:
time: 250 us; the launch traced here: 247 us
  starting transfers between devices  141 us (56%)
  blocking collectives  29.8 us (12%)
  Pallas kernels  29.7 us (12%)
  local copies, waits for them, and re-layouts  23.3 us (9%)
  waiting for transfers between devices  21.6 us (9%)
    all_to_all x16, starting transfers between devices, on_device(): spread = lax.all_to_all(spread, 'inst', 0, 0)  81.4 us
    ppermute x16, starting transfers between devices, on_device(): far = lax.ppermute(far, 'cell', far_pairs)  59.2 us
    all_gather x16, blocking collectives, on_device(): near = lax.all_gather(near, 'cell', axis_index_groups=near_groups)  29.8 us
    pallas_call x35, Pallas kernels, call(): pl.pallas_call(kernel, in_specs=[spaces[c] for c in ins], out_specs=[spac...  29.7 us
    unnamed x50, local copies, waits for them, and re-layouts  23.3 us
    ppermute x16, waiting for transfers between devices, on_device(): far = lax.ppermute(far, 'cell', far_pairs)  21.6 us
  transfers between devices with their start and end apart: 32, of which 15 were waited for; matrix products, arithmetic and copies ran while one was open for 0% of the time, Pallas kernels for 5%

profile of v6, /device:TPU:2, one launch (start us, length us, event | category | flops | bytes accessed | tf_op | source)
XLA Modules:
  0.0 246.9 jit_solution(2986636026541136464)
XLA Ops:
  3.5 9.3 %all-to-all-start = ((f32[4,3,8,640]{3,2,1,0:T(8,128)}), f32[4,3,8,640]{3,2,1,0:T(8,128)S(1)}, u32[]{:S(2)}, u32[]{:S(2)}) async-start(f32[4,3,8,640]{3,2,1,0:T(8,128)} %get-tuple-element.76), calls=%async_computation | async-start | bytes 491520 | tf_op jit(solution)/shard_map/all_to_all | solution.py:260
  12.8 8.3 %collective-permute-start = (f32[2,8,640]{2,1,0:T(8,128)S(1)}, f32[2,8,640]{2,1,0:T(8,128)S(1)}, u32[]{:S(2)}, u32[]{:S(2)}) collective-permute-start(f32[2,8,640]{2,1,0:T(8,128)S(1)} %get-tuple-element.74), channel_id=1, source_target_pairs={{0,127},{1,2},{2,1},{3,4},{4,3},{5,6},{6,5},{7,8},{8,7},{9,10},{10... | collective-permute-start | bytes 122888 | tf_op jit(solution)/shard_map/ppermute | solution.py:261
  29.3 4.8 %all-to-all-start.1 = ((f32[4,3,8,640]{3,2,1,0:T(8,128)}), f32[4,3,8,640]{3,2,1,0:T(8,128)S(1)}, u32[]{:S(2)}, u32[]{:S(2)}) async-start(f32[4,3,8,640]{3,2,1,0:T(8,128)} %get-tuple-element.85), calls=%async_computation.1 | async-start | bytes 491520 | tf_op jit(solution)/shard_map/all_to_all | solution.py:260
  43.8 4.8 %all-to-all-start.2 = ((f32[4,3,8,640]{3,2,1,0:T(8,128)}), f32[4,3,8,640]{3,2,1,0:T(8,128)S(1)}, u32[]{:S(2)}, u32[]{:S(2)}) async-start(f32[4,3,8,640]{3,2,1,0:T(8,128)} %get-tuple-element.89), calls=%async_computation.2 | async-start | bytes 491520 | tf_op jit(solution)/shard_map/all_to_all | solution.py:260
  58.3 4.8 %all-to-all-start.3 = ((f32[4,3,8,640]{3,2,1,0:T(8,128)}), f32[4,3,8,640]{3,2,1,0:T(8,128)S(1)}, u32[]{:S(2)}, u32[]{:S(2)}) async-start(f32[4,3,8,640]{3,2,1,0:T(8,128)} %get-tuple-element.93), calls=%async_computation.3 | async-start | bytes 491520 | tf_op jit(solution)/shard_map/all_to_all | solution.py:260
  63.1 3.5 %collective-permute-start.3 = (f32[2,8,640]{2,1,0:T(8,128)S(1)}, f32[2,8,640]{2,1,0:T(8,128)S(1)}, u32[]{:S(2)}, u32[]{:S(2)}) collective-permute-start(f32[2,8,640]{2,1,0:T(8,128)S(1)} %get-tuple-element.92), channel_id=1, source_target_pairs={{0,127},{1,2},{2,1},{3,4},{4,3},{5,6},{6,5},{7,8},{8,7},{9,10},{10... | collective-permute-start | bytes 122888 | tf_op jit(solution)/shard_map/ppermute | solution.py:261
  72.8 4.8 %all-to-all-start.4 = ((f32[4,3,8,640]{3,2,1,0:T(8,128)}), f32[4,3,8,640]{3,2,1,0:T(8,128)S(1)}, u32[]{:S(2)}, u32[]{:S(2)}) async-start(f32[4,3,8,640]{3,2,1,0:T(8,128)} %get-tuple-element.97), calls=%async_computation.4 | async-start | bytes 491520 | tf_op jit(solution)/shard_map/all_to_all | solution.py:260
  87.3 4.8 %all-to-all-start.5 = ((f32[4,3,8,640]{3,2,1,0:T(8,128)}), f32[4,3,8,640]{3,2,1,0:T(8,128)S(1)}, u32[]{:S(2)}, u32[]{:S(2)}) async-start(f32[4,3,8,640]{3,2,1,0:T(8,128)} %get-tuple-element.101), calls=%async_computation.5 | async-start | bytes 491520 | tf_op jit(solution)/shard_map/all_to_all | solution.py:260
  92.1 3.5 %collective-permute-start.5 = (f32[2,8,640]{2,1,0:T(8,128)S(1)}, f32[2,8,640]{2,1,0:T(8,128)S(1)}, u32[]{:S(2)}, u32[]{:S(2)}) collective-permute-start(f32[2,8,640]{2,1,0:T(8,128)S(1)} %get-tuple-element.100), channel_id=1, source_target_pairs={{0,127},{1,2},{2,1},{3,4},{4,3},{5,6},{6,5},{7,8},{8,7},{9,10},{10... | collective-permute-start | bytes 122888 | tf_op jit(solution)/shard_map/ppermute | solution.py:261
  101.8 4.8 %all-to-all-start.6 = ((f32[4,3,8,640]{3,2,1,0:T(8,128)}), f32[4,3,8,640]{3,2,1,0:T(8,128)S(1)}, u32[]{:S(2)}, u32[]{:S(2)}) async-start(f32[4,3,8,640]{3,2,1,0:T(8,128)} %get-tuple-element.105), calls=%async_computation.6 | async-start | bytes 491520 | tf_op jit(solution)/shard_map/all_to_all | solution.py:260
  116.3 4.8 %all-to-all-start.7 = ((f32[4,3,8,640]{3,2,1,0:T(8,128)}), f32[4,3,8,640]{3,2,1,0:T(8,128)S(1)}, u32[]{:S(2)}, u32[]{:S(2)}) async-start(f32[4,3,8,640]{3,2,1,0:T(8,128)} %get-tuple-element.109), calls=%async_computation.7 | async-start | bytes 491520 | tf_op jit(solution)/shard_map/all_to_all | solution.py:260
  121.1 3.5 %collective-permute-start.7 = (f32[2,8,640]{2,1,0:T(8,128)S(1)}, f32[2,8,640]{2,1,0:T(8,128)S(1)}, u32[]{:S(2)}, u32[]{:S(2)}) collective-permute-start(f32[2,8,640]{2,1,0:T(8,128)S(1)} %get-tuple-element.108), channel_id=1, source_target_pairs={{0,127},{1,2},{2,1},{3,4},{4,3},{5,6},{6,5},{7,8},{8,7},{9,10},{10... | collective-permute-start | bytes 122888 | tf_op jit(solution)/shard_map/ppermute | solution.py:261
  130.8 4.8 %all-to-all-start.8 = ((f32[4,3,8,640]{3,2,1,0:T(8,128)}), f32[4,3,8,640]{3,2,1,0:T(8,128)S(1)}, u32[]{:S(2)}, u32[]{:S(2)}) async-start(f32[4,3,8,640]{3,2,1,0:T(8,128)} %get-tuple-element.113), calls=%async_computation.8 | async-start | bytes 491520 | tf_op jit(solution)/shard_map/all_to_all | solution.py:260
  145.3 4.8 %all-to-all-start.9 = ((f32[4,3,8,640]{3,2,1,0:T(8,128)}), f32[4,3,8,640]{3,2,1,0:T(8,128)S(1)}, u32[]{:S(2)}, u32[]{:S(2)}) async-start(f32[4,3,8,640]{3,2,1,0:T(8,128)} %get-tuple-element.117), calls=%async_computation.9 | async-start | bytes 491520 | tf_op jit(solution)/shard_map/all_to_all | solution.py:260
  150.1 3.5 %collective-permute-start.9 = (f32[2,8,640]{2,1,0:T(8,128)S(1)}, f32[2,8,640]{2,1,0:T(8,128)S(1)}, u32[]{:S(2)}, u32[]{:S(2)}) collective-permute-start(f32[2,8,640]{2,1,0:T(8,128)S(1)} %get-tuple-element.116), channel_id=1, source_target_pairs={{0,127},{1,2},{2,1},{3,4},{4,3},{5,6},{6,5},{7,8},{8,7},{9,10},{10... | collective-permute-start | bytes 122888 | tf_op jit(solution)/shard_map/ppermute | solution.py:261
  159.8 4.8 %all-to-all-start.10 = ((f32[4,3,8,640]{3,2,1,0:T(8,128)}), f32[4,3,8,640]{3,2,1,0:T(8,128)S(1)}, u32[]{:S(2)}, u32[]{:S(2)}) async-start(f32[4,3,8,640]{3,2,1,0:T(8,128)} %get-tuple-element.121), calls=%async_computation.10 | async-start | bytes 491520 | tf_op jit(solution)/shard_map/all_to_all | solution.py:260
  174.3 4.8 %all-to-all-start.11 = ((f32[4,3,8,640]{3,2,1,0:T(8,128)}), f32[4,3,8,640]{3,2,1,0:T(8,128)S(1)}, u32[]{:S(2)}, u32[]{:S(2)}) async-start(f32[4,3,8,640]{3,2,1,0:T(8,128)} %get-tuple-element.125), calls=%async_computation.11 | async-start | bytes 491520 | tf_op jit(solution)/shard_map/all_to_all | solution.py:260
  179.1 3.5 %collective-permute-start.11 = (f32[2,8,640]{2,1,0:T(8,128)S(1)}, f32[2,8,640]{2,1,0:T(8,128)S(1)}, u32[]{:S(2)}, u32[]{:S(2)}) collective-permute-start(f32[2,8,640]{2,1,0:T(8,128)S(1)} %get-tuple-element.124), channel_id=1, source_target_pairs={{0,127},{1,2},{2,1},{3,4},{4,3},{5,6},{6,5},{7,8},{8,7},{9,10},{10... | collective-permute-start | bytes 122888 | tf_op jit(solution)/shard_map/ppermute | solution.py:261
  188.8 4.8 %all-to-all-start.12 = ((f32[4,3,8,640]{3,2,1,0:T(8,128)}), f32[4,3,8,640]{3,2,1,0:T(8,128)S(1)}, u32[]{:S(2)}, u32[]{:S(2)}) async-start(f32[4,3,8,640]{3,2,1,0:T(8,128)} %get-tuple-element.129), calls=%async_computation.12 | async-start | bytes 491520 | tf_op jit(solution)/shard_map/all_to_all | solution.py:260
  203.3 4.8 %all-to-all-start.13 = ((f32[4,3,8,640]{3,2,1,0:T(8,128)}), f32[4,3,8,640]{3,2,1,0:T(8,128)S(1)}, u32[]{:S(2)}, u32[]{:S(2)}) async-start(f32[4,3,8,640]{3,2,1,0:T(8,128)} %get-tuple-element.133), calls=%async_computation.13 | async-start | bytes 491520 | tf_op jit(solution)/shard_map/all_to_all | solution.py:260
  208.1 3.5 %collective-permute-start.13 = (f32[2,8,640]{2,1,0:T(8,128)S(1)}, f32[2,8,640]{2,1,0:T(8,128)S(1)}, u32[]{:S(2)}, u32[]{:S(2)}) collective-permute-start(f32[2,8,640]{2,1,0:T(8,128)S(1)} %get-tuple-element.132), channel_id=1, source_target_pairs={{0,127},{1,2},{2,1},{3,4},{4,3},{5,6},{6,5},{7,8},{8,7},{9,10},{10... | collective-permute-start | bytes 122888 | tf_op jit(solution)/shard_map/ppermute | solution.py:261
  217.8 4.8 %all-to-all-start.14 = ((f32[4,3,8,640]{3,2,1,0:T(8,128)}), f32[4,3,8,640]{3,2,1,0:T(8,128)S(1)}, u32[]{:S(2)}, u32[]{:S(2)}) async-start(f32[4,3,8,640]{3,2,1,0:T(8,128)} %get-tuple-element.137), calls=%async_computation.14 | async-start | bytes 491520 | tf_op jit(solution)/shard_map/all_to_all | solution.py:260
  232.3 4.8 %all-to-all-start.15 = ((f32[4,3,8,640]{3,2,1,0:T(8,128)}), f32[4,3,8,640]{3,2,1,0:T(8,128)S(1)}, u32[]{:S(2)}, u32[]{:S(2)}) async-start(f32[4,3,8,640]{3,2,1,0:T(8,128)} %get-tuple-element.141), calls=%async_computation.15 | async-start | bytes 491520 | tf_op jit(solution)/shard_map/all_to_all | solution.py:260
  237.1 3.5 %collective-permute-start.15 = (f32[2,8,640]{2,1,0:T(8,128)S(1)}, f32[2,8,640]{2,1,0:T(8,128)S(1)}, u32[]{:S(2)}, u32[]{:S(2)}) collective-permute-start(f32[2,8,640]{2,1,0:T(8,128)S(1)} %get-tuple-element.140), channel_id=1, source_target_pairs={{0,127},{1,2},{2,1},{3,4},{4,3},{5,6},{6,5},{7,8},{8,7},{9,10},{10... | collective-permute-start | bytes 122888 | tf_op jit(solution)/shard_map/ppermute | solution.py:261
  (141 shorter events, 131.1 us)
Async XLA Ops:
  3.5 24.7 %all-to-all-start = ((f32[4,3,8,640]{3,2,1,0:T(8,128)}), f32[4,3,8,640]{3,2,1,0:T(8,128)S(1)}, u32[]{:S(2)}, u32[]{:S(2)}) async-start(f32[4,3,8,640]{3,2,1,0:T(8,128)} %get-tuple-element.76), calls=%async_computation | async-start | bytes 491520 | tf_op jit(solution)/shard_map/all_to_all | solution.py:260
  12.8 15.4 %collective-permute-start = (f32[2,8,640]{2,1,0:T(8,128)S(1)}, f32[2,8,640]{2,1,0:T(8,128)S(1)}, u32[]{:S(2)}, u32[]{:S(2)}) collective-permute-start(f32[2,8,640]{2,1,0:T(8,128)S(1)} %get-tuple-element.74), channel_id=1, source_target_pairs={{0,127},{1,2},{2,1},{3,4},{4,3},{5,6},{6,5},{7,8},{8,7},{9,10},{10... | collective-permute-start | bytes 122888 | tf_op jit(solution)/shard_map/ppermute | solution.py:261
  29.3 13.4 %all-to-all-start.1 = ((f32[4,3,8,640]{3,2,1,0:T(8,128)}), f32[4,3,8,640]{3,2,1,0:T(8,128)S(1)}, u32[]{:S(2)}, u32[]{:S(2)}) async-start(f32[4,3,8,640]{3,2,1,0:T(8,128)} %get-tuple-element.85), calls=%async_computation.1 | async-start | bytes 491520 | tf_op jit(solution)/shard_map/all_to_all | solution.py:260
  34.1 8.6 %collective-permute-start.1 = (f32[2,8,640]{2,1,0:T(8,128)S(1)}, f32[2,8,640]{2,1,0:T(8,128)S(1)}, u32[]{:S(2)}, u32[]{:S(2)}) collective-permute-start(f32[2,8,640]{2,1,0:T(8,128)S(1)} %get-tuple-element.84), channel_id=1, source_target_pairs={{0,127},{1,2},{2,1},{3,4},{4,3},{5,6},{6,5},{7,8},{8,7},{9,10},{10... | collective-permute-start | bytes 122888 | tf_op jit(solution)/shard_map/ppermute | solution.py:261
  43.8 13.4 %all-to-all-start.2 = ((f32[4,3,8,640]{3,2,1,0:T(8,128)}), f32[4,3,8,640]{3,2,1,0:T(8,128)S(1)}, u32[]{:S(2)}, u32[]{:S(2)}) async-start(f32[4,3,8,640]{3,2,1,0:T(8,128)} %get-tuple-element.89), calls=%async_computation.2 | async-start | bytes 491520 | tf_op jit(solution)/shard_map/all_to_all | solution.py:260
  48.6 8.6 %collective-permute-start.2 = (f32[2,8,640]{2,1,0:T(8,128)S(1)}, f32[2,8,640]{2,1,0:T(8,128)S(1)}, u32[]{:S(2)}, u32[]{:S(2)}) collective-permute-start(f32[2,8,640]{2,1,0:T(8,128)S(1)} %get-tuple-element.88), channel_id=1, source_target_pairs={{0,127},{1,2},{2,1},{3,4},{4,3},{5,6},{6,5},{7,8},{8,7},{9,10},{10... | collective-permute-start | bytes 122888 | tf_op jit(solution)/shard_map/ppermute | solution.py:261
  58.3 13.4 %all-to-all-start.3 = ((f32[4,3,8,640]{3,2,1,0:T(8,128)}), f32[4,3,8,640]{3,2,1,0:T(8,128)S(1)}, u32[]{:S(2)}, u32[]{:S(2)}) async-start(f32[4,3,8,640]{3,2,1,0:T(8,128)} %get-tuple-element.93), calls=%async_computation.3 | async-start | bytes 491520 | tf_op jit(solution)/shard_map/all_to_all | solution.py:260
  63.1 8.6 %collective-permute-start.3 = (f32[2,8,640]{2,1,0:T(8,128)S(1)}, f32[2,8,640]{2,1,0:T(8,128)S(1)}, u32[]{:S(2)}, u32[]{:S(2)}) collective-permute-start(f32[2,8,640]{2,1,0:T(8,128)S(1)} %get-tuple-element.92), channel_id=1, source_target_pairs={{0,127},{1,2},{2,1},{3,4},{4,3},{5,6},{6,5},{7,8},{8,7},{9,10},{10... | collective-permute-start | bytes 122888 | tf_op jit(solution)/shard_map/ppermute | solution.py:261
  72.8 13.4 %all-to-all-start.4 = ((f32[4,3,8,640]{3,2,1,0:T(8,128)}), f32[4,3,8,640]{3,2,1,0:T(8,128)S(1)}, u32[]{:S(2)}, u32[]{:S(2)}) async-start(f32[4,3,8,640]{3,2,1,0:T(8,128)} %get-tuple-element.97), calls=%async_computation.4 | async-start | bytes 491520 | tf_op jit(solution)/shard_map/all_to_all | solution.py:260
  77.6 8.6 %collective-permute-start.4 = (f32[2,8,640]{2,1,0:T(8,128)S(1)}, f32[2,8,640]{2,1,0:T(8,128)S(1)}, u32[]{:S(2)}, u32[]{:S(2)}) collective-permute-start(f32[2,8,640]{2,1,0:T(8,128)S(1)} %get-tuple-element.96), channel_id=1, source_target_pairs={{0,127},{1,2},{2,1},{3,4},{4,3},{5,6},{6,5},{7,8},{8,7},{9,10},{10... | collective-permute-start | bytes 122888 | tf_op jit(solution)/shard_map/ppermute | solution.py:261
  87.3 13.4 %all-to-all-start.5 = ((f32[4,3,8,640]{3,2,1,0:T(8,128)}), f32[4,3,8,640]{3,2,1,0:T(8,128)S(1)}, u32[]{:S(2)}, u32[]{:S(2)}) async-start(f32[4,3,8,640]{3,2,1,0:T(8,128)} %get-tuple-element.101), calls=%async_computation.5 | async-start | bytes 491520 | tf_op jit(solution)/shard_map/all_to_all | solution.py:260
  101.8 13.4 %all-to-all-start.6 = ((f32[4,3,8,640]{3,2,1,0:T(8,128)}), f32[4,3,8,640]{3,2,1,0:T(8,128)S(1)}, u32[]{:S(2)}, u32[]{:S(2)}) async-start(f32[4,3,8,640]{3,2,1,0:T(8,128)} %get-tuple-element.105), calls=%async_computation.6 | async-start | bytes 491520 | tf_op jit(solution)/shard_map/all_to_all | solution.py:260
  116.3 13.4 %all-to-all-start.7 = ((f32[4,3,8,640]{3,2,1,0:T(8,128)}), f32[4,3,8,640]{3,2,1,0:T(8,128)S(1)}, u32[]{:S(2)}, u32[]{:S(2)}) async-start(f32[4,3,8,640]{3,2,1,0:T(8,128)} %get-tuple-element.109), calls=%async_computation.7 | async-start | bytes 491520 | tf_op jit(solution)/shard_map/all_to_all | solution.py:260
  130.8 13.4 %all-to-all-start.8 = ((f32[4,3,8,640]{3,2,1,0:T(8,128)}), f32[4,3,8,640]{3,2,1,0:T(8,128)S(1)}, u32[]{:S(2)}, u32[]{:S(2)}) async-start(f32[4,3,8,640]{3,2,1,0:T(8,128)} %get-tuple-element.113), calls=%async_computation.8 | async-start | bytes 491520 | tf_op jit(solution)/shard_map/all_to_all | solution.py:260
  145.3 13.4 %all-to-all-start.9 = ((f32[4,3,8,640]{3,2,1,0:T(8,128)}), f32[4,3,8,640]{3,2,1,0:T(8,128)S(1)}, u32[]{:S(2)}, u32[]{:S(2)}) async-start(f32[4,3,8,640]{3,2,1,0:T(8,128)} %get-tuple-element.117), calls=%async_computation.9 | async-start | bytes 491520 | tf_op jit(solution)/shard_map/all_to_all | solution.py:260
  159.8 13.4 %all-to-all-start.10 = ((f32[4,3,8,640]{3,2,1,0:T(8,128)}), f32[4,3,8,640]{3,2,1,0:T(8,128)S(1)}, u32[]{:S(2)}, u32[]{:S(2)}) async-start(f32[4,3,8,640]{3,2,1,0:T(8,128)} %get-tuple-element.121), calls=%async_computation.10 | async-start | bytes 491520 | tf_op jit(solution)/shard_map/all_to_all | solution.py:260
  164.6 8.6 %collective-permute-start.10 = (f32[2,8,640]{2,1,0:T(8,128)S(1)}, f32[2,8,640]{2,1,0:T(8,128)S(1)}, u32[]{:S(2)}, u32[]{:S(2)}) collective-permute-start(f32[2,8,640]{2,1,0:T(8,128)S(1)} %get-tuple-element.120), channel_id=1, source_target_pairs={{0,127},{1,2},{2,1},{3,4},{4,3},{5,6},{6,5},{7,8},{8,7},{9,10},{10... | collective-permute-start | bytes 122888 | tf_op jit(solution)/shard_map/ppermute | solution.py:261
  174.3 13.4 %all-to-all-start.11 = ((f32[4,3,8,640]{3,2,1,0:T(8,128)}), f32[4,3,8,640]{3,2,1,0:T(8,128)S(1)}, u32[]{:S(2)}, u32[]{:S(2)}) async-start(f32[4,3,8,640]{3,2,1,0:T(8,128)} %get-tuple-element.125), calls=%async_computation.11 | async-start | bytes 491520 | tf_op jit(solution)/shard_map/all_to_all | solution.py:260
  188.8 13.4 %all-to-all-start.12 = ((f32[4,3,8,640]{3,2,1,0:T(8,128)}), f32[4,3,8,640]{3,2,1,0:T(8,128)S(1)}, u32[]{:S(2)}, u32[]{:S(2)}) async-start(f32[4,3,8,640]{3,2,1,0:T(8,128)} %get-tuple-element.129), calls=%async_computation.12 | async-start | bytes 491520 | tf_op jit(solution)/shard_map/all_to_all | solution.py:260
  193.6 8.6 %collective-permute-start.12 = (f32[2,8,640]{2,1,0:T(8,128)S(1)}, f32[2,8,640]{2,1,0:T(8,128)S(1)}, u32[]{:S(2)}, u32[]{:S(2)}) collective-permute-start(f32[2,8,640]{2,1,0:T(8,128)S(1)} %get-tuple-element.128), channel_id=1, source_target_pairs={{0,127},{1,2},{2,1},{3,4},{4,3},{5,6},{6,5},{7,8},{8,7},{9,10},{10... | collective-permute-start | bytes 122888 | tf_op jit(solution)/shard_map/ppermute | solution.py:261
  203.3 13.4 %all-to-all-start.13 = ((f32[4,3,8,640]{3,2,1,0:T(8,128)}), f32[4,3,8,640]{3,2,1,0:T(8,128)S(1)}, u32[]{:S(2)}, u32[]{:S(2)}) async-start(f32[4,3,8,640]{3,2,1,0:T(8,128)} %get-tuple-element.133), calls=%async_computation.13 | async-start | bytes 491520 | tf_op jit(solution)/shard_map/all_to_all | solution.py:260
  217.8 13.4 %all-to-all-start.14 = ((f32[4,3,8,640]{3,2,1,0:T(8,128)}), f32[4,3,8,640]{3,2,1,0:T(8,128)S(1)}, u32[]{:S(2)}, u32[]{:S(2)}) async-start(f32[4,3,8,640]{3,2,1,0:T(8,128)} %get-tuple-element.137), calls=%async_computation.14 | async-start | bytes 491520 | tf_op jit(solution)/shard_map/all_to_all | solution.py:260
  232.3 13.4 %all-to-all-start.15 = ((f32[4,3,8,640]{3,2,1,0:T(8,128)}), f32[4,3,8,640]{3,2,1,0:T(8,128)S(1)}, u32[]{:S(2)}, u32[]{:S(2)}) async-start(f32[4,3,8,640]{3,2,1,0:T(8,128)} %get-tuple-element.141), calls=%async_computation.15 | async-start | bytes 491520 | tf_op jit(solution)/shard_map/all_to_all | solution.py:260
  237.1 8.6 %collective-permute-start.15 = (f32[2,8,640]{2,1,0:T(8,128)S(1)}, f32[2,8,640]{2,1,0:T(8,128)S(1)}, u32[]{:S(2)}, u32[]{:S(2)}) collective-permute-start(f32[2,8,640]{2,1,0:T(8,128)S(1)} %get-tuple-element.140), channel_id=1, source_target_pairs={{0,127},{1,2},{2,1},{3,4},{4,3},{5,6},{6,5},{7,8},{8,7},{9,10},{10... | collective-permute-start | bytes 122888 | tf_op jit(solution)/shard_map/ppermute | solution.py:261
  (33 other events, 100.8 us)
